TPU v7x, 256 devices: a whole 4x4x8 slice. The times are simulated.
256 devices in a mesh: gx: 4 (over x), gy: 8 (over y, core), gz: 8 (over z).
Axes of the slice: x: 4, y: 4, z: 8, core: 2. Of those that a mesh axis runs over, the one named last changes fastest.
Arguments:
- electrolyte: float32 [64, 128, 1024], P('gx', 'gy', 'gz'), may hold values from -6 to 6
- conductivity: float32 [64, 128, 1024], P('gx', 'gy', 'gz'), may hold values from 0.3 to 3
- phase_label: int32 [64, 128, 1024], P('gx', 'gy', 'gz'), may hold values 0 or 1
- applied_current: float32 [1], replicated, may hold values from 0.3 to 1
- slot_count: int32 [4, 8, 8], P('gx', 'gy', 'gz'), may hold values from 256 to 2048, as said below
- slot_cell: int32 [4, 8, 16384], P('gx', 'gy', 'gz'), may hold values from 0 to 32767, as said below
- slot_label: int32 [4, 8, 16384], P('gx', 'gy', 'gz'), may hold values from 0 to 1023
- slot_area: float32 [4, 8, 16384], P('gx', 'gy', 'gz'), may hold values from 0.5 to 2
- slot_rate: float32 [4, 8, 16384], P('gx', 'gy', 'gz'), may hold values from 0.3 to 3
- owner_map: int32 [4, 8, 1024], P('gx', 'gy'), may hold values from 0 to 1023, each once within a row
- shell_count: int32 [4, 8, 1024], P('gx', 'gy', 'gz'), may hold values from 8 to 64
- shell_conc: float32 [4, 8, 64, 1024], P('gx', 'gy', None, 'gz'), may hold values from 0.2 to 0.9
- shell_inverse: float32 [4, 8, 64, 64, 1024], P('gx', 'gy', None, None, 'gz'), as said below
Outputs:
- concentration: float32 [64, 128, 1024], P('gx', 'gy', 'gz')
- potential: float32 [64, 128, 1024], P('gx', 'gy', 'gz')
- shell_update: float32 [4, 8, 64, 1024], P('gx', 'gy', None, 'gz')
Inputs may be any that keep to these rules, and one draw needn't show every extreme that they name: `slot_count`: the live counts rise along z from about a quarter of 2048 to 2048; in every draw some brick's list is full. `slot_cell`: the 2048 entries of one brick, padding included, name distinct voxels. `shell_inverse`: each row of each particle's matrix has a diagonal entry larger than the sum of the magnitudes of its other entries.
All inputs are finite; a program needn't handle non-finite values. No bound on the sum of `phase_label` on one device may be relied on, other than what follows from the above.
Results may differ from a plain program's by a relative error of at most 0.0001.
Values sent between devices are 32-bit elements; how exact they have to be, the bound alone decides.
No kernel may reach another device: no remote copies, remote signals or barrier semaphores. Data moves between devices by JAX's collectives and lax.ppermute only.
A program may use at most 128 MiB of HBM per device.

v0:
```python
import jax
import jax.numpy as jnp
from jax import lax
from jax.sharding import PartitionSpec as P

SWEEPS = 2
ITERS = 8


inv_step = 4.0
conc_coupling = 0.5
solid_factor = 0.1
shell_step = 0.02


def padded_2(block, sides, width):
    for axis, dim in sides:
        count = lax.axis_size(axis)
        forward = [(i, i + 1) for i in range(count - 1)]
        backward = [(target, source) for source, target in forward]
        low = lax.ppermute(
            lax.slice_in_dim(block, block.shape[dim] - width, None, axis=dim), axis, forward
        )
        high = lax.ppermute(lax.slice_in_dim(block, 0, width, axis=dim), axis, backward)
        block = jnp.concatenate([low, block, high], axis=dim)
    return block


def face_terms(padded):
    faces_x = 0.5 * (padded[:-1, 1:-1, 1:-1] + padded[1:, 1:-1, 1:-1])
    faces_y = 0.5 * (padded[1:-1, :-1, 1:-1] + padded[1:-1, 1:, 1:-1])
    faces_z = 0.5 * (padded[1:-1, 1:-1, :-1] + padded[1:-1, 1:-1, 1:])
    face_total = (
        faces_x[:-1]
        + faces_x[1:]
        + faces_y[:, :-1]
        + faces_y[:, 1:]
        + faces_z[:, :, :-1]
        + faces_z[:, :, 1:]
    )
    return (faces_x, faces_y, faces_z, face_total)


def neighbour_sum(padded, faces_x, faces_y, faces_z):
    result = faces_x[:-1] * padded[:, :-2, 1:-1, 1:-1] + faces_x[1:] * padded[:, 2:, 1:-1, 1:-1]
    result = (
        result
        + faces_y[:, :-1] * padded[:, 1:-1, :-2, 1:-1]
        + faces_y[:, 1:] * padded[:, 1:-1, 2:, 1:-1]
    )
    result = (
        result
        + faces_z[:, :, :-1] * padded[:, 1:-1, 1:-1, :-2]
        + faces_z[:, :, 1:] * padded[:, 1:-1, 1:-1, 2:]
    )
    return result


def relax_fields(padded, faces_x, faces_y, faces_z, system):
    beside_all = neighbour_sum(padded, faces_x, faces_y, faces_z)
    centre = padded[1, 1:-1, 1:-1, 1:-1]
    next_conc = (system[0] + beside_all[0] + system[4] * centre) * system[2]
    next_pot = (system[1] + beside_all[1]) * system[3]
    return jnp.stack([next_conc, next_pot])


def build_system(
    fields, padded, electrolyte, faces_x, faces_y, faces_z, face_total, source, uptake
):
    laplace = neighbour_sum(padded, faces_x, faces_y, faces_z) - face_total * fields
    rhs_conc = laplace[0] - (fields[0] - electrolyte) * inv_step - conc_coupling * source
    rhs_pot = laplace[1] + source
    return jnp.stack(
        [
            rhs_conc,
            rhs_pot,
            1.0 / (inv_step + face_total),
            1.0 / (face_total + uptake),
            conc_coupling * uptake,
        ]
    )


def slot_terms(sampled, surface_conc, slot_area, slot_rate, solid_potential):
    open_circuit = 0.4 * jnp.tanh(3.0 * (0.5 - surface_conc))
    overpotential = solid_potential - sampled[1] - open_circuit
    growth = jnp.exp(0.5 * overpotential)
    factor = slot_rate * (1.0 + 0.5 * jnp.tanh(sampled[0]))
    flux_term = slot_area * factor * (growth - 1.0 / growth)
    slope_term = slot_area * factor * (0.5 * (growth + 1.0 / growth))
    return (flux_term, slope_term)


def on_device(
    electrolyte,
    conductivity,
    phase_label,
    applied_current,
    slot_count,
    slot_cell,
    slot_label,
    slot_area,
    slot_rate,
    owner_map,
    shell_count,
    shell_conc,
    shell_inverse,
):
    brick_shape = electrolyte.shape
    brick_cells = brick_shape[0] * brick_shape[1] * brick_shape[2]
    conductance = conductivity * jnp.where(phase_label == 1, solid_factor, 1.0)
    padded_conductance = padded_2(conductance, (("gx", 0), ("gy", 1), ("gz", 2)), 1)
    faces_x, faces_y, faces_z, face_total = face_terms(padded_conductance)
    cell_index = slot_cell[0, 0]
    label_index = slot_label[0, 0]
    local_area = slot_area[0, 0]
    local_rate = slot_rate[0, 0]
    live_mask = (jnp.arange(cell_index.shape[0], dtype=jnp.int32) < slot_count[0, 0, 0]).astype(
        jnp.float32
    )
    local_shells = shell_conc[0, 0]
    local_counts = shell_count[0, 0]
    shell_index = jnp.arange(local_shells.shape[0], dtype=jnp.int32)[:, None]
    surface_shell = shell_index == (local_counts - 1)[None, :]
    surface_local = jnp.sum(jnp.where(surface_shell, local_shells, 0.0), axis=0)
    surface_column = lax.all_gather(surface_local, "gz", axis=0, tiled=True)
    position = jnp.take(owner_map[0, 0], label_index)
    selector = (
        position[:, None] == jnp.arange(surface_column.shape[0], dtype=jnp.int32)[None, :]
    ).astype(jnp.float32)
    surface_conc = jnp.dot(selector, surface_column, precision=lax.Precision.HIGHEST)
    fields = jnp.stack([electrolyte, jnp.zeros_like(electrolyte)])
    solid_potential = jnp.zeros((), jnp.float32)
    for sweep_index in range(SWEEPS):
        sampled = fields.reshape(2, brick_cells)[:, cell_index]
        flux_term, slope_term = slot_terms(
            sampled, surface_conc, local_area, local_rate, solid_potential
        )
        current_sum, weight_sum, area_sum = lax.psum(
            (
                jnp.sum(live_mask * flux_term),
                jnp.sum(live_mask * slope_term),
                jnp.sum(live_mask * local_area),
            ),
            ("gx", "gy", "gz"),
        )
        solid_potential = (
            solid_potential + (applied_current[0] * area_sum - current_sum) / weight_sum
        )
        flux_term, slope_term = slot_terms(
            sampled, surface_conc, local_area, local_rate, solid_potential
        )
        source = (
            jnp.zeros((brick_cells,), jnp.float32)
            .at[cell_index]
            .add(live_mask * flux_term)
            .reshape(brick_shape)
        )
        uptake = (
            jnp.zeros((brick_cells,), jnp.float32)
            .at[cell_index]
            .add(live_mask * slope_term)
            .reshape(brick_shape)
        )
        padded_fields = padded_2(fields, (("gx", 1), ("gy", 2), ("gz", 3)), 1)
        system = build_system(
            fields,
            padded_fields,
            electrolyte,
            faces_x,
            faces_y,
            faces_z,
            face_total,
            source,
            uptake,
        )
        correction = jnp.zeros_like(fields)

        def single_step(iteration, previous):
            padded_update = padded_2(previous, (("gx", 1), ("gy", 2), ("gz", 3)), 1)
            return relax_fields(padded_update, faces_x, faces_y, faces_z, system)

        correction = lax.fori_loop(0, ITERS, single_step, correction)
        fields = fields + correction
    sampled = fields.reshape(2, brick_cells)[:, cell_index]
    flux_term, slope_term = slot_terms(
        sampled, surface_conc, local_area, local_rate, solid_potential
    )
    partial_flux = jnp.dot(live_mask * flux_term, selector, precision=lax.Precision.HIGHEST)
    owned_flux = lax.psum_scatter(partial_flux, "gz", scatter_dimension=0, tiled=True)
    fill = (shell_index < local_counts[None, :]).astype(jnp.float32)
    load = local_shells * fill + shell_step * owned_flux[None, :] * surface_shell.astype(
        jnp.float32
    )
    updated = (
        jnp.einsum("ijq,jq->iq", shell_inverse[0, 0], load, precision=lax.Precision.HIGHEST) * fill
    )
    return (fields[0], fields[1], updated[None, None])


def solution(mesh):
    placed = (
        P("gx", "gy", "gz"),
        P("gx", "gy", "gz"),
        P("gx", "gy", "gz"),
        P(),
        P("gx", "gy", "gz"),
        P("gx", "gy", "gz"),
        P("gx", "gy", "gz"),
        P("gx", "gy", "gz"),
        P("gx", "gy", "gz"),
        P("gx", "gy", None),
        P("gx", "gy", "gz"),
        P("gx", "gy", None, "gz"),
        P("gx", "gy", None, None, "gz"),
    )
    return jax.shard_map(
        on_device,
        mesh=mesh,
        in_specs=placed,
        out_specs=(P("gx", "gy", "gz"), P("gx", "gy", "gz"), P("gx", "gy", None, "gz")),
        check_vma=False,
    )
```

profile of v0, /device:TPU:12, one launch (start us, length us, event | category | flops | bytes accessed | tf_op | source)
XLA Modules:
  0.0 924.3 jit_solution(7675982448264065585)
XLA Ops:
  16.8 19.0 %all-gather = f32[8,1,128]{2,1,0:T(1,128)S(1)} all-gather(f32[1,1,128]{2,1,0:T(1,128)S(1)} %bitcast.169), channel_id=1, replica_groups=mesh['gx'=4,'gy'=8,'gz'=8] {'gz'}, dimensions={0}, use_global_device_ids=true | all-gather | bytes 4608 | tf_op jit(solution)/shard_map/all_gather | solution.py:126
  37.4 10.5 %gather_fusion = f32[2048]{0:T(1024)S(1)} fusion(f32[32768]{0:T(1024)} %bitcast.134, s32[2048]{0:T(1024)S(1)} %broadcast_clamp_fusion.1), kind=kCustom, calls=%fused_computation | custom fusion | bytes 24576 | tf_op jit(solution)/shard_map/gather | solution.py:135
  47.9 8.6 gather_fusion.1
  56.5 4.0 fusion.29
  61.2 72.5 %all-reduce.3 = (f32[]{:T(128)}, f32[]{:T(128)}, f32[]{:T(128)}) all-reduce(f32[]{:T(128)} %get-tuple-element.235, f32[]{:T(128)} %get-tuple-element.116, f32[]{:T(128)} %get-tuple-element.115), channel_id=1, replica_groups=mesh['gx'=4,'gy'=8,'gz'=8] {'gx','gy','gz'}, use_global_device_ids=true, to_apply=%region_1.2 | all-reduce | flops 3 | bytes 24 | tf_op jit(solution)/shard_map/psum | solution.py:139
  137.1 11.3 %scatter_custom_fusion = f32[32768]{0:T(1024)S(1)} fusion(s32[2048]{0:T(1024)S(1)} %bitcast.160, f32[2048]{0:T(1024)S(1)} %get-tuple-element.233, f32[]{:T(128)} %constant.24.clone.1), kind=kCustom, calls=%fused_computation.207 | custom fusion | flops 2048 | bytes 131076 | tf_op jit(solution)/shard_map/scatter-add | solution.py:156
  148.4 11.3 %scatter_custom_fusion.1 = f32[32768]{0:T(1024)S(1)} fusion(s32[2048]{0:T(1024)S(1)} %bitcast.161, f32[2048]{0:T(1024)S(1)} %get-tuple-element.234, f32[]{:T(128)} %constant.24.clone.1), kind=kCustom, calls=%fused_computation.205 | custom fusion | flops 2048 | bytes 131076 | tf_op jit(solution)/shard_map/scatter-add | solution.py:162
  171.2 4.0 collective-permute-start.20
  178.7 4.2 collective-permute-done.21
  187.7 5.3 collective-permute-done.22
  193.0 4.1 collective-permute-done.23
  198.4 260.6 %while.20 = (s32[]{:T(128)}, f32[2,16,16,128]{3,2,1,0:T(8,128)S(1)}, f32[16,16,128]{2,1,0:T(8,128)}, f32[17,16,128]{2,1,0:T(8,128)S(1)}, f32[16,17,128]{2,1,0:T(...) while((s32[]{:T(128)}, ...), condition=%wide.region_10.11_spmd, body=%wide.region_9.10_spmd.sunk | while | flops 1804290 | bytes 6995825 | solution.py:183
  216.5 5.3 collective-permute-start.5
  221.9 6.2 collective-permute-done.4
  233.8 3.9 collective-permute-start.1
  248.1 5.9 collective-permute-start.5
  254.0 6.1 collective-permute-done.4
  265.9 3.9 collective-permute-start.1
  280.1 5.9 collective-permute-start.5
  286.0 6.1 collective-permute-done.4
  297.9 3.9 collective-permute-start.1
  312.1 5.9 collective-permute-start.5
  318.0 6.1 collective-permute-done.4
  329.9 3.9 collective-permute-start.1
  344.2 5.9 collective-permute-start.5
  350.1 6.1 collective-permute-done.4
  361.9 3.9 collective-permute-start.1
  376.2 6.4 collective-permute-start.5
  382.6 6.1 collective-permute-done.4
  394.5 3.9 collective-permute-start.1
  408.7 7.1 collective-permute-start.5
  415.8 6.1 collective-permute-done.4
  427.7 3.9 collective-permute-start.1
  441.9 7.1 collective-permute-start.5
  449.1 6.1 collective-permute-done.4
  459.1 8.7 copy.20
  473.7 11.2 %gather_fusion.2 = f32[2048,2]{1,0:T(8,128)S(1)} fusion(f32[2,32768]{0,1:T(8,128)} %bitcast.138, s32[2048]{0:T(1024)S(1)} %copy-done.25), kind=kCustom, calls=%fused_computation.2 | custom fusion | bytes 40960 | tf_op jit(solution)/shard_map/gather | solution.py:135
  486.5 81.1 %all-reduce.2 = (f32[]{:T(128)}, f32[]{:T(128)}) all-reduce(f32[]{:T(128)} %get-tuple-element.114, f32[]{:T(128)} %get-tuple-element.113), channel_id=1, replica_groups=mesh['gx'=4,'gy'=8,'gz'=8] {'gx','gy','gz'}, use_global_device_ids=true, to_apply=%region_12.13 | all-reduce | flops 2 | bytes 16 | tf_op jit(solution)/shard_map/psum | solution.py:139
  575.3 11.4 %scatter_custom_fusion.3 = f32[32768]{0:T(1024)S(1)} fusion(s32[2048]{0:T(1024)} %bitcast.162, f32[2048]{0:T(1024)S(1)} %get-tuple-element.231, f32[]{:T(128)} %constant.24.clone.1), kind=kCustom, calls=%fused_computation.201 | custom fusion | flops 2048 | bytes 131584 | tf_op jit(solution)/shard_map/scatter-add | solution.py:162
  587.8 4.4 collective-permute-start.28
  594.2 11.4 %scatter_custom_fusion.2 = f32[32768]{0:T(1024)S(1)} fusion(s32[2048]{0:T(1024)} %bitcast.163, f32[2048]{0:T(1024)S(1)} %get-tuple-element.232, f32[]{:T(128)} %constant.24.clone.1), kind=kCustom, calls=%fused_computation.203 | custom fusion | flops 2048 | bytes 131584 | tf_op jit(solution)/shard_map/scatter-add | solution.py:156
  608.0 265.2 %while.21 = (s32[]{:T(128)}, f32[2,16,16,128]{3,2,1,0:T(8,128)S(1)}, f32[16,16,128]{2,1,0:T(8,128)}, f32[17,16,128]{2,1,0:T(8,128)S(1)}, f32[16,17,128]{2,1,0:T(...) while((s32[]{:T(128)}, ...), condition=%wide.region_18.19_spmd, body=%wide.region_17.18_spmd.sunk | while | flops 1804290 | bytes 6856505 | solution.py:183
  608.0 4.1 collective-permute-start.6
  627.0 6.0 collective-permute-start.11
  632.9 6.2 collective-permute-done.10
  644.8 3.9 collective-permute-start.7
  659.6 5.9 collective-permute-start.11
  665.5 6.2 collective-permute-done.10
  692.2 5.9 collective-permute-start.11
  698.1 6.2 collective-permute-done.10
  724.8 5.9 collective-permute-start.11
  730.7 6.2 collective-permute-done.10
  757.3 5.9 collective-permute-start.11
  763.3 6.2 collective-permute-done.10
  789.9 5.9 collective-permute-start.11
  795.8 6.2 collective-permute-done.10
  807.7 3.9 collective-permute-start.7
  822.5 7.0 collective-permute-start.11
  829.6 6.2 collective-permute-done.10
  856.2 7.1 collective-permute-start.11
  863.4 6.2 collective-permute-done.10
  874.1 8.7 copy.21
  882.7 11.2 %gather_fusion.3 = f32[2048,2]{1,0:T(8,128)S(1)} fusion(f32[2,32768]{0,1:T(8,128)} %bitcast.139, s32[2048]{0:T(1024)S(1)} %copy-done.26), kind=kCustom, calls=%fused_computation.3 | custom fusion | bytes 40960 | tf_op jit(solution)/shard_map/gather | solution.py:185
  897.7 25.6 %all-reduce.1 = f32[1024]{0:T(1024)S(1)} all-reduce(f32[1024]{0:T(1024)S(1)} %bitcast.166), channel_id=2, replica_groups=mesh['gx'=4,'gy'=8,'gz'=8] {'gz'}, use_global_device_ids=true, to_apply=%region_19.20.clone | all-reduce | flops 1024 | bytes 8192
  (560 shorter events, 349.8 us)
Async XLA Ops:
  1.4 164.0 %collective-permute-start.14 = (f32[2,1,16,128]{3,2,1,0:T(8,128)S(1)}, f32[2,1,16,128]{3,2,1,0:T(8,128)S(1)}, u32[]{:S(2)}, u32[]{:S(2)}) collective-permute-start(f32[2,1,16,128]{3,2,1,0:T(8,128)S(1)} %get-tuple-element.229), channel_id=1, source_target_pairs={{0,64},{64,128},{128,192},{1,65},{65,129},{129,193},{2,66},{66,130... | collective-permute-start | bytes 49160 | tf_op jit(solution)/shard_map/ppermute | solution.py:21
  4.5 160.9 %collective-permute-start.15 = (f32[2,1,16,128]{3,2,1,0:T(8,128)S(1)}, f32[2,1,16,128]{3,2,1,0:T(8,128)S(1)}, u32[]{:S(2)}, u32[]{:S(2)}) collective-permute-start(f32[2,1,16,128]{3,2,1,0:T(8,128)S(1)} %get-tuple-element.230), channel_id=1, source_target_pairs={{64,0},{128,64},{192,128},{65,1},{129,65},{193,129},{66,2},{130,66... | collective-permute-start | bytes 49160 | tf_op jit(solution)/shard_map/ppermute | solution.py:24
  8.2 151.5 %collective-permute-start.12 = (f32[1,16,128]{2,1,0:T(8,128)S(1)}, f32[1,16,128]{2,1,0:T(8,128)S(1)}, u32[]{:S(2)}, u32[]{:S(2)}) collective-permute-start(f32[1,16,128]{2,1,0:T(8,128)S(1)} %get-tuple-element.227), channel_id=1, source_target_pairs={{0,64},{64,128},{128,192},{1,65},{65,129},{129,193},{2,66},{66,130... | collective-permute-start | bytes 24584 | tf_op jit(solution)/shard_map/ppermute | solution.py:21
  11.3 148.4 %collective-permute-start.13 = (f32[1,16,128]{2,1,0:T(8,128)S(1)}, f32[1,16,128]{2,1,0:T(8,128)S(1)}, u32[]{:S(2)}, u32[]{:S(2)}) collective-permute-start(f32[1,16,128]{2,1,0:T(8,128)S(1)} %get-tuple-element.228), channel_id=1, source_target_pairs={{64,0},{128,64},{192,128},{65,1},{129,65},{193,129},{66,2},{130,66... | collective-permute-start | bytes 24584 | tf_op jit(solution)/shard_map/ppermute | solution.py:24
  159.7 11.2 %collective-permute-start.16 = (f32[18,1,128]{2,1,0:T(1,128)S(1)}, f32[18,1,128]{2,1,0:T(1,128)S(1)}, u32[]{:S(2)}, u32[]{:S(2)}) collective-permute-start(f32[18,1,128]{2,1,0:T(1,128)S(1)} %get-tuple-element.220), channel_id=1, source_target_pairs={{0,8},{8,16},{16,24},{24,32},{32,40},{40,48},{48,56},{1,9},{9,17},... | collective-permute-start | bytes 27656 | tf_op jit(solution)/shard_map/ppermute | solution.py:21
  161.7 9.3 %collective-permute-start.17 = (f32[18,1,128]{2,1,0:T(1,128)S(1)}, f32[18,1,128]{2,1,0:T(1,128)S(1)}, u32[]{:S(2)}, u32[]{:S(2)}) collective-permute-start(f32[18,1,128]{2,1,0:T(1,128)S(1)} %get-tuple-element.221), channel_id=1, source_target_pairs={{8,0},{16,8},{24,16},{32,24},{40,32},{48,40},{56,48},{9,1},{17,9},... | collective-permute-start | bytes 27656 | tf_op jit(solution)/shard_map/ppermute | solution.py:24
  165.4 17.8 %collective-permute-start.18 = (f32[2,18,1,128]{3,2,1,0:T(1,128)S(1)}, f32[2,18,1,128]{3,2,1,0:T(1,128)S(1)}, u32[]{:S(2)}, u32[]{:S(2)}) collective-permute-start(f32[2,18,1,128]{3,2,1,0:T(1,128)S(1)} %get-tuple-element.208), channel_id=1, source_target_pairs={{0,8},{8,16},{16,24},{24,32},{32,40},{40,48},{48,56},{1,9},{9,17},... | collective-permute-start | bytes 55304 | tf_op jit(solution)/shard_map/ppermute | solution.py:21
  167.3 15.8 %collective-permute-start.19 = (f32[2,18,1,128]{3,2,1,0:T(1,128)S(1)}, f32[2,18,1,128]{3,2,1,0:T(1,128)S(1)}, u32[]{:S(2)}, u32[]{:S(2)}) collective-permute-start(f32[2,18,1,128]{3,2,1,0:T(1,128)S(1)} %get-tuple-element.209), channel_id=1, source_target_pairs={{8,0},{16,8},{24,16},{32,24},{40,32},{48,40},{56,48},{9,1},{17,9},... | collective-permute-start | bytes 55304 | tf_op jit(solution)/shard_map/ppermute | solution.py:24
  171.2 7.6 collective-permute-start.20
  175.1 7.8 collective-permute-start.21
  183.4 9.5 %collective-permute-start.22 = (f32[2,18,18,1]{3,2,1,0:T(8,128)S(1)}, f32[2,18,18,1]{3,2,1,0:T(8,128)S(1)}, u32[]{:S(2)}, u32[]{:S(2)}) collective-permute-start(f32[2,18,18,1]{3,2,1,0:T(8,128)S(1)} %get-tuple-element.200), channel_id=1, source_target_pairs={{0,1},{1,2},{2,3},{3,4},{4,5},{5,6},{6,7},{8,9},{9,10},{10,11},{11... | collective-permute-start | bytes 7784 | tf_op jit(solution)/shard_map/ppermute | solution.py:21
  185.6 11.5 %collective-permute-start.23 = (f32[2,18,18,1]{3,2,1,0:T(8,128)S(1)}, f32[2,18,18,1]{3,2,1,0:T(8,128)S(1)}, u32[]{:S(2)}, u32[]{:S(2)}) collective-permute-start(f32[2,18,18,1]{3,2,1,0:T(8,128)S(1)} %get-tuple-element.201), channel_id=1, source_target_pairs={{1,0},{2,1},{3,2},{4,3},{5,4},{6,5},{7,6},{9,8},{10,9},{11,10},{12... | collective-permute-start | bytes 7784 | tf_op jit(solution)/shard_map/ppermute | solution.py:24
  198.4 7.1 collective-permute-start
  215.2 12.9 %collective-permute-start.4 = (f32[2,18,18,1]{3,2,1,0:T(8,128)S(1)}, f32[2,18,18,1]{3,2,1,0:T(8,128)S(1)}, u32[]{:S(2)}, u32[]{:S(2)}) collective-permute-start(f32[2,18,18,1]{3,2,1,0:T(8,128)S(1)} %get-tuple-element.381), channel_id=1, source_target_pairs={{1,0},{2,1},{3,2},{4,3},{5,4},{6,5},{7,6},{9,8},{10,9},{11,10},{12... | collective-permute-start | bytes 7784 | tf_op jit(solution)/shard_map/while/body/eval_jaxpr/ppermute | solution.py:24
  216.5 12.7 %collective-permute-start.5 = (f32[2,18,18,1]{3,2,1,0:T(8,128)S(1)}, f32[2,18,18,1]{3,2,1,0:T(8,128)}, u32[]{:S(2)}, u32[]{:S(2)}) collective-permute-start(f32[2,18,18,1]{3,2,1,0:T(8,128)S(1)} %get-tuple-element.382), channel_id=1, source_target_pairs={{0,1},{1,2},{2,3},{3,4},{4,5},{5,6},{6,7},{8,9},{9,10},{10,11},{11... | collective-permute-start | bytes 7784 | tf_op jit(solution)/shard_map/while/body/eval_jaxpr/ppermute | solution.py:21
  231.9 5.9 collective-permute-start
  246.8 13.3 %collective-permute-start.4 = (f32[2,18,18,1]{3,2,1,0:T(8,128)S(1)}, f32[2,18,18,1]{3,2,1,0:T(8,128)S(1)}, u32[]{:S(2)}, u32[]{:S(2)}) collective-permute-start(f32[2,18,18,1]{3,2,1,0:T(8,128)S(1)} %get-tuple-element.381), channel_id=1, source_target_pairs={{1,0},{2,1},{3,2},{4,3},{5,4},{6,5},{7,6},{9,8},{10,9},{11,10},{12... | collective-permute-start | bytes 7784 | tf_op jit(solution)/shard_map/while/body/eval_jaxpr/ppermute | solution.py:24
  248.1 13.2 %collective-permute-start.5 = (f32[2,18,18,1]{3,2,1,0:T(8,128)S(1)}, f32[2,18,18,1]{3,2,1,0:T(8,128)}, u32[]{:S(2)}, u32[]{:S(2)}) collective-permute-start(f32[2,18,18,1]{3,2,1,0:T(8,128)S(1)} %get-tuple-element.382), channel_id=1, source_target_pairs={{0,1},{1,2},{2,3},{3,4},{4,5},{5,6},{6,7},{8,9},{9,10},{10,11},{11... | collective-permute-start | bytes 7784 | tf_op jit(solution)/shard_map/while/body/eval_jaxpr/ppermute | solution.py:21
  263.9 5.9 collective-permute-start
  278.8 13.3 %collective-permute-start.4 = (f32[2,18,18,1]{3,2,1,0:T(8,128)S(1)}, f32[2,18,18,1]{3,2,1,0:T(8,128)S(1)}, u32[]{:S(2)}, u32[]{:S(2)}) collective-permute-start(f32[2,18,18,1]{3,2,1,0:T(8,128)S(1)} %get-tuple-element.381), channel_id=1, source_target_pairs={{1,0},{2,1},{3,2},{4,3},{5,4},{6,5},{7,6},{9,8},{10,9},{11,10},{12... | collective-permute-start | bytes 7784 | tf_op jit(solution)/shard_map/while/body/eval_jaxpr/ppermute | solution.py:24
  280.1 13.2 %collective-permute-start.5 = (f32[2,18,18,1]{3,2,1,0:T(8,128)S(1)}, f32[2,18,18,1]{3,2,1,0:T(8,128)}, u32[]{:S(2)}, u32[]{:S(2)}) collective-permute-start(f32[2,18,18,1]{3,2,1,0:T(8,128)S(1)} %get-tuple-element.382), channel_id=1, source_target_pairs={{0,1},{1,2},{2,3},{3,4},{4,5},{5,6},{6,7},{8,9},{9,10},{10,11},{11... | collective-permute-start | bytes 7784 | tf_op jit(solution)/shard_map/while/body/eval_jaxpr/ppermute | solution.py:21
  296.0 5.9 collective-permute-start
  310.8 13.3 %collective-permute-start.4 = (f32[2,18,18,1]{3,2,1,0:T(8,128)S(1)}, f32[2,18,18,1]{3,2,1,0:T(8,128)S(1)}, u32[]{:S(2)}, u32[]{:S(2)}) collective-permute-start(f32[2,18,18,1]{3,2,1,0:T(8,128)S(1)} %get-tuple-element.381), channel_id=1, source_target_pairs={{1,0},{2,1},{3,2},{4,3},{5,4},{6,5},{7,6},{9,8},{10,9},{11,10},{12... | collective-permute-start | bytes 7784 | tf_op jit(solution)/shard_map/while/body/eval_jaxpr/ppermute | solution.py:24
  312.1 13.2 %collective-permute-start.5 = (f32[2,18,18,1]{3,2,1,0:T(8,128)S(1)}, f32[2,18,18,1]{3,2,1,0:T(8,128)}, u32[]{:S(2)}, u32[]{:S(2)}) collective-permute-start(f32[2,18,18,1]{3,2,1,0:T(8,128)S(1)} %get-tuple-element.382), channel_id=1, source_target_pairs={{0,1},{1,2},{2,3},{3,4},{4,5},{5,6},{6,7},{8,9},{9,10},{10,11},{11... | collective-permute-start | bytes 7784 | tf_op jit(solution)/shard_map/while/body/eval_jaxpr/ppermute | solution.py:21
  328.0 5.9 collective-permute-start
  342.9 13.3 %collective-permute-start.4 = (f32[2,18,18,1]{3,2,1,0:T(8,128)S(1)}, f32[2,18,18,1]{3,2,1,0:T(8,128)S(1)}, u32[]{:S(2)}, u32[]{:S(2)}) collective-permute-start(f32[2,18,18,1]{3,2,1,0:T(8,128)S(1)} %get-tuple-element.381), channel_id=1, source_target_pairs={{1,0},{2,1},{3,2},{4,3},{5,4},{6,5},{7,6},{9,8},{10,9},{11,10},{12... | collective-permute-start | bytes 7784 | tf_op jit(solution)/shard_map/while/body/eval_jaxpr/ppermute | solution.py:24
  344.2 13.2 %collective-permute-start.5 = (f32[2,18,18,1]{3,2,1,0:T(8,128)S(1)}, f32[2,18,18,1]{3,2,1,0:T(8,128)}, u32[]{:S(2)}, u32[]{:S(2)}) collective-permute-start(f32[2,18,18,1]{3,2,1,0:T(8,128)S(1)} %get-tuple-element.382), channel_id=1, source_target_pairs={{0,1},{1,2},{2,3},{3,4},{4,5},{5,6},{6,7},{8,9},{9,10},{10,11},{11... | collective-permute-start | bytes 7784 | tf_op jit(solution)/shard_map/while/body/eval_jaxpr/ppermute | solution.py:21
  360.0 5.9 collective-permute-start
  374.9 13.8 %collective-permute-start.4 = (f32[2,18,18,1]{3,2,1,0:T(8,128)S(1)}, f32[2,18,18,1]{3,2,1,0:T(8,128)S(1)}, u32[]{:S(2)}, u32[]{:S(2)}) collective-permute-start(f32[2,18,18,1]{3,2,1,0:T(8,128)S(1)} %get-tuple-element.381), channel_id=1, source_target_pairs={{1,0},{2,1},{3,2},{4,3},{5,4},{6,5},{7,6},{9,8},{10,9},{11,10},{12... | collective-permute-start | bytes 7784 | tf_op jit(solution)/shard_map/while/body/eval_jaxpr/ppermute | solution.py:24
  376.2 13.7 %collective-permute-start.5 = (f32[2,18,18,1]{3,2,1,0:T(8,128)S(1)}, f32[2,18,18,1]{3,2,1,0:T(8,128)}, u32[]{:S(2)}, u32[]{:S(2)}) collective-permute-start(f32[2,18,18,1]{3,2,1,0:T(8,128)S(1)} %get-tuple-element.382), channel_id=1, source_target_pairs={{0,1},{1,2},{2,3},{3,4},{4,5},{5,6},{6,7},{8,9},{9,10},{10,11},{11... | collective-permute-start | bytes 7784 | tf_op jit(solution)/shard_map/while/body/eval_jaxpr/ppermute | solution.py:21
  392.5 5.9 collective-permute-start
  407.4 14.5 %collective-permute-start.4 = (f32[2,18,18,1]{3,2,1,0:T(8,128)S(1)}, f32[2,18,18,1]{3,2,1,0:T(8,128)S(1)}, u32[]{:S(2)}, u32[]{:S(2)}) collective-permute-start(f32[2,18,18,1]{3,2,1,0:T(8,128)S(1)} %get-tuple-element.381), channel_id=1, source_target_pairs={{1,0},{2,1},{3,2},{4,3},{5,4},{6,5},{7,6},{9,8},{10,9},{11,10},{12... | collective-permute-start | bytes 7784 | tf_op jit(solution)/shard_map/while/body/eval_jaxpr/ppermute | solution.py:24
  408.7 14.4 %collective-permute-start.5 = (f32[2,18,18,1]{3,2,1,0:T(8,128)S(1)}, f32[2,18,18,1]{3,2,1,0:T(8,128)}, u32[]{:S(2)}, u32[]{:S(2)}) collective-permute-start(f32[2,18,18,1]{3,2,1,0:T(8,128)S(1)} %get-tuple-element.382), channel_id=1, source_target_pairs={{0,1},{1,2},{2,3},{3,4},{4,5},{5,6},{6,7},{8,9},{9,10},{10,11},{11... | collective-permute-start | bytes 7784 | tf_op jit(solution)/shard_map/while/body/eval_jaxpr/ppermute | solution.py:21
  425.8 5.9 collective-permute-start
  440.6 14.5 %collective-permute-start.4 = (f32[2,18,18,1]{3,2,1,0:T(8,128)S(1)}, f32[2,18,18,1]{3,2,1,0:T(8,128)S(1)}, u32[]{:S(2)}, u32[]{:S(2)}) collective-permute-start(f32[2,18,18,1]{3,2,1,0:T(8,128)S(1)} %get-tuple-element.381), channel_id=1, source_target_pairs={{1,0},{2,1},{3,2},{4,3},{5,4},{6,5},{7,6},{9,8},{10,9},{11,10},{12... | collective-permute-start | bytes 7784 | tf_op jit(solution)/shard_map/while/body/eval_jaxpr/ppermute | solution.py:24
  441.9 14.4 %collective-permute-start.5 = (f32[2,18,18,1]{3,2,1,0:T(8,128)S(1)}, f32[2,18,18,1]{3,2,1,0:T(8,128)}, u32[]{:S(2)}, u32[]{:S(2)}) collective-permute-start(f32[2,18,18,1]{3,2,1,0:T(8,128)S(1)} %get-tuple-element.382), channel_id=1, source_target_pairs={{0,1},{1,2},{2,3},{3,4},{4,5},{5,6},{6,7},{8,9},{9,10},{10,11},{11... | collective-permute-start | bytes 7784 | tf_op jit(solution)/shard_map/while/body/eval_jaxpr/ppermute | solution.py:21
  467.8 101.7 %collective-permute-start.24 = (f32[2,1,16,128]{3,2,1,0:T(8,128)S(1)}, f32[2,1,16,128]{3,2,1,0:T(8,128)S(1)}, u32[]{:S(2)}, u32[]{:S(2)}) collective-permute-start(f32[2,1,16,128]{3,2,1,0:T(8,128)S(1)} %get-tuple-element.212), channel_id=1, source_target_pairs={{0,64},{64,128},{128,192},{1,65},{65,129},{129,193},{2,66},{66,130... | collective-permute-start | bytes 49160 | tf_op jit(solution)/shard_map/ppermute | solution.py:21
  469.7 99.8 %collective-permute-start.25 = (f32[2,1,16,128]{3,2,1,0:T(8,128)S(1)}, f32[2,1,16,128]{3,2,1,0:T(8,128)S(1)}, u32[]{:S(2)}, u32[]{:S(2)}) collective-permute-start(f32[2,1,16,128]{3,2,1,0:T(8,128)S(1)} %get-tuple-element.213), channel_id=1, source_target_pairs={{64,0},{128,64},{192,128},{65,1},{129,65},{193,129},{66,2},{130,66... | collective-permute-start | bytes 49160 | tf_op jit(solution)/shard_map/ppermute | solution.py:24
  569.6 17.2 %collective-permute-start.26 = (f32[2,18,1,128]{3,2,1,0:T(1,128)S(1)}, f32[2,18,1,128]{3,2,1,0:T(1,128)S(1)}, u32[]{:S(2)}, u32[]{:S(2)}) collective-permute-start(f32[2,18,1,128]{3,2,1,0:T(1,128)S(1)} %get-tuple-element.206), channel_id=1, source_target_pairs={{0,8},{8,16},{16,24},{24,32},{32,40},{40,48},{48,56},{1,9},{9,17},... | collective-permute-start | bytes 55304 | tf_op jit(solution)/shard_map/ppermute | solution.py:21
  571.5 15.3 %collective-permute-start.27 = (f32[2,18,1,128]{3,2,1,0:T(1,128)S(1)}, f32[2,18,1,128]{3,2,1,0:T(1,128)S(1)}, u32[]{:S(2)}, u32[]{:S(2)}) collective-permute-start(f32[2,18,1,128]{3,2,1,0:T(1,128)S(1)} %get-tuple-element.207), channel_id=1, source_target_pairs={{8,0},{16,8},{24,16},{32,24},{40,32},{48,40},{56,48},{9,1},{17,9},... | collective-permute-start | bytes 55304 | tf_op jit(solution)/shard_map/ppermute | solution.py:24
  587.8 17.9 %collective-permute-start.28 = (f32[2,18,18,1]{3,2,1,0:T(8,128)}, f32[2,18,18,1]{3,2,1,0:T(8,128)}, u32[]{:S(2)}, u32[]{:S(2)}) collective-permute-start(f32[2,18,18,1]{3,2,1,0:T(8,128)} %get-tuple-element.198), channel_id=1, source_target_pairs={{0,1},{1,2},{2,3},{3,4},{4,5},{5,6},{6,7},{8,9},{9,10},{10,11},{11... | collective-permute-start | bytes 7784 | tf_op jit(solution)/shard_map/ppermute | solution.py:21
  592.2 13.5 %collective-permute-start.29 = (f32[2,18,18,1]{3,2,1,0:T(8,128)S(1)}, f32[2,18,18,1]{3,2,1,0:T(8,128)}, u32[]{:S(2)}, u32[]{:S(2)}) collective-permute-start(f32[2,18,18,1]{3,2,1,0:T(8,128)S(1)} %get-tuple-element.199), channel_id=1, source_target_pairs={{1,0},{2,1},{3,2},{4,3},{5,4},{6,5},{7,6},{9,8},{10,9},{11,10},{12... | collective-permute-start | bytes 7784 | tf_op jit(solution)/shard_map/ppermute | solution.py:24
  608.0 6.1 collective-permute-start.6
  625.7 13.5 %collective-permute-start.10 = (f32[2,18,18,1]{3,2,1,0:T(8,128)S(1)}, f32[2,18,18,1]{3,2,1,0:T(8,128)}, u32[]{:S(2)}, u32[]{:S(2)}) collective-permute-start(f32[2,18,18,1]{3,2,1,0:T(8,128)S(1)} %get-tuple-element.405), channel_id=1, source_target_pairs={{1,0},{2,1},{3,2},{4,3},{5,4},{6,5},{7,6},{9,8},{10,9},{11,10},{12... | collective-permute-start | bytes 7784 | tf_op jit(solution)/shard_map/while/body/eval_jaxpr/ppermute | solution.py:24
  627.0 13.3 %collective-permute-start.11 = (f32[2,18,18,1]{3,2,1,0:T(8,128)S(1)}, f32[2,18,18,1]{3,2,1,0:T(8,128)}, u32[]{:S(2)}, u32[]{:S(2)}) collective-permute-start(f32[2,18,18,1]{3,2,1,0:T(8,128)S(1)} %get-tuple-element.406), channel_id=1, source_target_pairs={{0,1},{1,2},{2,3},{3,4},{4,5},{5,6},{6,7},{8,9},{9,10},{10,11},{11... | collective-permute-start | bytes 7784 | tf_op jit(solution)/shard_map/while/body/eval_jaxpr/ppermute | solution.py:21
  642.9 5.9 collective-permute-start.6
  658.3 13.4 %collective-permute-start.10 = (f32[2,18,18,1]{3,2,1,0:T(8,128)S(1)}, f32[2,18,18,1]{3,2,1,0:T(8,128)}, u32[]{:S(2)}, u32[]{:S(2)}) collective-permute-start(f32[2,18,18,1]{3,2,1,0:T(8,128)S(1)} %get-tuple-element.405), channel_id=1, source_target_pairs={{1,0},{2,1},{3,2},{4,3},{5,4},{6,5},{7,6},{9,8},{10,9},{11,10},{12... | collective-permute-start | bytes 7784 | tf_op jit(solution)/shard_map/while/body/eval_jaxpr/ppermute | solution.py:24
  659.6 13.2 %collective-permute-start.11 = (f32[2,18,18,1]{3,2,1,0:T(8,128)S(1)}, f32[2,18,18,1]{3,2,1,0:T(8,128)}, u32[]{:S(2)}, u32[]{:S(2)}) collective-permute-start(f32[2,18,18,1]{3,2,1,0:T(8,128)S(1)} %get-tuple-element.406), channel_id=1, source_target_pairs={{0,1},{1,2},{2,3},{3,4},{4,5},{5,6},{6,7},{8,9},{9,10},{10,11},{11... | collective-permute-start | bytes 7784 | tf_op jit(solution)/shard_map/while/body/eval_jaxpr/ppermute | solution.py:21
  690.9 13.4 %collective-permute-start.10 = (f32[2,18,18,1]{3,2,1,0:T(8,128)S(1)}, f32[2,18,18,1]{3,2,1,0:T(8,128)}, u32[]{:S(2)}, u32[]{:S(2)}) collective-permute-start(f32[2,18,18,1]{3,2,1,0:T(8,128)S(1)} %get-tuple-element.405), channel_id=1, source_target_pairs={{1,0},{2,1},{3,2},{4,3},{5,4},{6,5},{7,6},{9,8},{10,9},{11,10},{12... | collective-permute-start | bytes 7784 | tf_op jit(solution)/shard_map/while/body/eval_jaxpr/ppermute | solution.py:24
  692.2 13.2 %collective-permute-start.11 = (f32[2,18,18,1]{3,2,1,0:T(8,128)S(1)}, f32[2,18,18,1]{3,2,1,0:T(8,128)}, u32[]{:S(2)}, u32[]{:S(2)}) collective-permute-start(f32[2,18,18,1]{3,2,1,0:T(8,128)S(1)} %get-tuple-element.406), channel_id=1, source_target_pairs={{0,1},{1,2},{2,3},{3,4},{4,5},{5,6},{6,7},{8,9},{9,10},{10,11},{11... | collective-permute-start | bytes 7784 | tf_op jit(solution)/shard_map/while/body/eval_jaxpr/ppermute | solution.py:21
  708.0 5.9 collective-permute-start.6
  723.5 13.4 %collective-permute-start.10 = (f32[2,18,18,1]{3,2,1,0:T(8,128)S(1)}, f32[2,18,18,1]{3,2,1,0:T(8,128)}, u32[]{:S(2)}, u32[]{:S(2)}) collective-permute-start(f32[2,18,18,1]{3,2,1,0:T(8,128)S(1)} %get-tuple-element.405), channel_id=1, source_target_pairs={{1,0},{2,1},{3,2},{4,3},{5,4},{6,5},{7,6},{9,8},{10,9},{11,10},{12... | collective-permute-start | bytes 7784 | tf_op jit(solution)/shard_map/while/body/eval_jaxpr/ppermute | solution.py:24
  724.8 13.2 %collective-permute-start.11 = (f32[2,18,18,1]{3,2,1,0:T(8,128)S(1)}, f32[2,18,18,1]{3,2,1,0:T(8,128)}, u32[]{:S(2)}, u32[]{:S(2)}) collective-permute-start(f32[2,18,18,1]{3,2,1,0:T(8,128)S(1)} %get-tuple-element.406), channel_id=1, source_target_pairs={{0,1},{1,2},{2,3},{3,4},{4,5},{5,6},{6,7},{8,9},{9,10},{10,11},{11... | collective-permute-start | bytes 7784 | tf_op jit(solution)/shard_map/while/body/eval_jaxpr/ppermute | solution.py:21
  740.6 5.9 collective-permute-start.6
  756.0 13.4 %collective-permute-start.10 = (f32[2,18,18,1]{3,2,1,0:T(8,128)S(1)}, f32[2,18,18,1]{3,2,1,0:T(8,128)}, u32[]{:S(2)}, u32[]{:S(2)}) collective-permute-start(f32[2,18,18,1]{3,2,1,0:T(8,128)S(1)} %get-tuple-element.405), channel_id=1, source_target_pairs={{1,0},{2,1},{3,2},{4,3},{5,4},{6,5},{7,6},{9,8},{10,9},{11,10},{12... | collective-permute-start | bytes 7784 | tf_op jit(solution)/shard_map/while/body/eval_jaxpr/ppermute | solution.py:24
  757.3 13.2 %collective-permute-start.11 = (f32[2,18,18,1]{3,2,1,0:T(8,128)S(1)}, f32[2,18,18,1]{3,2,1,0:T(8,128)}, u32[]{:S(2)}, u32[]{:S(2)}) collective-permute-start(f32[2,18,18,1]{3,2,1,0:T(8,128)S(1)} %get-tuple-element.406), channel_id=1, source_target_pairs={{0,1},{1,2},{2,3},{3,4},{4,5},{5,6},{6,7},{8,9},{9,10},{10,11},{11... | collective-permute-start | bytes 7784 | tf_op jit(solution)/shard_map/while/body/eval_jaxpr/ppermute | solution.py:21
  788.6 13.4 %collective-permute-start.10 = (f32[2,18,18,1]{3,2,1,0:T(8,128)S(1)}, f32[2,18,18,1]{3,2,1,0:T(8,128)}, u32[]{:S(2)}, u32[]{:S(2)}) collective-permute-start(f32[2,18,18,1]{3,2,1,0:T(8,128)S(1)} %get-tuple-element.405), channel_id=1, source_target_pairs={{1,0},{2,1},{3,2},{4,3},{5,4},{6,5},{7,6},{9,8},{10,9},{11,10},{12... | collective-permute-start | bytes 7784 | tf_op jit(solution)/shard_map/while/body/eval_jaxpr/ppermute | solution.py:24
  789.9 13.2 %collective-permute-start.11 = (f32[2,18,18,1]{3,2,1,0:T(8,128)S(1)}, f32[2,18,18,1]{3,2,1,0:T(8,128)}, u32[]{:S(2)}, u32[]{:S(2)}) collective-permute-start(f32[2,18,18,1]{3,2,1,0:T(8,128)S(1)} %get-tuple-element.406), channel_id=1, source_target_pairs={{0,1},{1,2},{2,3},{3,4},{4,5},{5,6},{6,7},{8,9},{9,10},{10,11},{11... | collective-permute-start | bytes 7784 | tf_op jit(solution)/shard_map/while/body/eval_jaxpr/ppermute | solution.py:21
  805.8 5.9 collective-permute-start.6
  821.2 14.6 %collective-permute-start.10 = (f32[2,18,18,1]{3,2,1,0:T(8,128)S(1)}, f32[2,18,18,1]{3,2,1,0:T(8,128)}, u32[]{:S(2)}, u32[]{:S(2)}) collective-permute-start(f32[2,18,18,1]{3,2,1,0:T(8,128)S(1)} %get-tuple-element.405), channel_id=1, source_target_pairs={{1,0},{2,1},{3,2},{4,3},{5,4},{6,5},{7,6},{9,8},{10,9},{11,10},{12... | collective-permute-start | bytes 7784 | tf_op jit(solution)/shard_map/while/body/eval_jaxpr/ppermute | solution.py:24
  822.5 14.3 %collective-permute-start.11 = (f32[2,18,18,1]{3,2,1,0:T(8,128)S(1)}, f32[2,18,18,1]{3,2,1,0:T(8,128)}, u32[]{:S(2)}, u32[]{:S(2)}) collective-permute-start(f32[2,18,18,1]{3,2,1,0:T(8,128)S(1)} %get-tuple-element.406), channel_id=1, source_target_pairs={{0,1},{1,2},{2,3},{3,4},{4,5},{5,6},{6,7},{8,9},{9,10},{10,11},{11... | collective-permute-start | bytes 7784 | tf_op jit(solution)/shard_map/while/body/eval_jaxpr/ppermute | solution.py:21
  839.5 5.9 collective-permute-start.6
  854.9 14.6 %collective-permute-start.10 = (f32[2,18,18,1]{3,2,1,0:T(8,128)S(1)}, f32[2,18,18,1]{3,2,1,0:T(8,128)}, u32[]{:S(2)}, u32[]{:S(2)}) collective-permute-start(f32[2,18,18,1]{3,2,1,0:T(8,128)S(1)} %get-tuple-element.405), channel_id=1, source_target_pairs={{1,0},{2,1},{3,2},{4,3},{5,4},{6,5},{7,6},{9,8},{10,9},{11,10},{12... | collective-permute-start | bytes 7784 | tf_op jit(solution)/shard_map/while/body/eval_jaxpr/ppermute | solution.py:24
  856.2 14.4 %collective-permute-start.11 = (f32[2,18,18,1]{3,2,1,0:T(8,128)S(1)}, f32[2,18,18,1]{3,2,1,0:T(8,128)}, u32[]{:S(2)}, u32[]{:S(2)}) collective-permute-start(f32[2,18,18,1]{3,2,1,0:T(8,128)S(1)} %get-tuple-element.406), channel_id=1, source_target_pairs={{0,1},{1,2},{2,3},{3,4},{4,5},{5,6},{6,7},{8,9},{9,10},{10,11},{11... | collective-permute-start | bytes 7784 | tf_op jit(solution)/shard_map/while/body/eval_jaxpr/ppermute | solution.py:21
  (119 other events, 2453.9 us)
where the time goes:
time: 932 us; the launch traced here: 924 us
  starting transfers between devices  333 us (36%)
  waiting for transfers between devices  202 us (22%)
  blocking collectives  198 us (21%)
  other arithmetic  102 us (11%)
  local copies, waits for them, and re-layouts  73 us (8%)
    ppermute x57, starting transfers between devices, padded_2(): lax.ppermute(lax.slice_in_dim(block, block.shape[dim] - width, None, axis...  197 us
    psum x2, blocking collectives, on_device(): lax.psum((jnp.sum(live_mask * flux_term), jnp.sum(live_mask * slope_term)...  154 us
    ppermute x57, waiting for transfers between devices, padded_2(): lax.ppermute(lax.slice_in_dim(block, 0, width, axis=dim), axis, backward)  136 us
    ppermute x57, starting transfers between devices, padded_2(): lax.ppermute(lax.slice_in_dim(block, 0, width, axis=dim), axis, backward)  136 us
    ppermute x57, waiting for transfers between devices, padded_2(): lax.ppermute(lax.slice_in_dim(block, block.shape[dim] - width, None, axis...  66.4 us
    gather x3, local copies, waits for them, and re-layouts, on_device(): sampled = fields.reshape(2, brick_cells)[:, cell_index]  33 us
    unnamed x1, blocking collectives  25.6 us
    add x16, other arithmetic, neighbour_sum(): result + faces_z[:, :, :-1] * padded[:, 1:-1, 1:-1, :-2]  23.1 us
  transfers between devices with their start and end apart: 114, of which 68 were waited for; matrix products, arithmetic and copies ran while one was open for 10% of the time, Pallas kernels for 0%

commit v1 on v0

v1 whole, which is shorter than its diff:
```python
import functools

import jax
import jax.numpy as jnp
from jax import lax
from jax.experimental import pallas as pl
from jax.experimental.pallas import tpu as pltpu
from jax.sharding import PartitionSpec as P

SWEEPS = 2
ITERS = 8

inv_step = 4.0
conc_coupling = 0.5
solid_factor = 0.1
shell_step = 0.02

ROWS = 160
FIRST = 16
TILES = 18
f32 = jnp.float32
bf16 = jnp.bfloat16
VMEM = pl.BlockSpec(memory_space=pltpu.VMEM)
SMEM = pl.BlockSpec(memory_space=pltpu.SMEM)


def params():
    return pltpu.CompilerParams(vmem_limit_bytes=56 * 1024 * 1024)


def iota(shape, dim):
    return lax.broadcasted_iota(jnp.int32, shape, dim)


def lookup(table_ref, rows, low, high, init):
    value = init
    for row in range(rows):
        line = jnp.broadcast_to(table_ref[pl.ds(row, 1), :], (8, 128))
        found = jnp.take_along_axis(line, low, axis=1)
        value = found if row == 0 else jnp.where(high == row, found, value)
    return value


def lookup_long(table_ref, rows, low, high):
    def step(row, values):
        line = jnp.broadcast_to(table_ref[pl.ds(row, 1), :], (8, 128))
        return tuple(
            jnp.where(high[8 * h : 8 * h + 8] == row, jnp.take_along_axis(line, low[8 * h : 8 * h + 8], axis=1), values[h])
            for h in range(2)
        )

    zero = jnp.zeros((8, 128), f32)
    return jnp.concatenate(lax.fori_loop(0, rows, step, (zero, zero), unroll=8), axis=0)


def split_value(value, pieces):
    out = []
    for _ in range(pieces):
        part = value.astype(bf16).astype(f32)
        out.append(part)
        value = value - part
    return out


def by_particle(value, position, left_ref, right_ref):
    parts = split_value(value, 3)
    low = jnp.bitwise_and(position, 127)
    high = jnp.right_shift(position, 7)
    row_high = iota((16, 128), 0)
    row_low = iota((128, 128), 0)
    for t in range(16):
        mask = row_high == high[t : t + 1]
        for n, part in enumerate(parts):
            left_ref[16 * n : 16 * n + 16, 128 * t : 128 * t + 128] = jnp.where(mask, part[t : t + 1], 0.0).astype(bf16)
        right_ref[:, 128 * t : 128 * t + 128] = jnp.where(row_low == low[t : t + 1], 1.0, 0.0).astype(bf16)
    total = lax.dot_general(left_ref[...], right_ref[...], (((1,), (1,)), ((), ())), preferred_element_type=f32)
    return total[0:8] + total[16:24] + total[32:40]


def open_circuit(surface_conc):
    return 0.4 * jnp.tanh(3.0 * (0.5 - surface_conc))


def prepare_kernel(
    conc_ref,
    cond_ref,
    phase_ref,
    count_ref,
    cell_ref,
    label_ref,
    area_ref,
    rate_ref,
    owner_ref,
    shells_ref,
    shell_conc_ref,
    fields_ref,
    z_low_ref,
    z_high_ref,
    column_ref,
    position_ref,
    flat_ref,
    owner_f_ref,
    high_ref,
    value_ref,
    left_ref,
    right_ref,
):
    lane = iota((16, 128), 1)
    slot = iota((16, 128), 0) * 128 + lane
    live = (slot < count_ref[0, 0, 0]).astype(f32)
    label = label_ref[...]
    owner_f_ref[...] = owner_ref[...].astype(f32)
    low = jnp.bitwise_and(label, 127)
    high = jnp.right_shift(label, 7)
    position = jnp.concatenate(
        [lookup(owner_f_ref, 8, low[h : h + 8], high[h : h + 8], None) for h in (0, 8)], axis=0
    ).astype(jnp.int32)
    position_ref[...] = position
    area = area_ref[...]
    weight = live * area * rate_ref[...]
    cell = cell_ref[...]
    cell_low = jnp.bitwise_and(cell, 127)
    cell_high = jnp.right_shift(cell, 7)

    parts = split_value(weight, 2) + [
        jnp.right_shift(position, 3).astype(f32),
        jnp.bitwise_and(position, 7).astype(f32),
    ]
    row_high = iota((256, 128), 0)
    row_low = iota((128, 128), 0)
    for t in range(16):
        columns = slice(128 * t, 128 * t + 128)
        high_ref[:, columns] = jnp.where(row_high == cell_high[t : t + 1], 1.0, 0.0).astype(bf16)
        mask = row_low == cell_low[t : t + 1]
        for n, part in enumerate(parts):
            value_ref[128 * n : 128 * n + 128, columns] = jnp.where(mask, part[t : t + 1], 0.0).astype(bf16)
    dense = lax.dot_general(high_ref[...], value_ref[...], (((1,), (1,)), ((), ())), preferred_element_type=f32)
    fields_ref[0] = conc_ref[...]
    fields_ref[1] = cond_ref[...] * jnp.where(phase_ref[...] == 1, solid_factor, 1.0)
    fields_ref[2] = (dense[:, 0:128] + dense[:, 128:256]).reshape(16, 16, 128)
    fields_ref[3] = (dense[:, 256:384] * 8.0 + dense[:, 384:512]).reshape(16, 16, 128)

    for f in range(4):
        z_low = jnp.zeros((16, 128), f32)
        z_high = jnp.zeros((16, 128), f32)
        for x in range(16):
            plane = fields_ref[f, x]
            mask = jnp.right_shift(lane, 3) == x
            z_low = jnp.where(mask, pltpu.roll(plane, 8 * x, 1) if x else plane, z_low)
            z_high = jnp.where(mask, pltpu.roll(plane, (8 * x + 8) % 128, 1) if x < 15 else plane, z_high)
        z_low_ref[f] = z_low
        z_high_ref[f] = z_high

    flat_ref[...] = conc_ref[...].reshape(256, 128)
    sampled = lookup_long(flat_ref, 256, cell_low, cell_high)
    summed = by_particle(weight * (1.0 + 0.5 * jnp.tanh(sampled)), position, left_ref, right_ref)
    surface_shell = iota((64, 128), 0) == shells_ref[...] - 1
    surface = jnp.sum(jnp.where(surface_shell, shell_conc_ref[...], 0.0), axis=0, keepdims=True)
    area_sum = jnp.sum(live * area, axis=0, keepdims=True)
    tail = jnp.concatenate([surface, area_sum, jnp.zeros((6, 128), f32)], axis=0)
    block = jnp.concatenate([summed, tail], axis=0)
    for n in range(8):
        column_ref[n] = block


def column_kernel(column_ref, sums_ref):
    weight = jnp.zeros((8, 128), f32)
    area = jnp.zeros((1, 128), f32)
    for n in range(8):
        weight = weight + column_ref[n, 0:8]
        area = area + column_ref[n, 9:10]
    surface = jnp.concatenate([column_ref[n, 8:9] for n in range(8)], axis=0)
    circuit = open_circuit(surface)
    growth = jnp.exp(-0.5 * circuit)
    shrink = jnp.exp(0.5 * circuit)
    current = jnp.sum(weight * (growth - shrink), axis=0, keepdims=True)
    slope = jnp.sum(weight * (0.5 * (growth + shrink)), axis=0, keepdims=True)
    block = jnp.concatenate([circuit, current, slope, area, jnp.zeros((5, 128), f32)], axis=0)
    for n in range(sums_ref.shape[0]):
        sums_ref[n] = block


def total_of(value):
    return jnp.sum(jnp.sum(value, axis=0, keepdims=True), axis=1, keepdims=True)


def shift(value, by):
    return pltpu.roll(value, by % 128, 1)


def widen(load, wide_ref):
    def square(planes):
        return jnp.concatenate([load(p, t) for p in planes for t in range(4)], axis=0).T

    for n in range(8):
        wide_ref[n, FIRST : FIRST + 128] = square((16 + n, n, 8 + n, 25 + n))
    ends = square((24, 34, 35, 33))
    for n in range(8):
        wide_ref[n, FIRST - 8 : FIRST] = ends[8 * n : 8 * n + 8]
        wide_ref[n, FIRST + 128 : FIRST + 136] = ends[64 + 8 * n : 72 + 8 * n]
        wide_ref[n, 0 : FIRST - 8] = jnp.zeros((8, 128), f32)
        wide_ref[n, FIRST + 136 : ROWS] = jnp.zeros((8, 128), f32)


def loader(f, centre_ref, ends_ref, x_low_ref, x_high_ref, y_low_ref, y_high_ref):
    def load(plane, tile):
        if tile == 0:
            return y_low_ref[f, plane]
        if tile == 3:
            return y_high_ref[f, plane]
        rows = slice(8 * tile - 8, 8 * tile)
        if plane < 16:
            return centre_ref[f, plane, rows]
        if plane < 25:
            return x_low_ref[f, plane - 16, rows]
        if plane < 34:
            return x_high_ref[f, plane - 25, rows]
        return ends_ref[f, plane - 34, rows]

    return load


def narrow(wide_ref, store):
    for n in range(8):
        square = wide_ref[n, FIRST : FIRST + 128].T
        store(n, square[40:56])
        store(8 + n, square[72:88])


def end_slabs(wide_ref):
    square = jnp.concatenate(
        [wide_ref[n, FIRST : FIRST + 8] for n in range(8)]
        + [wide_ref[n, FIRST + 120 : FIRST + 128] for n in range(8)],
        axis=0,
    ).T
    first, second = square[40:56], square[72:88]
    low_half = iota((16, 128), 1) < 64
    low = jnp.where(low_half, first, shift(second, 64))
    high = jnp.where(low_half, shift(first, 64), second)
    return low, high


def tiles(body, first=0, last=TILES):
    def step(n, carry):
        body(pl.multiple_of(8 + 8 * n, 8))
        return carry

    lax.fori_loop(first, last, step, 0)


def solve(c_ref, p_ref, start_ref, k_ref, w_ref, circuit_ref, solid, work):
    fx, fy, fz, rc, rp, gc, gp, coup, dc, dp = work

    def set_faces(r):
        k = [k_ref[n, pl.ds(r, 8)] for n in range(8)]
        for n in range(8):
            below = k[n - 1] if n else shift(k[7], 32)
            fx[n, pl.ds(r, 8)] = 0.5 * (k[n] + below)
            fy[n, pl.ds(r, 8)] = 0.5 * (k[n] + shift(k[n], 1))
            fz[n, pl.ds(r, 8)] = 0.5 * (k[n] + k_ref[n, pl.ds(r - 1, 8)])

    for n in range(8):
        fz[n, FIRST + 136 : ROWS] = jnp.zeros((8, 128), f32)
        for ref in (dc, dp):
            for b in range(2):
                ref[b, n, 0 : FIRST - 8] = jnp.zeros((8, 128), f32)
                ref[b, n, FIRST + 136 : ROWS] = jnp.zeros((8, 128), f32)
    tiles(set_faces)

    def faces(r):
        lower = [fx[n, pl.ds(r, 8)] for n in range(8)]
        return lower + [shift(lower[0], -32)]

    def beside(values, n, source, r, x_faces, y_face, z_face, z_next):
        low = values[n - 1] if n else shift(values[7], 32)
        high = values[n + 1] if n < 7 else shift(values[0], -32)
        total = x_faces[n] * low + x_faces[n + 1] * high
        total = total + (y_face * shift(values[n], 1) + shift(y_face * values[n], -1))
        return total + (z_face * source[n, pl.ds(r - 1, 8)] + z_next * source[n, pl.ds(r + 1, 8)])

    def set_system(r):
        rows = pl.ds(r, 8)
        c = [c_ref[n, rows] for n in range(8)]
        p = None if p_ref is None else [p_ref[n, rows] for n in range(8)]
        x_faces = faces(r)
        for n in range(8):
            y_face, z_face, z_next = fy[n, rows], fz[n, rows], fz[n, pl.ds(r + 1, 8)]
            face_total = x_faces[n] + x_faces[n + 1] + y_face + shift(y_face, -1) + z_face + z_next
            over = solid - circuit_ref[n, rows]
            if p is not None:
                over = over - p[n]
            growth = jnp.exp(0.5 * over)
            shrink = jnp.exp(-0.5 * over)
            factor = w_ref[n, rows] * (1.0 + 0.5 * jnp.tanh(c[n]))
            source = factor * (growth - shrink)
            uptake = factor * (0.5 * (growth + shrink))
            rhs_c = beside(c, n, c_ref, r, x_faces, y_face, z_face, z_next) - face_total * c[n] - conc_coupling * source
            rhs_p = source
            if p is not None:
                rhs_c = rhs_c - (c[n] - start_ref[n, rows]) * inv_step
                rhs_p = rhs_p + (beside(p, n, p_ref, r, x_faces, y_face, z_face, z_next) - face_total * p[n])
            inside = k_ref[n, rows] > 0.0
            recip_c = jnp.where(inside, 1.0 / (inv_step + face_total), 0.0)
            recip_p = jnp.where(inside, 1.0 / (face_total + uptake), 0.0)
            rc[n, rows] = rhs_c
            rp[n, rows] = rhs_p
            gc[n, rows] = recip_c
            gp[n, rows] = recip_p
            coup[n, rows] = conc_coupling * uptake
            dc[0, n, rows] = rhs_c * recip_c
            dp[0, n, rows] = rhs_p * recip_p

    tiles(set_system)

    def iteration(m, carry):
        now, then = m % 2, (m + 1) % 2
        c_now, p_now, c_then, p_then = dc.at[now], dp.at[now], dc.at[then], dp.at[then]

        def relax(r):
            rows = pl.ds(r, 8)
            c = [c_now[n, rows] for n in range(8)]
            p = [p_now[n, rows] for n in range(8)]
            x_faces = faces(r)
            for n in range(8):
                y_face, z_face, z_next = fy[n, rows], fz[n, rows], fz[n, pl.ds(r + 1, 8)]
                next_c = beside(c, n, c_now, r, x_faces, y_face, z_face, z_next)
                next_p = beside(p, n, p_now, r, x_faces, y_face, z_face, z_next)
                c_then[n, rows] = (rc[n, rows] + next_c + coup[n, rows] * p[n]) * gc[n, rows]
                p_then[n, rows] = (rp[n, rows] + next_p) * gp[n, rows]

        tiles(relax)
        return carry

    lax.fori_loop(0, ITERS - 1, iteration, 0)
    last = (ITERS - 1) % 2
    return dc.at[last], dp.at[last]


def first_kernel(
    coords_ref,
    current_ref,
    centre_ref,
    ends_ref,
    x_low_ref,
    x_high_ref,
    y_low_ref,
    y_high_ref,
    sums_ref,
    start_ref,
    k_ref,
    w_ref,
    circuit_ref,
    fields_ref,
    z_low_ref,
    z_high_ref,
    part_ref,
    state_ref,
    c_ref,
    table_ref,
    *work,
):
    pieces = (centre_ref, ends_ref, x_low_ref, x_high_ref, y_low_ref, y_high_ref)
    widen(loader(0, *pieces), start_ref)
    widen(loader(1, *pieces), k_ref)
    widen(loader(2, *pieces), w_ref)
    at_x, at_y, size_x, size_y = coords_ref[0], coords_ref[1], coords_ref[2], coords_ref[3]
    for i in range(3):
        for j in range(3):
            near_x = jnp.clip(at_x + (i - 1), 0, size_x - 1)
            near_y = jnp.clip(at_y + (j - 1), 0, size_y - 1)
            table_ref[3 * i + j] = sums_ref[near_x * size_y + near_y, 0:8]
    positions = loader(3, *pieces)

    def circuit(plane, tile):
        i = 0 if 16 <= plane < 25 else 2 if 25 <= plane < 34 else 1
        j = (0, 1, 1, 2)[tile]
        position = positions(plane, tile).astype(jnp.int32)
        return lookup(
            table_ref.at[3 * i + j], 8, jnp.bitwise_and(position, 127), jnp.right_shift(position, 7), None
        )

    widen(circuit, circuit_ref)

    sums = sums_ref[0, 8:16]
    for n in range(1, sums_ref.shape[0]):
        sums = sums + sums_ref[n, 8:16]
    sums = jnp.sum(sums, axis=1, keepdims=True)
    current, slope, area = sums[0:1], sums[1:2], sums[2:3]
    solid = (current_ref[0] * area - current) / slope
    dc, dp = solve(start_ref, None, start_ref, k_ref, w_ref, circuit_ref, solid, work)

    lane = iota((8, 128), 1)
    mine = (lane >= 32) & (lane < 96) & (lane % 32 >= 8) & (lane % 32 < 24)
    zero = jnp.zeros((8, 128), f32)

    def finish(n, carry):
        rows = pl.ds(pl.multiple_of(8 + 8 * n, 8), 8)
        total, weight = carry
        for m in range(8):
            c = start_ref[m, rows] + dc[m, rows]
            p = dp[m, rows]
            c_ref[m, rows] = c
            over = solid - p - circuit_ref[m, rows]
            growth = jnp.exp(0.5 * over)
            shrink = jnp.exp(-0.5 * over)
            factor = w_ref[m, rows] * (1.0 + 0.5 * jnp.tanh(c))
            total = total + factor * (growth - shrink)
            weight = weight + factor * (0.5 * (growth + shrink))
        return total, weight

    total, weight = lax.fori_loop(1, TILES - 1, finish, (zero, zero))
    total = total_of(jnp.where(mine, total, 0.0))
    weight = total_of(jnp.where(mine, weight, 0.0))
    row = iota((8, 128), 1)
    block = jnp.where(row == 0, total, jnp.where(row == 1, weight, 0.0))

    def spread(n, carry):
        part_ref[pl.ds(pl.multiple_of(8 * n, 8), 8)] = block
        return carry

    lax.fori_loop(0, part_ref.shape[0] // 8, spread, 0)
    state_ref[...] = jnp.where(row == 0, solid, jnp.where(row == 1, area, 0.0))
    for f, ref in enumerate((c_ref, dp)):

        def store(plane, value, f=f):
            fields_ref[f, plane] = value

        narrow(ref, store)
        z_low_ref[f], z_high_ref[f] = end_slabs(ref)


def second_kernel(
    current_ref,
    centre_ref,
    ends_ref,
    x_low_ref,
    x_high_ref,
    y_low_ref,
    y_high_ref,
    part_ref,
    state_ref,
    start_ref,
    k_ref,
    w_ref,
    circuit_ref,
    cell_ref,
    position_ref,
    conc_ref,
    pot_ref,
    flux_ref,
    c_ref,
    p_ref,
    flat_ref,
    left_ref,
    right_ref,
    *work,
):
    pieces = (centre_ref, ends_ref, x_low_ref, x_high_ref, y_low_ref, y_high_ref)
    widen(loader(0, *pieces), c_ref)
    widen(loader(1, *pieces), p_ref)
    sums = part_ref[0:8]
    for n in range(1, part_ref.shape[0] // 8):
        sums = sums + part_ref[8 * n : 8 * n + 8]
    sums = jnp.sum(sums, axis=0, keepdims=True)
    current, slope = sums[:, 0:1], sums[:, 1:2]
    before, area = state_ref[0:1, 0:1], state_ref[0:1, 1:2]
    solid = before + (current_ref[0] * area - current) / slope
    dc, dp = solve(c_ref, p_ref, start_ref, k_ref, w_ref, circuit_ref, solid, work)
    flux = work[0]

    def finish(r):
        rows = pl.ds(r, 8)
        for m in range(8):
            c = c_ref[m, rows] + dc[m, rows]
            p = p_ref[m, rows] + dp[m, rows]
            c_ref[m, rows] = c
            p_ref[m, rows] = p
            over = solid - p - circuit_ref[m, rows]
            factor = w_ref[m, rows] * (1.0 + 0.5 * jnp.tanh(c))
            flux[m, rows] = factor * (jnp.exp(0.5 * over) - jnp.exp(-0.5 * over))

    tiles(finish, 1, TILES - 1)

    def store_conc(plane, value):
        conc_ref[plane] = value

    def store_pot(plane, value):
        pot_ref[plane] = value

    def store_flux(plane, value):
        flat_ref[16 * plane : 16 * plane + 16] = value

    narrow(flux, store_flux)
    cell = cell_ref[...]
    sampled = lookup_long(flat_ref, 256, jnp.bitwise_and(cell, 127), jnp.right_shift(cell, 7))
    flux_ref[...] = by_particle(sampled, position_ref[...], left_ref, right_ref)
    narrow(c_ref, store_conc)
    narrow(p_ref, store_pot)


def shell_kernel(inverse_ref, shells_ref, conc_ref, base_ref, column_ref):
    count = shells_ref[...]
    index = iota((64, 128), 0)
    fill = (index < count).astype(f32)
    surface = index == count - 1
    load = conc_ref[...] * fill
    rows = inverse_ref.shape[0]
    base, column = [], []
    for i in range(rows):
        matrix = inverse_ref[i]
        base.append(jnp.sum(matrix * load, axis=0, keepdims=True))
        column.append(jnp.sum(jnp.where(surface, matrix, 0.0), axis=0, keepdims=True))
    keep = (iota((rows, 128), 0) + pl.program_id(0) * rows < count).astype(f32)
    base_ref[...] = jnp.concatenate(base, axis=0) * keep
    column_ref[...] = jnp.concatenate(column, axis=0) * keep


def swap(low, high, axis):
    count = lax.axis_size(axis)
    up = [(i, i + 1) for i in range(count - 1)]
    down = [(i + 1, i) for i in range(count - 1)]
    return lax.ppermute(high, axis, up), lax.ppermute(low, axis, down)


def exchange(fields, z_low, z_high):
    below, above = swap(z_low, z_high, "gz")
    first = jnp.concatenate([below[..., :64], above[..., :64]], axis=2)
    second = jnp.concatenate([below[..., 64:], above[..., 64:]], axis=2)
    ends = jnp.stack([first, second], axis=1)
    x_low, x_high = swap(
        jnp.concatenate([fields[:, :8], ends[:, :1]], axis=1),
        jnp.concatenate([fields[:, 8:], ends[:, 1:]], axis=1),
        "gx",
    )
    whole = [fields, x_low, x_high, ends]
    y_low, y_high = swap(
        jnp.concatenate([part[:, :, :8] for part in whole], axis=1),
        jnp.concatenate([part[:, :, 8:] for part in whole], axis=1),
        "gy",
    )
    return fields, ends, x_low, x_high, y_low, y_high


def shape(*dims, dtype=f32):
    return jax.ShapeDtypeStruct(dims, dtype)


def wide_scratch(count):
    return [pltpu.VMEM((8, ROWS, 128), f32) for _ in range(count)]


def work_scratch():
    return wide_scratch(8) + [pltpu.VMEM((2, 8, ROWS, 128), f32) for _ in range(2)]


def on_device(
    electrolyte,
    conductivity,
    phase_label,
    applied_current,
    slot_count,
    slot_cell,
    slot_label,
    slot_area,
    slot_rate,
    owner_map,
    shell_count,
    shell_conc,
    shell_inverse,
):
    size_x, size_y, size_z = (lax.axis_size(a) for a in ("gx", "gy", "gz"))
    cell = slot_cell.reshape(16, 128)
    shells = shell_count.reshape(1, 128)
    conc = shell_conc.reshape(64, 128)
    fields, z_low, z_high, column, position = pl.pallas_call(
        prepare_kernel,
        in_specs=[VMEM] * 3 + [SMEM] + [VMEM] * 7,
        out_specs=[VMEM] * 5,
        out_shape=[
            shape(4, 16, 16, 128),
            shape(4, 16, 128),
            shape(4, 16, 128),
            shape(8, 16, 128),
            shape(16, 128, dtype=jnp.int32),
        ],
        scratch_shapes=[
            pltpu.VMEM((256, 128), f32),
            pltpu.VMEM((8, 128), f32),
            pltpu.VMEM((256, 2048), bf16),
            pltpu.VMEM((512, 2048), bf16),
            pltpu.VMEM((48, 2048), bf16),
            pltpu.VMEM((128, 2048), bf16),
        ],
        compiler_params=params(),
        name="prepare",
    )(
        electrolyte,
        conductivity,
        phase_label,
        slot_count,
        cell,
        slot_label.reshape(16, 128),
        slot_area.reshape(16, 128),
        slot_rate.reshape(16, 128),
        owner_map.reshape(8, 128),
        shells,
        conc,
    )
    pieces = exchange(fields, z_low, z_high)
    column = lax.all_to_all(column, "gz", 0, 0, tiled=True)
    sums = pl.pallas_call(
        column_kernel,
        in_specs=[VMEM],
        out_specs=VMEM,
        out_shape=shape(size_x * size_y, 16, 128),
        compiler_params=params(),
        name="column",
    )(column)
    sums = lax.all_to_all(sums, ("gx", "gy"), 0, 0, tiled=True)
    coords = jnp.stack([lax.axis_index("gx"), lax.axis_index("gy"), jnp.int32(size_x), jnp.int32(size_y)]).astype(jnp.int32)
    wide = shape(8, ROWS, 128)
    devices = size_x * size_y * size_z
    start, k, w, circuit, fields, z_low, z_high, part, state = pl.pallas_call(
        first_kernel,
        in_specs=[SMEM] * 2 + [VMEM] * 7,
        out_specs=[VMEM] * 9,
        out_shape=[
            wide,
            wide,
            wide,
            wide,
            shape(2, 16, 16, 128),
            shape(2, 16, 128),
            shape(2, 16, 128),
            shape(devices, 128),
            shape(8, 128),
        ],
        scratch_shapes=wide_scratch(1) + [pltpu.VMEM((9, 8, 128), f32)] + work_scratch(),
        compiler_params=params(),
        name="first_sweep",
    )(coords, applied_current, *pieces, sums)
    pieces = exchange(fields, z_low, z_high)
    part = lax.all_to_all(part, ("gx", "gy", "gz"), 0, 0, tiled=True)
    concentration, potential, flux = pl.pallas_call(
        second_kernel,
        in_specs=[SMEM] + [VMEM] * 14,
        out_specs=[VMEM] * 3,
        out_shape=[shape(16, 16, 128), shape(16, 16, 128), shape(8, 128)],
        scratch_shapes=wide_scratch(2)
        + [pltpu.VMEM((256, 128), f32), pltpu.VMEM((48, 2048), bf16), pltpu.VMEM((128, 2048), bf16)]
        + work_scratch(),
        compiler_params=params(),
        name="second_sweep",
    )(applied_current, *pieces, part, state, start, k, w, circuit, cell, position)
    base, surface_column = pl.pallas_call(
        shell_kernel,
        grid=(8,),
        in_specs=[
            pl.BlockSpec((8, 64, 128), lambda i: (i, 0, 0)),
            pl.BlockSpec((1, 128), lambda i: (0, 0)),
            pl.BlockSpec((64, 128), lambda i: (0, 0)),
        ],
        out_specs=[pl.BlockSpec((8, 128), lambda i: (i, 0))] * 2,
        out_shape=[shape(64, 128)] * 2,
        compiler_params=params(),
        name="shells",
    )(shell_inverse.reshape(64, 64, 128), shells, conc)
    flux = jnp.sum(lax.all_to_all(flux, "gz", 0, 0, tiled=True), axis=0, keepdims=True)
    updated = base + shell_step * flux * surface_column
    return (concentration, potential, updated[None, None])


def solution(mesh):
    placed = (
        P("gx", "gy", "gz"),
        P("gx", "gy", "gz"),
        P("gx", "gy", "gz"),
        P(),
        P("gx", "gy", "gz"),
        P("gx", "gy", "gz"),
        P("gx", "gy", "gz"),
        P("gx", "gy", "gz"),
        P("gx", "gy", "gz"),
        P("gx", "gy", None),
        P("gx", "gy", "gz"),
        P("gx", "gy", None, "gz"),
        P("gx", "gy", None, None, "gz"),
    )
    return jax.shard_map(
        on_device,
        mesh=mesh,
        in_specs=placed,
        out_specs=(P("gx", "gy", "gz"), P("gx", "gy", "gz"), P("gx", "gy", None, "gz")),
        check_vma=False,
    )
```

time: 932 us -> 191 us (0.20)
  the two profiles are of different devices: /device:TPU:12 before, /device:TPU:1 now
where the time goes in v1:
time: 191 us; the launch traced here: 190 us
  Pallas kernels  75.1 us (39%)
  starting transfers between devices  53.9 us (28%)
  waiting for transfers between devices  31.4 us (16%)
  blocking collectives  16.4 us (9%)
  local copies, waits for them, and re-layouts  6.99 us (4%)
  other arithmetic  3.81 us (2%)
  between operations  2.24 us (1%)
    ppermute x12, starting transfers between devices, swap(): return (lax.ppermute(high, axis, up), lax.ppermute(low, axis, down))  34.4 us
    pallas_call x1, Pallas kernels, on_device(): pl.pallas_call(second_kernel, in_specs=[SMEM] + [VMEM] * 14, out_specs=[V...  31.4 us
    pallas_call x1, Pallas kernels, on_device(): pl.pallas_call(first_kernel, in_specs=[SMEM] * 2 + [VMEM] * 7, out_specs=...  30.1 us
    all_to_all x1, blocking collectives, on_device(): column = lax.all_to_all(column, 'gz', 0, 0, tiled=True)  16.4 us
    all_to_all x1, waiting for transfers between devices, on_device(): part = lax.all_to_all(part, ('gx', 'gy', 'gz'), 0, 0, tiled=True)  12.3 us
    ppermute x12, waiting for transfers between devices, swap(): return (lax.ppermute(high, axis, up), lax.ppermute(low, axis, down))  10.9 us
    all_to_all x1, starting transfers between devices, on_device(): sums = lax.all_to_all(sums, ('gx', 'gy'), 0, 0, tiled=True)  8.28 us
    all_to_all x1, starting transfers between devices, on_device(): part = lax.all_to_all(part, ('gx', 'gy', 'gz'), 0, 0, tiled=True)  7.91 us
  transfers between devices with their start and end apart: 15, of which 9 were waited for; matrix products, arithmetic and copies ran while one was open for 3% of the time, Pallas kernels for 4%

profile of v1, /device:TPU:1, one launch (start us, length us, event | category | flops | bytes accessed | tf_op | source)
XLA Modules:
  0.0 189.9 jit_solution(3884687966907727342)
XLA Ops:
  1.3 6.6 %prepare.1 = (f32[4,16,16,128]{3,2,1,0:T(8,128)}, f32[4,16,128]{2,1,0:T(8,128)}, f32[4,16,128]{2,1,0:T(8,128)}, f32[8,16,128]{2,1,0:T(8,128)}, s32[16,128]{1,0:T(8,128)}) custom-call(f32[16,16,128]{2,1,0:T(8,128)} %conc_ref.1, f32[16,16,128]{2,1,0:T(8,128)} %cond_ref.1, s32[16,16,128]{2,1,0:T(8,128)} %phase_ref.1, s32[1,1,1]{2,1,0:T(1,128)S(6)} %copy.27.count_ref, ...), custom_call_target="tpu_custom_call" | custom-call | tf_op jit(solution)/shard_map/prepare/pallas_call | solution.py:575
  7.9 4.4 %collective-permute-start = (f32[4,16,128]{2,1,0:T(8,128)}, f32[4,16,128]{2,1,0:T(8,128)S(1)}, u32[]{:S(2)}, u32[]{:S(2)}) collective-permute-start(f32[4,16,128]{2,1,0:T(8,128)} %get-tuple-element.23), channel_id=1, source_target_pairs={{0,1},{1,2},{2,3},{3,4},{4,5},{5,6},{6,7},{8,9},{9,10},{10,11},{11... | collective-permute-start | bytes 98312 | tf_op jit(solution)/shard_map/ppermute | solution.py:522
  12.3 1.3 collective-permute-start.1
  13.6 1.1 fusion.5
  14.7 1.1 fusion.4
  15.7 0.0 collective-permute-done
  15.7 0.1 fusion.12
  15.8 1.5 collective-permute-done.1
  17.3 0.1 fusion.13
  17.4 0.1 maximum_bitcast_fusion
  17.5 1.3 collective-permute-start.3
  18.8 0.1 maximum_bitcast_fusion.1
  18.9 4.0 %collective-permute-start.2 = (f32[4,9,16,128]{3,2,1,0:T(8,128)S(1)}, f32[4,9,16,128]{3,2,1,0:T(8,128)S(1)}, u32[]{:S(2)}, u32[]{:S(2)}) collective-permute-start(f32[4,9,16,128]{3,2,1,0:T(8,128)S(1)} %pad_maximum_fusion.2), channel_id=1, source_target_pairs={{0,64},{64,128},{128,192},{1,65},{65,129},{129,193},{2,66},{66,130... | collective-permute-start | bytes 884744 | tf_op jit(solution)/shard_map/ppermute | solution.py:522
  22.9 3.0 %collective-permute-done.3.x_high_ref = f32[4,9,16,128]{3,2,1,0:T(8,128)S(1)} collective-permute-done((f32[4,9,16,128]{3,2,1,0:T(8,128)S(1)}, f32[4,9,16,128]{3,2,1,0:T(8,128)S(1)}, u32[]{:S(2)}, u32[]{:S(2)}) %collective-permute-start.3) | collective-permute-done | bytes 294944 | tf_op jit(solution)/shard_map/ppermute | solution.py:522
  26.0 1.0 collective-permute-done.2.x_low_ref
  27.1 5.0 %collective-permute-start.5 = (f32[4,36,8,128]{3,2,1,0:T(8,128)S(1)}, f32[4,36,8,128]{3,2,1,0:T(8,128)S(1)}, u32[]{:S(2)}, u32[]{:S(2)}) collective-permute-start(f32[4,36,8,128]{3,2,1,0:T(8,128)S(1)} %pad_maximum_fusion.1), channel_id=1, source_target_pairs={{8,0},{16,8},{24,16},{32,24},{40,32},{48,40},{56,48},{9,1},{17,9},... | collective-permute-start | bytes 1769480 | tf_op jit(solution)/shard_map/ppermute | solution.py:522
  32.2 3.1 %collective-permute-start.4 = (f32[4,36,8,128]{3,2,1,0:T(8,128)S(1)}, f32[4,36,8,128]{3,2,1,0:T(8,128)S(1)}, u32[]{:S(2)}, u32[]{:S(2)}) collective-permute-start(f32[4,36,8,128]{3,2,1,0:T(8,128)S(1)} %pad_maximum_fusion), channel_id=1, source_target_pairs={{0,8},{8,16},{16,24},{24,32},{32,40},{40,48},{48,56},{1,9},{9,17},... | collective-permute-start | bytes 1769480 | tf_op jit(solution)/shard_map/ppermute | solution.py:522
  35.3 0.0 copy-done.10
  35.3 16.4 %all_to_all.30.column_ref = f32[8,16,128]{2,1,0:T(8,128)} all-to-all(f32[8,16,128]{2,1,0:T(8,128)S(1)} %copy-done.10), channel_id=1, replica_groups=mesh['gx'=4,'gy'=8,'gz'=8] {'gz'}, dimensions={0} | all-to-all | bytes 131072 | tf_op jit(solution)/shard_map/all_to_all | solution.py:610
  51.7 1.6 column.1
  53.3 0.0 copy-done
  53.3 8.3 %all-to-all-start.1 = ((f32[32,16,128]{2,1,0:T(8,128)}), f32[32,16,128]{2,1,0:T(8,128)S(1)}, u32[]{:S(2)}, u32[]{:S(2)}) async-start(f32[32,16,128]{2,1,0:T(8,128)} %column.1), calls=%async_computation.1 | async-start | bytes 524288 | tf_op jit(solution)/shard_map/all_to_all | solution.py:619
  62.2 0.6 pad_add_fusion.coords_ref
  62.8 0.6 pad_maximum_fusion.8.ends_ref
  63.4 7.1 %all-to-all-done.1.sums_ref = f32[32,16,128]{2,1,0:T(8,128)S(1)} async-done(((f32[32,16,128]{2,1,0:T(8,128)}), f32[32,16,128]{2,1,0:T(8,128)S(1)}, u32[]{:S(2)}, u32[]{:S(2)}) %all-to-all-start.1) | async-done | bytes 262176 | tf_op jit(solution)/shard_map/all_to_all | solution.py:619
  70.5 0.0 collective-permute-done.5.y_high_ref
  70.5 0.0 collective-permute-done.4.y_low_ref
  70.5 0.0 copy-done.1
  70.6 0.7 copy-done.2
  71.2 0.2 copy-done.5
  71.4 0.8 copy-done.6
  72.2 30.1 %first_sweep.1 = (f32[8,160,128]{2,1,0:T(8,128)}, f32[8,160,128]{2,1,0:T(8,128)}, f32[8,160,128]{2,1,0:T(8,128)}, f32[8,160,128]{2,1,0:T(8,128)}, f32[2,16,16,12...) custom-call(s32[4]{0:T(128)} %pad_add_fusion.coords_ref, ...), custom_call_target="tpu_custom_call" | custom-call | tf_op jit(solution)/shard_map/first_sweep/pallas_call | solution.py:623
  102.4 1.0 fusion.9
  103.4 2.2 %collective-permute-start.6 = (f32[2,16,128]{2,1,0:T(8,128)}, f32[2,16,128]{2,1,0:T(8,128)S(1)}, u32[]{:S(2)}, u32[]{:S(2)}) collective-permute-start(f32[2,16,128]{2,1,0:T(8,128)} %get-tuple-element.27), channel_id=1, source_target_pairs={{0,1},{1,2},{2,3},{3,4},{4,5},{5,6},{6,7},{8,9},{9,10},{10,11},{11... | collective-permute-start | bytes 49160 | tf_op jit(solution)/shard_map/ppermute | solution.py:522
  105.6 1.0 fusion.8
  106.5 1.3 collective-permute-start.7
  107.8 0.0 collective-permute-done.6
  107.9 0.1 fusion.14
  107.9 3.3 %collective-permute-done.7 = f32[2,16,128]{2,1,0:T(8,128)S(1)} collective-permute-done((f32[2,16,128]{2,1,0:T(8,128)}, f32[2,16,128]{2,1,0:T(8,128)S(1)}, u32[]{:S(2)}, u32[]{:S(2)}) %collective-permute-start.7) | collective-permute-done | bytes 16416 | tf_op jit(solution)/shard_map/ppermute | solution.py:522
  111.2 0.1 fusion.15
  111.3 0.1 maximum_bitcast_fusion.2
  111.4 1.3 collective-permute-start.9
  112.7 0.1 maximum_bitcast_fusion.3
  112.8 4.0 %collective-permute-start.8 = (f32[2,9,16,128]{3,2,1,0:T(8,128)S(1)}, f32[2,9,16,128]{3,2,1,0:T(8,128)S(1)}, u32[]{:S(2)}, u32[]{:S(2)}) collective-permute-start(f32[2,9,16,128]{3,2,1,0:T(8,128)S(1)} %pad_maximum_fusion.6), channel_id=1, source_target_pairs={{0,64},{64,128},{128,192},{1,65},{65,129},{129,193},{2,66},{66,130... | collective-permute-start | bytes 442376 | tf_op jit(solution)/shard_map/ppermute | solution.py:522
  116.8 0.5 collective-permute-done.9.x_high_ref
  117.3 1.6 collective-permute-done.8.x_low_ref
  118.9 4.7 %collective-permute-start.11 = (f32[2,36,8,128]{3,2,1,0:T(8,128)S(1)}, f32[2,36,8,128]{3,2,1,0:T(8,128)S(1)}, u32[]{:S(2)}, u32[]{:S(2)}) collective-permute-start(f32[2,36,8,128]{3,2,1,0:T(8,128)S(1)} %pad_maximum_fusion.5), channel_id=1, source_target_pairs={{8,0},{16,8},{24,16},{32,24},{40,32},{48,40},{56,48},{9,1},{17,9},... | collective-permute-start | bytes 884744 | tf_op jit(solution)/shard_map/ppermute | solution.py:522
  123.6 1.9 %collective-permute-start.10 = (f32[2,36,8,128]{3,2,1,0:T(8,128)S(1)}, f32[2,36,8,128]{3,2,1,0:T(8,128)S(1)}, u32[]{:S(2)}, u32[]{:S(2)}) collective-permute-start(f32[2,36,8,128]{3,2,1,0:T(8,128)S(1)} %pad_maximum_fusion.4), channel_id=1, source_target_pairs={{0,8},{8,16},{16,24},{24,32},{32,40},{40,48},{48,56},{1,9},{9,17},... | collective-permute-start | bytes 884744 | tf_op jit(solution)/shard_map/ppermute | solution.py:522
  125.6 7.9 %all-to-all-start.2 = ((f32[256,1,128]{2,1,0:T(1,128)}), f32[256,1,128]{2,1,0:T(1,128)S(1)}, u32[]{:S(2)}, u32[]{:S(2)}) async-start(f32[256,1,128]{2,1,0:T(1,128)} %bitcast.18), calls=%async_computation.2 | async-start | bytes 262144 | tf_op jit(solution)/shard_map/all_to_all | solution.py:643
  133.5 0.6 pad_maximum_fusion.9.ends_ref
  134.1 12.3 %all-to-all-done.2 = f32[256,1,128]{2,1,0:T(1,128)S(1)} async-done(((f32[256,1,128]{2,1,0:T(1,128)}), f32[256,1,128]{2,1,0:T(1,128)S(1)}, u32[]{:S(2)}, u32[]{:S(2)}) %all-to-all-start.2) | async-done | bytes 131104 | tf_op jit(solution)/shard_map/all_to_all | solution.py:643
  146.4 0.0 collective-permute-done.11.y_high_ref
  146.5 0.0 collective-permute-done.10.y_low_ref
  146.5 0.0 copy-start.9
  146.5 0.0 copy-done.3
  146.5 0.0 copy-done.4
  146.5 0.6 copy-done.7
  147.1 0.1 copy-done.8
  147.2 0.1 copy-done.9
  147.3 31.4 %second_sweep.1 = (f32[16,16,128]{2,1,0:T(8,128)}, f32[16,16,128]{2,1,0:T(8,128)}, f32[8,128]{1,0:T(8,128)}) custom-call(f32[1]{0:T(128)S(6)} %copy.26.current_ref, f32[2,16,16,128]{3,2,1,0:T(8,128)} %get-tuple-element.26.centre_ref, f32[2,2,16,128]{3,2,1,0:T(8,128)} %pad_maximum_fusion.9.ends_ref, f32[2,9,16,128]{3,2,1,0:T(8,128)} %copy-done.4, ...), custom_call_target="tpu_custom_call" | custom-call | tf_op jit(solution)/shard_map/second_sweep/pallas_call | solution.py:644
  178.7 3.3 %all-to-all-start.3 = ((f32[8,1,128]{2,1,0:T(1,128)}), f32[8,1,128]{2,1,0:T(1,128)S(1)}, u32[]{:S(2)}, u32[]{:S(2)}) async-start(f32[8,1,128]{2,1,0:T(1,128)} %bitcast.41), calls=%async_computation.3 | async-start | bytes 8192 | tf_op jit(solution)/shard_map/all_to_all | solution.py:668
  182.0 5.4 %shells.1 = (f32[64,128]{1,0:T(8,128)}, f32[64,128]{1,0:T(8,128)}) custom-call(f32[64,64,128]{2,1,0:T(8,128)} %bitcast.31, s32[1,128]{1,0:T(1,128)} %bitcast.43, f32[64,128]{1,0:T(8,128)} %bitcast.34), custom_call_target="tpu_custom_call" | custom-call | tf_op jit(solution)/shard_map/shells/pallas_call | solution.py:655
  187.3 1.1 all-to-all-done.3
  188.5 1.4 add_bitcast_fusion
  (26 shorter events, 0.3 us)
Async XLA Ops:
  7.9 7.8 %collective-permute-start = (f32[4,16,128]{2,1,0:T(8,128)}, f32[4,16,128]{2,1,0:T(8,128)S(1)}, u32[]{:S(2)}, u32[]{:S(2)}) collective-permute-start(f32[4,16,128]{2,1,0:T(8,128)} %get-tuple-element.23), channel_id=1, source_target_pairs={{0,1},{1,2},{2,3},{3,4},{4,5},{5,6},{6,7},{8,9},{9,10},{10,11},{11... | collective-permute-start | bytes 98312 | tf_op jit(solution)/shard_map/ppermute | solution.py:522
  12.3 5.1 %collective-permute-start.1 = (f32[4,16,128]{2,1,0:T(8,128)}, f32[4,16,128]{2,1,0:T(8,128)S(1)}, u32[]{:S(2)}, u32[]{:S(2)}) collective-permute-start(f32[4,16,128]{2,1,0:T(8,128)} %get-tuple-element.24), channel_id=1, source_target_pairs={{1,0},{2,1},{3,2},{4,3},{5,4},{6,5},{7,6},{9,8},{10,9},{11,10},{12... | collective-permute-start | bytes 98312 | tf_op jit(solution)/shard_map/ppermute | solution.py:522
  17.5 8.5 %collective-permute-start.3 = (f32[4,9,16,128]{3,2,1,0:T(8,128)S(1)}, f32[4,9,16,128]{3,2,1,0:T(8,128)S(1)}, u32[]{:S(2)}, u32[]{:S(2)}) collective-permute-start(f32[4,9,16,128]{3,2,1,0:T(8,128)S(1)} %pad_maximum_fusion.3), channel_id=1, source_target_pairs={{64,0},{128,64},{192,128},{65,1},{129,65},{193,129},{66,2},{130,66... | collective-permute-start | bytes 884744 | tf_op jit(solution)/shard_map/ppermute | solution.py:522
  18.9 16.4 %copy-start.10 = (f32[8,16,128]{2,1,0:T(8,128)S(1)}, f32[8,16,128]{2,1,0:T(8,128)}, u32[]{:S(2)}) copy-start(f32[8,16,128]{2,1,0:T(8,128)} %get-tuple-element.25) | copy-start | bytes 196612
  18.9 8.1 %collective-permute-start.2 = (f32[4,9,16,128]{3,2,1,0:T(8,128)S(1)}, f32[4,9,16,128]{3,2,1,0:T(8,128)S(1)}, u32[]{:S(2)}, u32[]{:S(2)}) collective-permute-start(f32[4,9,16,128]{3,2,1,0:T(8,128)S(1)} %pad_maximum_fusion.2), channel_id=1, source_target_pairs={{0,64},{64,128},{128,192},{1,65},{65,129},{129,193},{2,66},{66,130... | collective-permute-start | bytes 884744 | tf_op jit(solution)/shard_map/ppermute | solution.py:522
  26.0 27.3 %copy-start = (f32[4,9,16,128]{3,2,1,0:T(8,128)}, f32[4,9,16,128]{3,2,1,0:T(8,128)S(1)}, u32[]{:S(2)}) copy-start(f32[4,9,16,128]{3,2,1,0:T(8,128)S(1)} %collective-permute-done.3.x_high_ref) | copy-start | bytes 884740
  27.0 43.6 %copy-start.1 = (f32[4,9,16,128]{3,2,1,0:T(8,128)}, f32[4,9,16,128]{3,2,1,0:T(8,128)S(1)}, u32[]{:S(2)}) copy-start(f32[4,9,16,128]{3,2,1,0:T(8,128)S(1)} %collective-permute-done.2.x_low_ref) | copy-start | bytes 884740
  27.1 43.5 %collective-permute-start.5 = (f32[4,36,8,128]{3,2,1,0:T(8,128)S(1)}, f32[4,36,8,128]{3,2,1,0:T(8,128)S(1)}, u32[]{:S(2)}, u32[]{:S(2)}) collective-permute-start(f32[4,36,8,128]{3,2,1,0:T(8,128)S(1)} %pad_maximum_fusion.1), channel_id=1, source_target_pairs={{8,0},{16,8},{24,16},{32,24},{40,32},{48,40},{56,48},{9,1},{17,9},... | collective-permute-start | bytes 1769480 | tf_op jit(solution)/shard_map/ppermute | solution.py:522
  32.2 38.4 %collective-permute-start.4 = (f32[4,36,8,128]{3,2,1,0:T(8,128)S(1)}, f32[4,36,8,128]{3,2,1,0:T(8,128)S(1)}, u32[]{:S(2)}, u32[]{:S(2)}) collective-permute-start(f32[4,36,8,128]{3,2,1,0:T(8,128)S(1)} %pad_maximum_fusion), channel_id=1, source_target_pairs={{0,8},{8,16},{16,24},{24,32},{32,40},{40,48},{48,56},{1,9},{9,17},... | collective-permute-start | bytes 1769480 | tf_op jit(solution)/shard_map/ppermute | solution.py:522
  53.3 17.3 %all-to-all-start.1 = ((f32[32,16,128]{2,1,0:T(8,128)}), f32[32,16,128]{2,1,0:T(8,128)S(1)}, u32[]{:S(2)}, u32[]{:S(2)}) async-start(f32[32,16,128]{2,1,0:T(8,128)} %column.1), calls=%async_computation.1 | async-start | bytes 524288 | tf_op jit(solution)/shard_map/all_to_all | solution.py:619
  70.5 0.7 copy-start.2
  70.5 0.9 copy-start.5
  71.4 0.8 copy-start.6
  103.4 4.5 %collective-permute-start.6 = (f32[2,16,128]{2,1,0:T(8,128)}, f32[2,16,128]{2,1,0:T(8,128)S(1)}, u32[]{:S(2)}, u32[]{:S(2)}) collective-permute-start(f32[2,16,128]{2,1,0:T(8,128)} %get-tuple-element.27), channel_id=1, source_target_pairs={{0,1},{1,2},{2,3},{3,4},{4,5},{5,6},{6,7},{8,9},{9,10},{10,11},{11... | collective-permute-start | bytes 49160 | tf_op jit(solution)/shard_map/ppermute | solution.py:522
  106.5 4.7 %collective-permute-start.7 = (f32[2,16,128]{2,1,0:T(8,128)}, f32[2,16,128]{2,1,0:T(8,128)S(1)}, u32[]{:S(2)}, u32[]{:S(2)}) collective-permute-start(f32[2,16,128]{2,1,0:T(8,128)} %get-tuple-element.28), channel_id=1, source_target_pairs={{1,0},{2,1},{3,2},{4,3},{5,4},{6,5},{7,6},{9,8},{10,9},{11,10},{12... | collective-permute-start | bytes 49160 | tf_op jit(solution)/shard_map/ppermute | solution.py:522
  111.4 5.9 %collective-permute-start.9 = (f32[2,9,16,128]{3,2,1,0:T(8,128)S(1)}, f32[2,9,16,128]{3,2,1,0:T(8,128)S(1)}, u32[]{:S(2)}, u32[]{:S(2)}) collective-permute-start(f32[2,9,16,128]{3,2,1,0:T(8,128)S(1)} %pad_maximum_fusion.7), channel_id=1, source_target_pairs={{64,0},{128,64},{192,128},{65,1},{129,65},{193,129},{66,2},{130,66... | collective-permute-start | bytes 442376 | tf_op jit(solution)/shard_map/ppermute | solution.py:522
  112.8 6.1 %collective-permute-start.8 = (f32[2,9,16,128]{3,2,1,0:T(8,128)S(1)}, f32[2,9,16,128]{3,2,1,0:T(8,128)S(1)}, u32[]{:S(2)}, u32[]{:S(2)}) collective-permute-start(f32[2,9,16,128]{3,2,1,0:T(8,128)S(1)} %pad_maximum_fusion.6), channel_id=1, source_target_pairs={{0,64},{64,128},{128,192},{1,65},{65,129},{129,193},{2,66},{66,130... | collective-permute-start | bytes 442376 | tf_op jit(solution)/shard_map/ppermute | solution.py:522
  117.3 29.2 %copy-start.3 = (f32[2,9,16,128]{3,2,1,0:T(8,128)}, f32[2,9,16,128]{3,2,1,0:T(8,128)S(1)}, u32[]{:S(2)}) copy-start(f32[2,9,16,128]{3,2,1,0:T(8,128)S(1)} %collective-permute-done.9.x_high_ref) | copy-start | bytes 442372
  118.9 27.6 %copy-start.4 = (f32[2,9,16,128]{3,2,1,0:T(8,128)}, f32[2,9,16,128]{3,2,1,0:T(8,128)S(1)}, u32[]{:S(2)}) copy-start(f32[2,9,16,128]{3,2,1,0:T(8,128)S(1)} %collective-permute-done.8.x_low_ref) | copy-start | bytes 442372
  118.9 27.5 %collective-permute-start.11 = (f32[2,36,8,128]{3,2,1,0:T(8,128)S(1)}, f32[2,36,8,128]{3,2,1,0:T(8,128)S(1)}, u32[]{:S(2)}, u32[]{:S(2)}) collective-permute-start(f32[2,36,8,128]{3,2,1,0:T(8,128)S(1)} %pad_maximum_fusion.5), channel_id=1, source_target_pairs={{8,0},{16,8},{24,16},{32,24},{40,32},{48,40},{56,48},{9,1},{17,9},... | collective-permute-start | bytes 884744 | tf_op jit(solution)/shard_map/ppermute | solution.py:522
  123.6 22.8 %collective-permute-start.10 = (f32[2,36,8,128]{3,2,1,0:T(8,128)S(1)}, f32[2,36,8,128]{3,2,1,0:T(8,128)S(1)}, u32[]{:S(2)}, u32[]{:S(2)}) collective-permute-start(f32[2,36,8,128]{3,2,1,0:T(8,128)S(1)} %pad_maximum_fusion.4), channel_id=1, source_target_pairs={{0,8},{8,16},{16,24},{24,32},{32,40},{40,48},{48,56},{1,9},{9,17},... | collective-permute-start | bytes 884744 | tf_op jit(solution)/shard_map/ppermute | solution.py:522
  125.6 20.9 %all-to-all-start.2 = ((f32[256,1,128]{2,1,0:T(1,128)}), f32[256,1,128]{2,1,0:T(1,128)S(1)}, u32[]{:S(2)}, u32[]{:S(2)}) async-start(f32[256,1,128]{2,1,0:T(1,128)} %bitcast.18), calls=%async_computation.2 | async-start | bytes 262144 | tf_op jit(solution)/shard_map/all_to_all | solution.py:643
  146.4 0.6 copy-start.7
  146.4 0.8 copy-start.8
  146.5 0.8 copy-start.9
  178.7 9.7 %all-to-all-start.3 = ((f32[8,1,128]{2,1,0:T(1,128)}), f32[8,1,128]{2,1,0:T(1,128)S(1)}, u32[]{:S(2)}, u32[]{:S(2)}) async-start(f32[8,1,128]{2,1,0:T(1,128)} %bitcast.41), calls=%async_computation.3 | async-start | bytes 8192 | tf_op jit(solution)/shard_map/all_to_all | solution.py:668

commit v2 on v1

--- a/solution.py
+++ b/solution.py
@@ -18,14 +18,31 @@
 ROWS = 160
 FIRST = 16
 TILES = 18
+UNROLL = 18
+PART_ROWS = 2
+SUM_ROWS = 40
+SETUP = 6
+LAST = 4
 f32 = jnp.float32
 bf16 = jnp.bfloat16
 VMEM = pl.BlockSpec(memory_space=pltpu.VMEM)
 SMEM = pl.BlockSpec(memory_space=pltpu.SMEM)
-
-
-def params():
-    return pltpu.CompilerParams(vmem_limit_bytes=56 * 1024 * 1024)
+HBM = pl.BlockSpec(memory_space=pltpu.HBM)
+
+
+LONG = pl.CostEstimate(flops=0, bytes_accessed=160 * 1024 * 1024, transcendentals=0)
+
+
+def params(mebibytes=24):
+    return pltpu.CompilerParams(vmem_limit_bytes=mebibytes * 1024 * 1024)
+
+
+def in_hbm(*arrays):
+    return [pltpu.with_memory_space_constraint(array, pltpu.HBM) for array in arrays]
+
+
+def copies(sources, targets, sems):
+    return [pltpu.make_async_copy(s, t, sems.at[n]) for n, (s, t) in enumerate(zip(sources, targets))]
 
 
 def iota(shape, dim):
@@ -39,18 +56,6 @@
         found = jnp.take_along_axis(line, low, axis=1)
         value = found if row == 0 else jnp.where(high == row, found, value)
     return value
-
-
-def lookup_long(table_ref, rows, low, high):
-    def step(row, values):
-        line = jnp.broadcast_to(table_ref[pl.ds(row, 1), :], (8, 128))
-        return tuple(
-            jnp.where(high[8 * h : 8 * h + 8] == row, jnp.take_along_axis(line, low[8 * h : 8 * h + 8], axis=1), values[h])
-            for h in range(2)
-        )
-
-    zero = jnp.zeros((8, 128), f32)
-    return jnp.concatenate(lax.fori_loop(0, rows, step, (zero, zero), unroll=8), axis=0)
 
 
 def split_value(value, pieces):
@@ -77,34 +82,74 @@
     return total[0:8] + total[16:24] + total[32:40]
 
 
+def mark_rows(cell, high_ref):
+    high = jnp.right_shift(cell, 7)
+    row = iota((256, 128), 0)
+    for t in range(16):
+        high_ref[:, 128 * t : 128 * t + 128] = jnp.where(row == high[t : t + 1], 1.0, 0.0).astype(bf16)
+
+
+def sample(flat, cell, high_ref):
+    parts = split_value(flat.T, 2)
+    left = jnp.concatenate(parts, axis=0).astype(bf16)
+    low = jnp.bitwise_and(cell, 127)
+    row = iota((128, 128), 0)
+    out = []
+    for t in range(0, 16, 2):
+        found = jnp.dot(left, high_ref[:, 128 * t : 128 * t + 256], preferred_element_type=f32)
+        found = found[0:128] + found[128:256]
+        for u in range(2):
+            mask = row == low[t + u : t + u + 1]
+            out.append(jnp.sum(jnp.where(mask, found[:, 128 * u : 128 * u + 128], 0.0), axis=0, keepdims=True))
+    return jnp.concatenate(out, axis=0)
+
+
 def open_circuit(surface_conc):
     return 0.4 * jnp.tanh(3.0 * (0.5 - surface_conc))
 
 
 def prepare_kernel(
-    conc_ref,
-    cond_ref,
-    phase_ref,
+    place_ref,
     count_ref,
-    cell_ref,
-    label_ref,
-    area_ref,
-    rate_ref,
-    owner_ref,
-    shells_ref,
-    shell_conc_ref,
+    cell_hbm,
+    label_hbm,
+    owner_hbm,
+    area_hbm,
+    rate_hbm,
+    conc_hbm,
+    cond_hbm,
+    phase_hbm,
+    shells_hbm,
+    shell_conc_hbm,
     fields_ref,
-    z_low_ref,
-    z_high_ref,
+    z_first_ref,
+    z_second_ref,
     column_ref,
     position_ref,
-    flat_ref,
     owner_f_ref,
     high_ref,
     value_ref,
     left_ref,
     right_ref,
+    cell_ref,
+    label_ref,
+    owner_ref,
+    area_ref,
+    rate_ref,
+    conc_ref,
+    cond_ref,
+    phase_ref,
+    shells_ref,
+    shell_conc_ref,
+    sems,
 ):
+    held = (cell_ref, label_ref, owner_ref, area_ref, rate_ref, conc_ref, cond_ref, phase_ref, shells_ref, shell_conc_ref)
+    given = (cell_hbm, label_hbm, owner_hbm, area_hbm, rate_hbm, conc_hbm, cond_hbm, phase_hbm, shells_hbm, shell_conc_hbm)
+    reads = copies(given, held, sems)
+    for read in reads:
+        read.start()
+    for read in reads:
+        read.wait()
     lane = iota((16, 128), 1)
     slot = iota((16, 128), 0) * 128 + lane
     live = (slot < count_ref[0, 0, 0]).astype(f32)
@@ -120,17 +165,15 @@
     weight = live * area * rate_ref[...]
     cell = cell_ref[...]
     cell_low = jnp.bitwise_and(cell, 127)
-    cell_high = jnp.right_shift(cell, 7)
+    mark_rows(cell, high_ref)
 
     parts = split_value(weight, 2) + [
         jnp.right_shift(position, 3).astype(f32),
         jnp.bitwise_and(position, 7).astype(f32),
     ]
-    row_high = iota((256, 128), 0)
     row_low = iota((128, 128), 0)
     for t in range(16):
         columns = slice(128 * t, 128 * t + 128)
-        high_ref[:, columns] = jnp.where(row_high == cell_high[t : t + 1], 1.0, 0.0).astype(bf16)
         mask = row_low == cell_low[t : t + 1]
         for n, part in enumerate(parts):
             value_ref[128 * n : 128 * n + 128, columns] = jnp.where(mask, part[t : t + 1], 0.0).astype(bf16)
@@ -148,11 +191,9 @@
             mask = jnp.right_shift(lane, 3) == x
             z_low = jnp.where(mask, pltpu.roll(plane, 8 * x, 1) if x else plane, z_low)
             z_high = jnp.where(mask, pltpu.roll(plane, (8 * x + 8) % 128, 1) if x < 15 else plane, z_high)
-        z_low_ref[f] = z_low
-        z_high_ref[f] = z_high
-
-    flat_ref[...] = conc_ref[...].reshape(256, 128)
-    sampled = lookup_long(flat_ref, 256, cell_low, cell_high)
+        z_first_ref[f], z_second_ref[f] = give(place_ref[6] == 0, z_low, z_high)
+
+    sampled = sample(conc_ref[...].reshape(256, 128), cell, high_ref)
     summed = by_particle(weight * (1.0 + 0.5 * jnp.tanh(sampled)), position, left_ref, right_ref)
     surface_shell = iota((64, 128), 0) == shells_ref[...] - 1
     surface = jnp.sum(jnp.where(surface_shell, shell_conc_ref[...], 0.0), axis=0, keepdims=True)
@@ -177,7 +218,8 @@
     slope = jnp.sum(weight * (0.5 * (growth + shrink)), axis=0, keepdims=True)
     block = jnp.concatenate([circuit, current, slope, area, jnp.zeros((5, 128), f32)], axis=0)
     for n in range(sums_ref.shape[0]):
-        sums_ref[n] = block
+        sums_ref[n, 0:16] = block
+        sums_ref[n, 16:SUM_ROWS] = jnp.zeros((SUM_ROWS - 16, 128), f32)
 
 
 def total_of(value):
@@ -202,19 +244,18 @@
         wide_ref[n, FIRST + 136 : ROWS] = jnp.zeros((8, 128), f32)
 
 
-def loader(f, centre_ref, ends_ref, x_low_ref, x_high_ref, y_low_ref, y_high_ref):
+def loader(f, place_ref, centre_ref, ends_ref, x_first_ref, x_second_ref, y_first_ref, y_second_ref):
+    even_x, even_y = place_ref[4] == 0, place_ref[5] == 0
+
     def load(plane, tile):
-        if tile == 0:
-            return y_low_ref[f, plane]
-        if tile == 3:
-            return y_high_ref[f, plane]
+        if tile in (0, 3):
+            return take(even_y, y_first_ref[f, plane], y_second_ref[f, plane])[tile // 3]
         rows = slice(8 * tile - 8, 8 * tile)
         if plane < 16:
             return centre_ref[f, plane, rows]
-        if plane < 25:
-            return x_low_ref[f, plane - 16, rows]
         if plane < 34:
-            return x_high_ref[f, plane - 25, rows]
+            side, n = divmod(plane - 16, 9)
+            return take(even_x, x_first_ref[f, n, rows], x_second_ref[f, n, rows])[side]
         return ends_ref[f, plane - 34, rows]
 
     return load
@@ -240,16 +281,16 @@
     return low, high
 
 
-def tiles(body, first=0, last=TILES):
+def tiles(body, first=0, last=TILES, unroll=1):
     def step(n, carry):
         body(pl.multiple_of(8 + 8 * n, 8))
         return carry
 
-    lax.fori_loop(first, last, step, 0)
+    lax.fori_loop(first, last, step, 0, unroll=unroll)
 
 
 def solve(c_ref, p_ref, start_ref, k_ref, w_ref, circuit_ref, solid, work):
-    fx, fy, fz, rc, rp, gc, gp, coup, dc, dp = work
+    fx, fy, fz, rc, rp, gc, gp, coup, dc, dp, dc_next, dp_next = work
 
     def set_faces(r):
         k = [k_ref[n, pl.ds(r, 8)] for n in range(8)]
@@ -261,11 +302,10 @@
 
     for n in range(8):
         fz[n, FIRST + 136 : ROWS] = jnp.zeros((8, 128), f32)
-        for ref in (dc, dp):
-            for b in range(2):
-                ref[b, n, 0 : FIRST - 8] = jnp.zeros((8, 128), f32)
-                ref[b, n, FIRST + 136 : ROWS] = jnp.zeros((8, 128), f32)
-    tiles(set_faces)
+        for ref in (dc, dp, dc_next, dp_next):
+            ref[n, 0 : FIRST - 8] = jnp.zeros((8, 128), f32)
+            ref[n, FIRST + 136 : ROWS] = jnp.zeros((8, 128), f32)
+    tiles(set_faces, unroll=SETUP)
 
     def faces(r):
         lower = [fx[n, pl.ds(r, 8)] for n in range(8)]
@@ -307,15 +347,12 @@
             gc[n, rows] = recip_c
             gp[n, rows] = recip_p
             coup[n, rows] = conc_coupling * uptake
-            dc[0, n, rows] = rhs_c * recip_c
-            dp[0, n, rows] = rhs_p * recip_p
-
-    tiles(set_system)
-
-    def iteration(m, carry):
-        now, then = m % 2, (m + 1) % 2
-        c_now, p_now, c_then, p_then = dc.at[now], dp.at[now], dc.at[then], dp.at[then]
-
+            dc[n, rows] = rhs_c * recip_c
+            dp[n, rows] = rhs_p * recip_p
+
+    tiles(set_system, unroll=SETUP)
+
+    def iteration(c_now, p_now, c_then, p_then):
         def relax(r):
             rows = pl.ds(r, 8)
             c = [c_now[n, rows] for n in range(8)]
@@ -328,42 +365,54 @@
                 c_then[n, rows] = (rc[n, rows] + next_c + coup[n, rows] * p[n]) * gc[n, rows]
                 p_then[n, rows] = (rp[n, rows] + next_p) * gp[n, rows]
 
-        tiles(relax)
+        tiles(relax, unroll=UNROLL)
+
+    def pair(_, carry):
+        iteration(dc, dp, dc_next, dp_next)
+        iteration(dc_next, dp_next, dc, dp)
         return carry
 
-    lax.fori_loop(0, ITERS - 1, iteration, 0)
-    last = (ITERS - 1) % 2
-    return dc.at[last], dp.at[last]
+    lax.fori_loop(0, (ITERS - 1) // 2, pair, 0)
+    if ITERS % 2 == 0:
+        iteration(dc, dp, dc_next, dp_next)
+        return dc_next, dp_next
+    return dc, dp
 
 
 def first_kernel(
-    coords_ref,
+    place_ref,
     current_ref,
     centre_ref,
     ends_ref,
-    x_low_ref,
-    x_high_ref,
-    y_low_ref,
-    y_high_ref,
+    x_first_ref,
+    x_second_ref,
+    y_first_ref,
+    y_second_ref,
     sums_ref,
+    start_hbm,
+    k_hbm,
+    w_hbm,
+    circuit_hbm,
+    fields_ref,
+    z_first_ref,
+    z_second_ref,
+    part_ref,
+    state_ref,
     start_ref,
     k_ref,
     w_ref,
     circuit_ref,
-    fields_ref,
-    z_low_ref,
-    z_high_ref,
-    part_ref,
-    state_ref,
+    sems,
     c_ref,
     table_ref,
     *work,
 ):
-    pieces = (centre_ref, ends_ref, x_low_ref, x_high_ref, y_low_ref, y_high_ref)
+    writes = copies((start_ref, k_ref, w_ref, circuit_ref), (start_hbm, k_hbm, w_hbm, circuit_hbm), sems)
+    pieces = (place_ref, centre_ref, ends_ref, x_first_ref, x_second_ref, y_first_ref, y_second_ref)
     widen(loader(0, *pieces), start_ref)
     widen(loader(1, *pieces), k_ref)
     widen(loader(2, *pieces), w_ref)
-    at_x, at_y, size_x, size_y = coords_ref[0], coords_ref[1], coords_ref[2], coords_ref[3]
+    at_x, at_y, size_x, size_y = place_ref[0], place_ref[1], place_ref[2], place_ref[3]
     for i in range(3):
         for j in range(3):
             near_x = jnp.clip(at_x + (i - 1), 0, size_x - 1)
@@ -380,6 +429,8 @@
         )
 
     widen(circuit, circuit_ref)
+    for write in writes:
+        write.start()
 
     sums = sums_ref[0, 8:16]
     for n in range(1, sums_ref.shape[0]):
@@ -408,17 +459,17 @@
             weight = weight + factor * (0.5 * (growth + shrink))
         return total, weight
 
-    total, weight = lax.fori_loop(1, TILES - 1, finish, (zero, zero))
+    total, weight = lax.fori_loop(1, TILES - 1, finish, (zero, zero), unroll=LAST)
     total = total_of(jnp.where(mine, total, 0.0))
     weight = total_of(jnp.where(mine, weight, 0.0))
     row = iota((8, 128), 1)
     block = jnp.where(row == 0, total, jnp.where(row == 1, weight, 0.0))
 
     def spread(n, carry):
-        part_ref[pl.ds(pl.multiple_of(8 * n, 8), 8)] = block
+        part_ref[n] = block[: part_ref.shape[1]]
         return carry
 
-    lax.fori_loop(0, part_ref.shape[0] // 8, spread, 0)
+    lax.fori_loop(0, part_ref.shape[0], spread, 0, unroll=8)
     state_ref[...] = jnp.where(row == 0, solid, jnp.where(row == 1, area, 0.0))
     for f, ref in enumerate((c_ref, dp)):
 
@@ -426,42 +477,56 @@
             fields_ref[f, plane] = value
 
         narrow(ref, store)
-        z_low_ref[f], z_high_ref[f] = end_slabs(ref)
+        z_first_ref[f], z_second_ref[f] = give(place_ref[6] == 0, *end_slabs(ref))
+    for write in writes:
+        write.wait()
 
 
 def second_kernel(
+    place_ref,
     current_ref,
     centre_ref,
     ends_ref,
-    x_low_ref,
-    x_high_ref,
-    y_low_ref,
-    y_high_ref,
+    x_first_ref,
+    x_second_ref,
+    y_first_ref,
+    y_second_ref,
     part_ref,
     state_ref,
+    cell_ref,
+    position_ref,
+    start_hbm,
+    k_hbm,
+    w_hbm,
+    circuit_hbm,
+    conc_ref,
+    pot_ref,
+    flux_ref,
     start_ref,
     k_ref,
     w_ref,
     circuit_ref,
-    cell_ref,
-    position_ref,
-    conc_ref,
-    pot_ref,
-    flux_ref,
+    sems,
     c_ref,
     p_ref,
     flat_ref,
+    high_ref,
     left_ref,
     right_ref,
     *work,
 ):
-    pieces = (centre_ref, ends_ref, x_low_ref, x_high_ref, y_low_ref, y_high_ref)
+    pieces = (place_ref, centre_ref, ends_ref, x_first_ref, x_second_ref, y_first_ref, y_second_ref)
+    reads = copies((start_hbm, k_hbm, w_hbm, circuit_hbm), (start_ref, k_ref, w_ref, circuit_ref), sems)
+    for read in reads:
+        read.start()
     widen(loader(0, *pieces), c_ref)
     widen(loader(1, *pieces), p_ref)
-    sums = part_ref[0:8]
-    for n in range(1, part_ref.shape[0] // 8):
-        sums = sums + part_ref[8 * n : 8 * n + 8]
-    sums = jnp.sum(sums, axis=0, keepdims=True)
+    for read in reads:
+        read.wait()
+    sums = part_ref[0]
+    for n in range(1, part_ref.shape[0]):
+        sums = sums + part_ref[n]
+    sums = sums[0:1]
     current, slope = sums[:, 0:1], sums[:, 1:2]
     before, area = state_ref[0:1, 0:1], state_ref[0:1, 1:2]
     solid = before + (current_ref[0] * area - current) / slope
@@ -479,7 +544,7 @@
             factor = w_ref[m, rows] * (1.0 + 0.5 * jnp.tanh(c))
             flux[m, rows] = factor * (jnp.exp(0.5 * over) - jnp.exp(-0.5 * over))
 
-    tiles(finish, 1, TILES - 1)
+    tiles(finish, 1, TILES - 1, unroll=LAST)
 
     def store_conc(plane, value):
         conc_ref[plane] = value
@@ -492,7 +557,8 @@
 
     narrow(flux, store_flux)
     cell = cell_ref[...]
-    sampled = lookup_long(flat_ref, 256, jnp.bitwise_and(cell, 127), jnp.right_shift(cell, 7))
+    mark_rows(cell, high_ref)
+    sampled = sample(flat_ref[...], cell, high_ref)
     flux_ref[...] = by_particle(sampled, position_ref[...], left_ref, right_ref)
     narrow(c_ref, store_conc)
     narrow(p_ref, store_pot)
@@ -515,30 +581,78 @@
     column_ref[...] = jnp.concatenate(column, axis=0) * keep
 
 
-def swap(low, high, axis):
+def trade(first, second, axis):
     count = lax.axis_size(axis)
-    up = [(i, i + 1) for i in range(count - 1)]
-    down = [(i + 1, i) for i in range(count - 1)]
-    return lax.ppermute(high, axis, up), lax.ppermute(low, axis, down)
-
-
-def exchange(fields, z_low, z_high):
-    below, above = swap(z_low, z_high, "gz")
-    first = jnp.concatenate([below[..., :64], above[..., :64]], axis=2)
-    second = jnp.concatenate([below[..., 64:], above[..., 64:]], axis=2)
-    ends = jnp.stack([first, second], axis=1)
-    x_low, x_high = swap(
-        jnp.concatenate([fields[:, :8], ends[:, :1]], axis=1),
-        jnp.concatenate([fields[:, 8:], ends[:, 1:]], axis=1),
-        "gx",
-    )
-    whole = [fields, x_low, x_high, ends]
-    y_low, y_high = swap(
-        jnp.concatenate([part[:, :, :8] for part in whole], axis=1),
-        jnp.concatenate([part[:, :, 8:] for part in whole], axis=1),
-        "gy",
-    )
-    return fields, ends, x_low, x_high, y_low, y_high
+    pairs = [(i, i ^ 1) for i in range(count)]
+    others = [(i, i + 1) for i in range(1, count - 1, 2)]
+    others = others + [(target, source) for source, target in others]
+    return lax.ppermute(first, axis, pairs), lax.ppermute(second, axis, others)
+
+
+def give(even, low, high):
+    return jnp.where(even, high, low), jnp.where(even, low, high)
+
+
+def take(even, first, second):
+    return jnp.where(even, second, first), jnp.where(even, first, second)
+
+
+def pack_x_kernel(place_ref, fields_ref, z_first_ref, z_second_ref, *rest):
+    x_first_ref, x_second_ref, ends_ref = rest[-3:]
+    even_x, even_z = place_ref[4] == 0, place_ref[6] == 0
+    low_half = iota((16, 128), 1) < 64
+    for f in range(fields_ref.shape[0]):
+        below, above = take(even_z, z_first_ref[f], z_second_ref[f])
+        first = jnp.where(low_half, below, shift(above, 64))
+        second = jnp.where(low_half, shift(below, 64), above)
+        ends_ref[f, 0] = first
+        ends_ref[f, 1] = second
+        x_first_ref[f, 8], x_second_ref[f, 8] = give(even_x, first, second)
+        for n in range(8):
+            x_first_ref[f, n], x_second_ref[f, n] = give(even_x, fields_ref[f, n], fields_ref[f, 8 + n])
+
+
+def pack_y_kernel(place_ref, fields_ref, ends_ref, x_first_ref, x_second_ref, y_first_ref, y_second_ref):
+    even_x, even_y = place_ref[4] == 0, place_ref[5] == 0
+
+    def put(f, plane, value):
+        y_first_ref[f, plane], y_second_ref[f, plane] = give(even_y, value[0:8], value[8:16])
+
+    for f in range(fields_ref.shape[0]):
+        for n in range(16):
+            put(f, n, fields_ref[f, n])
+        for n in range(9):
+            low, high = take(even_x, x_first_ref[f, n], x_second_ref[f, n])
+            put(f, 16 + n, low)
+            put(f, 25 + n, high)
+        for n in range(2):
+            put(f, 34 + n, ends_ref[f, n])
+
+
+def exchange(place, fields, z_first, z_second, before=()):
+    count = fields.shape[0]
+    z_first, z_second = trade(z_first, z_second, "gz")
+    x_first, x_second, ends = pl.pallas_call(
+        pack_x_kernel,
+        in_specs=[SMEM] + [VMEM] * 3 + [HBM] * len(before),
+        out_specs=[VMEM] * 3,
+        out_shape=[shape(count, 9, 16, 128), shape(count, 9, 16, 128), shape(count, 2, 16, 128)],
+        compiler_params=params(8),
+        cost_estimate=LONG,
+        name="pack_x",
+    )(place, fields, z_first, z_second, *in_hbm(*before))
+    x_first, x_second = trade(x_first, x_second, "gx")
+    y_first, y_second = pl.pallas_call(
+        pack_y_kernel,
+        in_specs=[SMEM] + [VMEM] * 4,
+        out_specs=[VMEM] * 2,
+        out_shape=[shape(count, 36, 8, 128)] * 2,
+        compiler_params=params(8),
+        cost_estimate=LONG,
+        name="pack_y",
+    )(place, fields, ends, x_first, x_second)
+    y_first, y_second = trade(y_first, y_second, "gy")
+    return fields, ends, x_first, x_second, y_first, y_second
 
 
 def shape(*dims, dtype=f32):
@@ -550,7 +664,7 @@
 
 
 def work_scratch():
-    return wide_scratch(8) + [pltpu.VMEM((2, 8, ROWS, 128), f32) for _ in range(2)]
+    return wide_scratch(12)
 
 
 def on_device(
@@ -569,12 +683,26 @@
     shell_inverse,
 ):
     size_x, size_y, size_z = (lax.axis_size(a) for a in ("gx", "gy", "gz"))
+    at = [lax.axis_index(a) for a in ("gx", "gy", "gz")]
+    place = jnp.stack(at[:2] + [size_x, size_y] + [a % 2 for a in at]).astype(jnp.int32)
     cell = slot_cell.reshape(16, 128)
     shells = shell_count.reshape(1, 128)
     conc = shell_conc.reshape(64, 128)
-    fields, z_low, z_high, column, position = pl.pallas_call(
+    given = (
+        cell,
+        slot_label.reshape(16, 128),
+        owner_map.reshape(8, 128),
+        slot_area.reshape(16, 128),
+        slot_rate.reshape(16, 128),
+        electrolyte,
+        conductivity,
+        phase_label,
+        shells,
+        conc,
+    )
+    fields, z_first, z_second, column, position = pl.pallas_call(
         prepare_kernel,
-        in_specs=[VMEM] * 3 + [SMEM] + [VMEM] * 7,
+        in_specs=[SMEM] * 2 + [HBM] * 10,
         out_specs=[VMEM] * 5,
         out_shape=[
             shape(4, 16, 16, 128),
@@ -584,74 +712,66 @@
             shape(16, 128, dtype=jnp.int32),
         ],
         scratch_shapes=[
-            pltpu.VMEM((256, 128), f32),
             pltpu.VMEM((8, 128), f32),
             pltpu.VMEM((256, 2048), bf16),
             pltpu.VMEM((512, 2048), bf16),
             pltpu.VMEM((48, 2048), bf16),
             pltpu.VMEM((128, 2048), bf16),
-        ],
-        compiler_params=params(),
+        ]
+        + [pltpu.VMEM(array.shape, array.dtype) for array in given]
+        + [pltpu.SemaphoreType.DMA((len(given),))],
+        compiler_params=params(12),
         name="prepare",
-    )(
-        electrolyte,
-        conductivity,
-        phase_label,
-        slot_count,
-        cell,
-        slot_label.reshape(16, 128),
-        slot_area.reshape(16, 128),
-        slot_rate.reshape(16, 128),
-        owner_map.reshape(8, 128),
-        shells,
-        conc,
-    )
-    pieces = exchange(fields, z_low, z_high)
+    )(place, slot_count, *in_hbm(*given))
     column = lax.all_to_all(column, "gz", 0, 0, tiled=True)
+    pieces = exchange(place, fields, z_first, z_second, (column,))
     sums = pl.pallas_call(
         column_kernel,
         in_specs=[VMEM],
         out_specs=VMEM,
-        out_shape=shape(size_x * size_y, 16, 128),
-        compiler_params=params(),
+        out_shape=shape(size_x * size_y, SUM_ROWS, 128),
+        compiler_params=params(4),
         name="column",
     )(column)
     sums = lax.all_to_all(sums, ("gx", "gy"), 0, 0, tiled=True)
-    coords = jnp.stack([lax.axis_index("gx"), lax.axis_index("gy"), jnp.int32(size_x), jnp.int32(size_y)]).astype(jnp.int32)
     wide = shape(8, ROWS, 128)
     devices = size_x * size_y * size_z
-    start, k, w, circuit, fields, z_low, z_high, part, state = pl.pallas_call(
+    start, k, w, circuit, fields, z_first, z_second, part, state = pl.pallas_call(
         first_kernel,
         in_specs=[SMEM] * 2 + [VMEM] * 7,
-        out_specs=[VMEM] * 9,
+        out_specs=[HBM] * 4 + [VMEM] * 5,
         out_shape=[
-            wide,
-            wide,
-            wide,
-            wide,
+            *[pltpu.HBM(wide.shape, f32)] * 4,
             shape(2, 16, 16, 128),
             shape(2, 16, 128),
             shape(2, 16, 128),
-            shape(devices, 128),
+            shape(devices, PART_ROWS, 128),
             shape(8, 128),
         ],
-        scratch_shapes=wide_scratch(1) + [pltpu.VMEM((9, 8, 128), f32)] + work_scratch(),
+        scratch_shapes=wide_scratch(4)
+        + [pltpu.SemaphoreType.DMA((4,))]
+        + wide_scratch(1)
+        + [pltpu.VMEM((9, 8, 128), f32)]
+        + work_scratch(),
         compiler_params=params(),
         name="first_sweep",
-    )(coords, applied_current, *pieces, sums)
-    pieces = exchange(fields, z_low, z_high)
+    )(place, applied_current, *pieces, sums)
+    pieces = exchange(place, fields, z_first, z_second)
     part = lax.all_to_all(part, ("gx", "gy", "gz"), 0, 0, tiled=True)
     concentration, potential, flux = pl.pallas_call(
         second_kernel,
-        in_specs=[SMEM] + [VMEM] * 14,
+        in_specs=[SMEM] * 2 + [VMEM] * 10 + [HBM] * 4,
         out_specs=[VMEM] * 3,
         out_shape=[shape(16, 16, 128), shape(16, 16, 128), shape(8, 128)],
-        scratch_shapes=wide_scratch(2)
-        + [pltpu.VMEM((256, 128), f32), pltpu.VMEM((48, 2048), bf16), pltpu.VMEM((128, 2048), bf16)]
+        scratch_shapes=wide_scratch(4)
+        + [pltpu.SemaphoreType.DMA((4,))]
+        + wide_scratch(2)
+        + [pltpu.VMEM((256, 128), f32), pltpu.VMEM((256, 2048), bf16)]
+        + [pltpu.VMEM((48, 2048), bf16), pltpu.VMEM((128, 2048), bf16)]
         + work_scratch(),
         compiler_params=params(),
         name="second_sweep",
-    )(applied_current, *pieces, part, state, start, k, w, circuit, cell, position)
+    )(place, applied_current, *pieces, part, state, cell, position, *in_hbm(start, k, w, circuit))
     base, surface_column = pl.pallas_call(
         shell_kernel,
         grid=(8,),
@@ -662,7 +782,7 @@
         ],
         out_specs=[pl.BlockSpec((8, 128), lambda i: (i, 0))] * 2,
         out_shape=[shape(64, 128)] * 2,
-        compiler_params=params(),
+        compiler_params=params(8),
         name="shells",
     )(shell_inverse.reshape(64, 64, 128), shells, conc)
     flux = jnp.sum(lax.all_to_all(flux, "gz", 0, 0, tiled=True), axis=0, keepdims=True)

time: 191 us -> 136 us (0.71)
  the two profiles are of different devices: /device:TPU:1 before, /device:TPU:12 now
where the time goes in v2:
time: 136 us
  starting transfers between devices  53.8 us (40%)
  Pallas kernels  37.5 us (28%)
  waiting for transfers between devices  37.3 us (27%)
  local copies, waits for them, and re-layouts  4.27 us (3%)
  between operations  2.18 us (2%)
    pallas_call x1, Pallas kernels, on_device(): pl.pallas_call(second_kernel, in_specs=[SMEM] * 2 + [VMEM] * 10 + [HBM] *...  14.3 us
    ppermute x6, waiting for transfers between devices, trade(): lax.ppermute(second, axis, others)  13.8 us
    pallas_call x1, Pallas kernels, on_device(): pl.pallas_call(first_kernel, in_specs=[SMEM] * 2 + [VMEM] * 7, out_specs=...  13.6 us
    all_to_all x1, starting transfers between devices, on_device(): part = lax.all_to_all(part, ('gx', 'gy', 'gz'), 0, 0, tiled=True)  12.4 us
    ppermute x6, starting transfers between devices, trade(): lax.ppermute(second, axis, others)  10 us
    ppermute x6, waiting for transfers between devices, trade(): lax.ppermute(first, axis, pairs)  8.74 us
    all_to_all x1, starting transfers between devices, on_device(): lax.all_to_all(flux, 'gz', 0, 0, tiled=True)  8.64 us
    all_to_all x1, starting transfers between devices, on_device(): column = lax.all_to_all(column, 'gz', 0, 0, tiled=True)  8.47 us
  transfers between devices with their start and end apart: 16, of which 9 were waited for; matrix products, arithmetic and copies ran while one was open for 0% of the time, Pallas kernels for 3%

profile of v2, /device:TPU:12, one launch (start us, length us, event | category | flops | bytes accessed | tf_op | source)
XLA Modules:
  0.0 135.7 jit_solution(14037772359954238850)
XLA Ops:
  1.3 0.1 stack.23.place_ref
  1.4 4.6 %prepare.1 = (f32[4,16,16,128]{3,2,1,0:T(8,128)S(1)}, f32[4,16,128]{2,1,0:T(8,128)S(1)}, f32[4,16,128]{2,1,0:T(8,128)S(1)}, f32[8,16,128]{2,1,0:T(8,128)}, s32[16,128]{1,0:T(8,128)S(1)}) custom-call(s32[7]{0:T(128)S(1)} %stack.23.place_ref, s32[1,1,1]{2,1,0:T(1,128)S(6)} %copy.18.count_ref, s32[16,128]{1,0:T(8,128)} %bitcast.21, s32[16,128]{1,0:T(8,128)} %bitcast.25, ...), custom_call_target="tpu_custom_call" | custom-call | tf_op jit(solution)/shard_map/prepare/pallas_call | solution.py:703
  6.0 0.0 copy-start.7
  6.0 0.6 copy-done.7
  6.6 8.5 %all-to-all-start = ((f32[8,16,128]{2,1,0:T(8,128)}), f32[8,16,128]{2,1,0:T(8,128)S(1)}, u32[]{:S(2)}, u32[]{:S(2)}) async-start(f32[8,16,128]{2,1,0:T(8,128)} %get-tuple-element.35), calls=%async_computation | async-start | bytes 131072 | tf_op jit(solution)/shard_map/all_to_all | solution.py:726
  15.0 2.0 %collective-permute-start = (f32[4,16,128]{2,1,0:T(8,128)S(1)}, f32[4,16,128]{2,1,0:T(8,128)S(1)}, u32[]{:S(2)}, u32[]{:S(2)}) collective-permute-start(f32[4,16,128]{2,1,0:T(8,128)S(1)} %get-tuple-element.33), channel_id=1, source_target_pairs={{0,1},{1,0},{2,3},{3,2},{4,5},{5,4},{6,7},{7,6},{8,9},{9,8},{10,11... | collective-permute-start | bytes 98312 | tf_op jit(solution)/shard_map/ppermute | solution.py:589
  17.1 0.7 collective-permute-start.1
  17.7 2.0 %collective-permute-done.z_first_ref = f32[4,16,128]{2,1,0:T(8,128)S(1)} collective-permute-done((f32[4,16,128]{2,1,0:T(8,128)S(1)}, f32[4,16,128]{2,1,0:T(8,128)S(1)}, u32[]{:S(2)}, u32[]{:S(2)}) %collective-permute-start) | collective-permute-done | bytes 32800 | tf_op jit(solution)/shard_map/ppermute | solution.py:589
  19.7 0.0 collective-permute-done.1.z_second_ref
  19.7 3.7 %all-to-all-done.rest_0_.column_ref = f32[8,16,128]{2,1,0:T(8,128)S(1)} async-done(((f32[8,16,128]{2,1,0:T(8,128)}), f32[8,16,128]{2,1,0:T(8,128)S(1)}, u32[]{:S(2)}, u32[]{:S(2)}) %all-to-all-start) | async-done | bytes 65568 | tf_op jit(solution)/shard_map/all_to_all | solution.py:726
  23.4 0.0 copy-start.1
  23.4 0.6 copy-done.1
  24.1 0.6 pack_x.2
  24.7 1.3 collective-permute-start.2
  26.0 1.9 %collective-permute-start.3 = (f32[4,9,16,128]{3,2,1,0:T(8,128)S(1)}, f32[4,9,16,128]{3,2,1,0:T(8,128)S(1)}, u32[]{:S(2)}, u32[]{:S(2)}) collective-permute-start(f32[4,9,16,128]{3,2,1,0:T(8,128)S(1)} %get-tuple-element.38), channel_id=1, source_target_pairs={{64,128},{128,64},{65,129},{129,65},{66,130},{130,66},{67,131},{13... | collective-permute-start | bytes 884744 | tf_op jit(solution)/shard_map/ppermute | solution.py:589
  27.9 0.0 copy-start.2
  27.9 0.8 copy-done.2
  28.7 0.9 column.1
  29.6 7.5 %all-to-all-start.1 = ((f32[32,40,128]{2,1,0:T(8,128)}), f32[32,40,128]{2,1,0:T(8,128)S(1)}, u32[]{:S(2)}, u32[]{:S(2)}) async-start(f32[32,40,128]{2,1,0:T(8,128)} %column.1), calls=%async_computation.1 | async-start | bytes 1310720 | tf_op jit(solution)/shard_map/all_to_all | solution.py:736
  37.1 0.0 collective-permute-done.2.x_first_ref
  37.1 0.0 collective-permute-done.3.x_second_ref
  37.1 1.7 %pack_y.2 = (f32[4,36,8,128]{3,2,1,0:T(8,128)}, f32[4,36,8,128]{3,2,1,0:T(8,128)}) custom-call(s32[7]{0:T(128)S(1)} %stack.23.place_ref, f32[4,16,16,128]{3,2,1,0:T(8,128)S(1)} %get-tuple-element.32.fields_ref.centre_ref, f32[4,2,16,128]{3,2,1,0:T(8,128)S(1)} %get-tuple-element.36.ends_ref, f32[4,9,16,128]{3,2,1,0:T(8,128)S(1)} %collective-permute-done.2.x_first_ref, ...), custom_call_target="tpu_custom_call" | custom-call | bytes 167772160 | tf_op jit(solution)/shard_map/pack_y/pallas_call | solution.py:645
  38.8 0.1 collective-permute-start.4
  39.0 2.4 %collective-permute-start.5 = (f32[4,36,8,128]{3,2,1,0:T(8,128)}, f32[4,36,8,128]{3,2,1,0:T(8,128)S(1)}, u32[]{:S(2)}, u32[]{:S(2)}) collective-permute-start(f32[4,36,8,128]{3,2,1,0:T(8,128)} %get-tuple-element.40), channel_id=1, source_target_pairs={{8,16},{24,32},{40,48},{16,8},{32,24},{48,40},{9,17},{25,33},{41,4... | collective-permute-start | bytes 1769480 | tf_op jit(solution)/shard_map/ppermute | solution.py:589
  42.0 0.0 copy-start.6
  42.1 4.7 %all-to-all-done.1.sums_ref = f32[32,40,128]{2,1,0:T(8,128)S(1)} async-done(((f32[32,40,128]{2,1,0:T(8,128)}), f32[32,40,128]{2,1,0:T(8,128)S(1)}, u32[]{:S(2)}, u32[]{:S(2)}) %all-to-all-start.1) | async-done | bytes 655392 | tf_op jit(solution)/shard_map/all_to_all | solution.py:736
  46.7 0.0 collective-permute-done.4.y_first_ref
  46.7 5.4 %collective-permute-done.5.y_second_ref = f32[4,36,8,128]{3,2,1,0:T(8,128)S(1)} collective-permute-done((f32[4,36,8,128]{3,2,1,0:T(8,128)}, f32[4,36,8,128]{3,2,1,0:T(8,128)S(1)}, u32[]{:S(2)}, u32[]{:S(2)}) %collective-permute-start.5) | collective-permute-done | bytes 589856 | tf_op jit(solution)/shard_map/ppermute | solution.py:589
  52.1 13.6 %first_sweep.1 = (f32[8,160,128]{2,1,0:T(8,128)}, f32[8,160,128]{2,1,0:T(8,128)}, f32[8,160,128]{2,1,0:T(8,128)}, f32[8,160,128]{2,1,0:T(8,128)}, f32[2,16,16,12...) custom-call(s32[7]{0:T(128)S(1)} %stack.23.place_ref, ...), custom_call_target="tpu_custom_call" | custom-call | tf_op jit(solution)/shard_map/first_sweep/pallas_call | solution.py:739
  65.7 12.4 %all-to-all-start.2 = ((f32[256,2,128]{2,1,0:T(2,128)}), f32[256,2,128]{2,1,0:T(2,128)S(1)}, u32[]{:S(2)}, u32[]{:S(2)}) async-start(f32[256,2,128]{2,1,0:T(2,128)} %get-tuple-element.49), calls=%async_computation.2 | async-start | bytes 524288 | tf_op jit(solution)/shard_map/all_to_all | solution.py:760
  78.2 1.9 %collective-permute-start.6 = (f32[2,16,128]{2,1,0:T(8,128)S(1)}, f32[2,16,128]{2,1,0:T(8,128)S(1)}, u32[]{:S(2)}, u32[]{:S(2)}) collective-permute-start(f32[2,16,128]{2,1,0:T(8,128)S(1)} %get-tuple-element.42), channel_id=1, source_target_pairs={{0,1},{1,0},{2,3},{3,2},{4,5},{5,4},{6,7},{7,6},{8,9},{9,8},{10,11... | collective-permute-start | bytes 49160 | tf_op jit(solution)/shard_map/ppermute | solution.py:589
  80.1 0.7 collective-permute-start.7
  80.8 4.4 %collective-permute-done.6.z_first_ref = f32[2,16,128]{2,1,0:T(8,128)S(1)} collective-permute-done((f32[2,16,128]{2,1,0:T(8,128)S(1)}, f32[2,16,128]{2,1,0:T(8,128)S(1)}, u32[]{:S(2)}, u32[]{:S(2)}) %collective-permute-start.6) | collective-permute-done | bytes 16416 | tf_op jit(solution)/shard_map/ppermute | solution.py:589
  85.1 0.0 collective-permute-done.7.z_second_ref
  85.2 0.6 pack_x.3
  85.8 0.0 copy-start.4
  85.8 1.3 collective-permute-start.8
  87.0 1.9 %collective-permute-start.9 = (f32[2,9,16,128]{3,2,1,0:T(8,128)S(1)}, f32[2,9,16,128]{3,2,1,0:T(8,128)S(1)}, u32[]{:S(2)}, u32[]{:S(2)}) collective-permute-start(f32[2,9,16,128]{3,2,1,0:T(8,128)S(1)} %get-tuple-element.46), channel_id=1, source_target_pairs={{64,128},{128,64},{65,129},{129,65},{66,130},{130,66},{67,131},{13... | collective-permute-start | bytes 442376 | tf_op jit(solution)/shard_map/ppermute | solution.py:589
  89.0 2.4 %collective-permute-done.8.x_first_ref = f32[2,9,16,128]{3,2,1,0:T(8,128)S(1)} collective-permute-done((f32[2,9,16,128]{3,2,1,0:T(8,128)S(1)}, f32[2,9,16,128]{3,2,1,0:T(8,128)S(1)}, u32[]{:S(2)}, u32[]{:S(2)}) %collective-permute-start.8) | collective-permute-done | bytes 147488 | tf_op jit(solution)/shard_map/ppermute | solution.py:589
  91.3 2.7 %collective-permute-done.9.x_second_ref = f32[2,9,16,128]{3,2,1,0:T(8,128)S(1)} collective-permute-done((f32[2,9,16,128]{3,2,1,0:T(8,128)S(1)}, f32[2,9,16,128]{3,2,1,0:T(8,128)S(1)}, u32[]{:S(2)}, u32[]{:S(2)}) %collective-permute-start.9) | collective-permute-done | bytes 147488 | tf_op jit(solution)/shard_map/ppermute | solution.py:589
  94.1 0.6 pack_y.3
  94.7 0.0 copy-start
  94.7 0.0 copy-start.3
  94.7 0.1 collective-permute-start.10
  94.8 2.5 %collective-permute-start.11 = (f32[2,36,8,128]{3,2,1,0:T(8,128)S(1)}, f32[2,36,8,128]{3,2,1,0:T(8,128)S(1)}, u32[]{:S(2)}, u32[]{:S(2)}) collective-permute-start(f32[2,36,8,128]{3,2,1,0:T(8,128)S(1)} %get-tuple-element.48), channel_id=1, source_target_pairs={{8,16},{24,32},{40,48},{16,8},{32,24},{48,40},{9,17},{25,33},{41,4... | collective-permute-start | bytes 884744 | tf_op jit(solution)/shard_map/ppermute | solution.py:589
  97.3 0.0 collective-permute-done.10.y_first_ref
  97.3 0.0 copy-done.4
  97.3 5.7 %collective-permute-done.11.y_second_ref = f32[2,36,8,128]{3,2,1,0:T(8,128)S(1)} collective-permute-done((f32[2,36,8,128]{3,2,1,0:T(8,128)S(1)}, f32[2,36,8,128]{3,2,1,0:T(8,128)S(1)}, u32[]{:S(2)}, u32[]{:S(2)}) %collective-permute-start.11) | collective-permute-done | bytes 294944 | tf_op jit(solution)/shard_map/ppermute | solution.py:589
  103.0 0.0 all-to-all-done.2.part_ref
  103.0 0.0 copy-done.6
  103.0 0.0 copy-start.5
  103.0 0.8 copy-done.5
  103.7 0.0 copy-start.8
  103.7 0.7 copy-done.8
  104.4 14.3 %second_sweep.1 = (f32[16,16,128]{2,1,0:T(8,128)}, f32[16,16,128]{2,1,0:T(8,128)}, f32[8,128]{1,0:T(8,128)}) custom-call(s32[7]{0:T(128)S(1)} %stack.23.place_ref, f32[1]{0:T(128)S(6)} %copy.17.current_ref, f32[2,16,16,128]{3,2,1,0:T(8,128)S(1)} %get-tuple-element.41.fields_ref.centre_ref, f32[2,2,16,128]{3,2,1,0:T(8,128)S(1)} %copy-done.5, ...), custom_call_target="tpu_custom_call" | custom-call | tf_op jit(solution)/shard_map/second_sweep/pallas_call | solution.py:761
  118.8 8.6 %all-to-all-start.3 = ((f32[8,1,128]{2,1,0:T(1,128)}), f32[8,1,128]{2,1,0:T(1,128)S(1)}, u32[]{:S(2)}, u32[]{:S(2)}) async-start(f32[8,1,128]{2,1,0:T(1,128)} %bitcast.14), calls=%async_computation.3 | async-start | bytes 8192 | tf_op jit(solution)/shard_map/all_to_all | solution.py:788
  127.4 0.0 copy-done
  127.4 0.0 copy-done.3
  127.4 0.0 copy-start.9
  127.4 0.6 copy-done.9
  128.1 0.6 shells.1
  128.6 6.3 %all-to-all-done.3 = f32[8,1,128]{2,1,0:T(1,128)S(1)} async-done(((f32[8,1,128]{2,1,0:T(1,128)}), f32[8,1,128]{2,1,0:T(1,128)S(1)}, u32[]{:S(2)}, u32[]{:S(2)}) %all-to-all-start.3) | async-done | bytes 4128 | tf_op jit(solution)/shard_map/all_to_all | solution.py:788
  135.0 0.6 add_bitcast_fusion
  (2 shorter events, 0.0 us)
Async XLA Ops:
  6.0 0.6 copy-start.7
  6.6 16.8 %all-to-all-start = ((f32[8,16,128]{2,1,0:T(8,128)}), f32[8,16,128]{2,1,0:T(8,128)S(1)}, u32[]{:S(2)}, u32[]{:S(2)}) async-start(f32[8,16,128]{2,1,0:T(8,128)} %get-tuple-element.35), calls=%async_computation | async-start | bytes 131072 | tf_op jit(solution)/shard_map/all_to_all | solution.py:726
  15.0 4.6 %collective-permute-start = (f32[4,16,128]{2,1,0:T(8,128)S(1)}, f32[4,16,128]{2,1,0:T(8,128)S(1)}, u32[]{:S(2)}, u32[]{:S(2)}) collective-permute-start(f32[4,16,128]{2,1,0:T(8,128)S(1)} %get-tuple-element.33), channel_id=1, source_target_pairs={{0,1},{1,0},{2,3},{3,2},{4,5},{5,4},{6,7},{7,6},{8,9},{9,8},{10,11... | collective-permute-start | bytes 98312 | tf_op jit(solution)/shard_map/ppermute | solution.py:589
  17.1 2.6 %collective-permute-start.1 = (f32[4,16,128]{2,1,0:T(8,128)S(1)}, f32[4,16,128]{2,1,0:T(8,128)S(1)}, u32[]{:S(2)}, u32[]{:S(2)}) collective-permute-start(f32[4,16,128]{2,1,0:T(8,128)S(1)} %get-tuple-element.34), channel_id=1, source_target_pairs={{1,2},{3,4},{5,6},{2,1},{4,3},{6,5},{9,10},{11,12},{13,14},{10,9},... | collective-permute-start | bytes 98312 | tf_op jit(solution)/shard_map/ppermute | solution.py:589
  23.4 0.6 copy-start.1
  24.7 12.4 %collective-permute-start.2 = (f32[4,9,16,128]{3,2,1,0:T(8,128)S(1)}, f32[4,9,16,128]{3,2,1,0:T(8,128)S(1)}, u32[]{:S(2)}, u32[]{:S(2)}) collective-permute-start(f32[4,9,16,128]{3,2,1,0:T(8,128)S(1)} %get-tuple-element.37), channel_id=1, source_target_pairs={{0,64},{64,0},{128,192},{192,128},{1,65},{65,1},{129,193},{193,129... | collective-permute-start | bytes 884744 | tf_op jit(solution)/shard_map/ppermute | solution.py:589
  26.0 11.2 %collective-permute-start.3 = (f32[4,9,16,128]{3,2,1,0:T(8,128)S(1)}, f32[4,9,16,128]{3,2,1,0:T(8,128)S(1)}, u32[]{:S(2)}, u32[]{:S(2)}) collective-permute-start(f32[4,9,16,128]{3,2,1,0:T(8,128)S(1)} %get-tuple-element.38), channel_id=1, source_target_pairs={{64,128},{128,64},{65,129},{129,65},{66,130},{130,66},{67,131},{13... | collective-permute-start | bytes 884744 | tf_op jit(solution)/shard_map/ppermute | solution.py:589
  27.9 0.8 copy-start.2
  29.6 17.1 %all-to-all-start.1 = ((f32[32,40,128]{2,1,0:T(8,128)}), f32[32,40,128]{2,1,0:T(8,128)S(1)}, u32[]{:S(2)}, u32[]{:S(2)}) async-start(f32[32,40,128]{2,1,0:T(8,128)} %column.1), calls=%async_computation.1 | async-start | bytes 1310720 | tf_op jit(solution)/shard_map/all_to_all | solution.py:736
  38.8 7.9 %collective-permute-start.4 = (f32[4,36,8,128]{3,2,1,0:T(8,128)}, f32[4,36,8,128]{3,2,1,0:T(8,128)S(1)}, u32[]{:S(2)}, u32[]{:S(2)}) collective-permute-start(f32[4,36,8,128]{3,2,1,0:T(8,128)} %get-tuple-element.39), channel_id=1, source_target_pairs={{0,8},{8,0},{16,24},{24,16},{32,40},{40,32},{48,56},{56,48},{1,9},... | collective-permute-start | bytes 1769480 | tf_op jit(solution)/shard_map/ppermute | solution.py:589
  39.0 13.2 %collective-permute-start.5 = (f32[4,36,8,128]{3,2,1,0:T(8,128)}, f32[4,36,8,128]{3,2,1,0:T(8,128)S(1)}, u32[]{:S(2)}, u32[]{:S(2)}) collective-permute-start(f32[4,36,8,128]{3,2,1,0:T(8,128)} %get-tuple-element.40), channel_id=1, source_target_pairs={{8,16},{24,32},{40,48},{16,8},{32,24},{48,40},{9,17},{25,33},{41,4... | collective-permute-start | bytes 1769480 | tf_op jit(solution)/shard_map/ppermute | solution.py:589
  42.0 60.9 %copy-start.6 = (s32[1,1,2048]{2,1,0:T(1,128)S(1)}, s32[1,1,2048]{2,1,0:T(1,128)}, u32[]{:S(2)}) copy-start(s32[1,1,2048]{2,1,0:T(1,128)} %param.18) | copy-start | bytes 24580
  65.7 37.2 %all-to-all-start.2 = ((f32[256,2,128]{2,1,0:T(2,128)}), f32[256,2,128]{2,1,0:T(2,128)S(1)}, u32[]{:S(2)}, u32[]{:S(2)}) async-start(f32[256,2,128]{2,1,0:T(2,128)} %get-tuple-element.49), calls=%async_computation.2 | async-start | bytes 524288 | tf_op jit(solution)/shard_map/all_to_all | solution.py:760
  78.2 7.0 %collective-permute-start.6 = (f32[2,16,128]{2,1,0:T(8,128)S(1)}, f32[2,16,128]{2,1,0:T(8,128)S(1)}, u32[]{:S(2)}, u32[]{:S(2)}) collective-permute-start(f32[2,16,128]{2,1,0:T(8,128)S(1)} %get-tuple-element.42), channel_id=1, source_target_pairs={{0,1},{1,0},{2,3},{3,2},{4,5},{5,4},{6,7},{7,6},{8,9},{9,8},{10,11... | collective-permute-start | bytes 49160 | tf_op jit(solution)/shard_map/ppermute | solution.py:589
  80.1 5.0 %collective-permute-start.7 = (f32[2,16,128]{2,1,0:T(8,128)S(1)}, f32[2,16,128]{2,1,0:T(8,128)S(1)}, u32[]{:S(2)}, u32[]{:S(2)}) collective-permute-start(f32[2,16,128]{2,1,0:T(8,128)S(1)} %get-tuple-element.43), channel_id=1, source_target_pairs={{1,2},{3,4},{5,6},{2,1},{4,3},{6,5},{9,10},{11,12},{13,14},{10,9},... | collective-permute-start | bytes 49160 | tf_op jit(solution)/shard_map/ppermute | solution.py:589
  85.8 11.5 %copy-start.4 = (f32[2,2,16,128]{3,2,1,0:T(8,128)}, f32[2,2,16,128]{3,2,1,0:T(8,128)S(1)}, u32[]{:S(2)}) copy-start(f32[2,2,16,128]{3,2,1,0:T(8,128)S(1)} %get-tuple-element.44.ends_ref) | copy-start | bytes 98308
  85.8 5.6 %collective-permute-start.8 = (f32[2,9,16,128]{3,2,1,0:T(8,128)S(1)}, f32[2,9,16,128]{3,2,1,0:T(8,128)S(1)}, u32[]{:S(2)}, u32[]{:S(2)}) collective-permute-start(f32[2,9,16,128]{3,2,1,0:T(8,128)S(1)} %get-tuple-element.45), channel_id=1, source_target_pairs={{0,64},{64,0},{128,192},{192,128},{1,65},{65,1},{129,193},{193,129... | collective-permute-start | bytes 442376 | tf_op jit(solution)/shard_map/ppermute | solution.py:589
  87.0 7.0 %collective-permute-start.9 = (f32[2,9,16,128]{3,2,1,0:T(8,128)S(1)}, f32[2,9,16,128]{3,2,1,0:T(8,128)S(1)}, u32[]{:S(2)}, u32[]{:S(2)}) collective-permute-start(f32[2,9,16,128]{3,2,1,0:T(8,128)S(1)} %get-tuple-element.46), channel_id=1, source_target_pairs={{64,128},{128,64},{65,129},{129,65},{66,130},{130,66},{67,131},{13... | collective-permute-start | bytes 442376 | tf_op jit(solution)/shard_map/ppermute | solution.py:589
  94.7 32.7 %copy-start = (f32[1,1,64,64,128]{4,3,2,1,0:T(8,128)S(1)}, f32[1,1,64,64,128]{4,3,2,1,0:T(8,128)}, u32[]{:S(2)}) copy-start(f32[1,1,64,64,128]{4,3,2,1,0:T(8,128)} %param.25) | copy-start | bytes 6291460
  94.7 32.7 %copy-start.3 = (f32[1,1,64,128]{3,2,1,0:T(8,128)S(1)}, f32[1,1,64,128]{3,2,1,0:T(8,128)}, u32[]{:S(2)}) copy-start(f32[1,1,64,128]{3,2,1,0:T(8,128)} %param.24) | copy-start | bytes 98308
  94.7 2.6 %collective-permute-start.10 = (f32[2,36,8,128]{3,2,1,0:T(8,128)S(1)}, f32[2,36,8,128]{3,2,1,0:T(8,128)S(1)}, u32[]{:S(2)}, u32[]{:S(2)}) collective-permute-start(f32[2,36,8,128]{3,2,1,0:T(8,128)S(1)} %get-tuple-element.47), channel_id=1, source_target_pairs={{0,8},{8,0},{16,24},{24,16},{32,40},{40,32},{48,56},{56,48},{1,9},... | collective-permute-start | bytes 884744 | tf_op jit(solution)/shard_map/ppermute | solution.py:589
  94.8 8.2 %collective-permute-start.11 = (f32[2,36,8,128]{3,2,1,0:T(8,128)S(1)}, f32[2,36,8,128]{3,2,1,0:T(8,128)S(1)}, u32[]{:S(2)}, u32[]{:S(2)}) collective-permute-start(f32[2,36,8,128]{3,2,1,0:T(8,128)S(1)} %get-tuple-element.48), channel_id=1, source_target_pairs={{8,16},{24,32},{40,48},{16,8},{32,24},{48,40},{9,17},{25,33},{41,4... | collective-permute-start | bytes 884744 | tf_op jit(solution)/shard_map/ppermute | solution.py:589
  103.0 0.8 copy-start.5
  103.7 0.7 copy-start.8
  118.8 16.2 %all-to-all-start.3 = ((f32[8,1,128]{2,1,0:T(1,128)}), f32[8,1,128]{2,1,0:T(1,128)S(1)}, u32[]{:S(2)}, u32[]{:S(2)}) async-start(f32[8,1,128]{2,1,0:T(1,128)} %bitcast.14), calls=%async_computation.3 | async-start | bytes 8192 | tf_op jit(solution)/shard_map/all_to_all | solution.py:788
  127.4 0.7 copy-start.9

commit v3 on v2

--- a/solution.py
+++ b/solution.py
@@ -20,7 +20,7 @@
 TILES = 18
 UNROLL = 18
 PART_ROWS = 2
-SUM_ROWS = 40
+SUM_ROWS = 16
 SETUP = 6
 LAST = 4
 f32 = jnp.float32
@@ -219,7 +219,6 @@
     block = jnp.concatenate([circuit, current, slope, area, jnp.zeros((5, 128), f32)], axis=0)
     for n in range(sums_ref.shape[0]):
         sums_ref[n, 0:16] = block
-        sums_ref[n, 16:SUM_ROWS] = jnp.zeros((SUM_ROWS - 16, 128), f32)
 
 
 def total_of(value):
@@ -612,7 +611,8 @@
             x_first_ref[f, n], x_second_ref[f, n] = give(even_x, fields_ref[f, n], fields_ref[f, 8 + n])
 
 
-def pack_y_kernel(place_ref, fields_ref, ends_ref, x_first_ref, x_second_ref, y_first_ref, y_second_ref):
+def pack_y_kernel(place_ref, fields_ref, ends_ref, x_first_ref, x_second_ref, *rest):
+    y_first_ref, y_second_ref = rest[-2:]
     even_x, even_y = place_ref[4] == 0, place_ref[5] == 0
 
     def put(f, plane, value):
@@ -629,28 +629,28 @@
             put(f, 34 + n, ends_ref[f, n])
 
 
-def exchange(place, fields, z_first, z_second, before=()):
+def exchange(place, fields, z_first, z_second, before_x=(), before_y=()):
     count = fields.shape[0]
     z_first, z_second = trade(z_first, z_second, "gz")
     x_first, x_second, ends = pl.pallas_call(
         pack_x_kernel,
-        in_specs=[SMEM] + [VMEM] * 3 + [HBM] * len(before),
+        in_specs=[SMEM] + [VMEM] * 3 + [HBM] * len(before_x),
         out_specs=[VMEM] * 3,
         out_shape=[shape(count, 9, 16, 128), shape(count, 9, 16, 128), shape(count, 2, 16, 128)],
         compiler_params=params(8),
         cost_estimate=LONG,
         name="pack_x",
-    )(place, fields, z_first, z_second, *in_hbm(*before))
+    )(place, fields, z_first, z_second, *in_hbm(*before_x))
     x_first, x_second = trade(x_first, x_second, "gx")
     y_first, y_second = pl.pallas_call(
         pack_y_kernel,
-        in_specs=[SMEM] + [VMEM] * 4,
+        in_specs=[SMEM] + [VMEM] * 4 + [HBM] * len(before_y),
         out_specs=[VMEM] * 2,
         out_shape=[shape(count, 36, 8, 128)] * 2,
         compiler_params=params(8),
         cost_estimate=LONG,
         name="pack_y",
-    )(place, fields, ends, x_first, x_second)
+    )(place, fields, ends, x_first, x_second, *in_hbm(*before_y))
     y_first, y_second = trade(y_first, y_second, "gy")
     return fields, ends, x_first, x_second, y_first, y_second
 
@@ -724,7 +724,6 @@
         name="prepare",
     )(place, slot_count, *in_hbm(*given))
     column = lax.all_to_all(column, "gz", 0, 0, tiled=True)
-    pieces = exchange(place, fields, z_first, z_second, (column,))
     sums = pl.pallas_call(
         column_kernel,
         in_specs=[VMEM],
@@ -733,6 +732,7 @@
         compiler_params=params(4),
         name="column",
     )(column)
+    pieces = exchange(place, fields, z_first, z_second, (column,), (sums,))
     sums = lax.all_to_all(sums, ("gx", "gy"), 0, 0, tiled=True)
     wide = shape(8, ROWS, 128)
     devices = size_x * size_y * size_z

time: 136 us -> 136 us (level)
  waiting for transfers between devices: 37.3 us -> 38.7 us
    ppermute x6, waiting for transfers between devices: 8.74 us -> 11.6 us  [trade(): lax.ppermute(first, axis, pairs)]
    ppermute x6, waiting for transfers between devices: 13.8 us -> 11.2 us  [trade(): lax.ppermute(second, axis, others)]
    unnamed x20 -> x18, local copies, waits for them, and re-layouts: 4.18 us -> 3.86 us
  transfers between devices with their start and end apart: 16 -> 16, of which waited for: 9 -> 10; matrix products, arithmetic and copies ran while one was open for 0% -> 0% of each run, Pallas kernels for 3% -> 1%
where the time goes in v3:
time: 136 us; the launch traced here: 135 us
  starting transfers between devices  52.8 us (39%)
  waiting for transfers between devices  38.7 us (28%)
  Pallas kernels  36.6 us (27%)
  local copies, waits for them, and re-layouts  3.94 us (3%)
  between operations  2.15 us (2%)
    pallas_call x1, Pallas kernels, on_device(): pl.pallas_call(second_kernel, in_specs=[SMEM] * 2 + [VMEM] * 10 + [HBM] *...  14.3 us
    pallas_call x1, Pallas kernels, on_device(): pl.pallas_call(first_kernel, in_specs=[SMEM] * 2 + [VMEM] * 7, out_specs=...  13.6 us
    ppermute x6, waiting for transfers between devices, trade(): lax.ppermute(first, axis, pairs)  11.6 us
    all_to_all x1, starting transfers between devices, on_device(): part = lax.all_to_all(part, ('gx', 'gy', 'gz'), 0, 0, tiled=True)  11.4 us
    ppermute x6, waiting for transfers between devices, trade(): lax.ppermute(second, axis, others)  11.2 us
    ppermute x6, starting transfers between devices, trade(): lax.ppermute(second, axis, others)  10.1 us
    all_to_all x1, starting transfers between devices, on_device(): column = lax.all_to_all(column, 'gz', 0, 0, tiled=True)  8.48 us
    all_to_all x1, starting transfers between devices, on_device(): lax.all_to_all(flux, 'gz', 0, 0, tiled=True)  8.45 us
  transfers between devices with their start and end apart: 16, of which 10 were waited for; matrix products, arithmetic and copies ran while one was open for 0% of the time, Pallas kernels for 1%

profile of v3, /device:TPU:12, one launch (start us, length us, event | category | flops | bytes accessed | tf_op | source)
XLA Modules:
  0.0 134.9 jit_solution(5805184511935216107)
XLA Ops:
  1.3 0.1 stack.23.place_ref
  1.4 4.6 %prepare.1 = (f32[4,16,16,128]{3,2,1,0:T(8,128)S(1)}, f32[4,16,128]{2,1,0:T(8,128)S(1)}, f32[4,16,128]{2,1,0:T(8,128)S(1)}, f32[8,16,128]{2,1,0:T(8,128)}, s32[16,128]{1,0:T(8,128)S(1)}) custom-call(s32[7]{0:T(128)S(1)} %stack.23.place_ref, s32[1,1,1]{2,1,0:T(1,128)S(6)} %copy.18.count_ref, s32[16,128]{1,0:T(8,128)} %bitcast.21, s32[16,128]{1,0:T(8,128)} %bitcast.25, ...), custom_call_target="tpu_custom_call" | custom-call | tf_op jit(solution)/shard_map/prepare/pallas_call | solution.py:703
  6.0 8.5 %all-to-all-start = ((f32[8,16,128]{2,1,0:T(8,128)}), f32[8,16,128]{2,1,0:T(8,128)S(1)}, u32[]{:S(2)}, u32[]{:S(2)}) async-start(f32[8,16,128]{2,1,0:T(8,128)} %get-tuple-element.35), calls=%async_computation | async-start | bytes 131072 | tf_op jit(solution)/shard_map/all_to_all | solution.py:726
  14.4 2.0 %collective-permute-start = (f32[4,16,128]{2,1,0:T(8,128)S(1)}, f32[4,16,128]{2,1,0:T(8,128)S(1)}, u32[]{:S(2)}, u32[]{:S(2)}) collective-permute-start(f32[4,16,128]{2,1,0:T(8,128)S(1)} %get-tuple-element.33), channel_id=1, source_target_pairs={{0,1},{1,0},{2,3},{3,2},{4,5},{5,4},{6,7},{7,6},{8,9},{9,8},{10,11... | collective-permute-start | bytes 98312 | tf_op jit(solution)/shard_map/ppermute | solution.py:588
  16.5 0.7 collective-permute-start.1
  17.1 2.0 %collective-permute-done.z_first_ref = f32[4,16,128]{2,1,0:T(8,128)S(1)} collective-permute-done((f32[4,16,128]{2,1,0:T(8,128)S(1)}, f32[4,16,128]{2,1,0:T(8,128)S(1)}, u32[]{:S(2)}, u32[]{:S(2)}) %collective-permute-start) | collective-permute-done | bytes 32800 | tf_op jit(solution)/shard_map/ppermute | solution.py:588
  19.1 0.0 collective-permute-done.1.z_second_ref
  19.1 3.7 %all-to-all-done.rest_0_.column_ref = f32[8,16,128]{2,1,0:T(8,128)S(1)} async-done(((f32[8,16,128]{2,1,0:T(8,128)}), f32[8,16,128]{2,1,0:T(8,128)S(1)}, u32[]{:S(2)}, u32[]{:S(2)}) %all-to-all-start) | async-done | bytes 65568 | tf_op jit(solution)/shard_map/all_to_all | solution.py:726
  22.8 0.0 copy-start.2
  22.8 0.6 copy-done.2
  23.5 0.6 pack_x.2
  24.1 1.3 collective-permute-start.2
  25.4 1.9 %collective-permute-start.3 = (f32[4,9,16,128]{3,2,1,0:T(8,128)S(1)}, f32[4,9,16,128]{3,2,1,0:T(8,128)S(1)}, u32[]{:S(2)}, u32[]{:S(2)}) collective-permute-start(f32[4,9,16,128]{3,2,1,0:T(8,128)S(1)} %get-tuple-element.38), channel_id=1, source_target_pairs={{64,128},{128,64},{65,129},{129,65},{66,130},{130,66},{67,131},{13... | collective-permute-start | bytes 884744 | tf_op jit(solution)/shard_map/ppermute | solution.py:588
  27.3 0.0 copy-start.3
  27.3 0.8 copy-done.3
  28.2 0.0 copy-start
  28.2 0.7 copy-done
  28.9 2.6 %collective-permute-done.2.x_first_ref = f32[4,9,16,128]{3,2,1,0:T(8,128)S(1)} collective-permute-done((f32[4,9,16,128]{3,2,1,0:T(8,128)S(1)}, f32[4,9,16,128]{3,2,1,0:T(8,128)S(1)}, u32[]{:S(2)}, u32[]{:S(2)}) %collective-permute-start.2) | collective-permute-done | bytes 294944 | tf_op jit(solution)/shard_map/ppermute | solution.py:588
  31.5 2.8 %collective-permute-done.3.x_second_ref = f32[4,9,16,128]{3,2,1,0:T(8,128)S(1)} collective-permute-done((f32[4,9,16,128]{3,2,1,0:T(8,128)S(1)}, f32[4,9,16,128]{3,2,1,0:T(8,128)S(1)}, u32[]{:S(2)}, u32[]{:S(2)}) %collective-permute-start.3) | collective-permute-done | bytes 294944 | tf_op jit(solution)/shard_map/ppermute | solution.py:588
  34.3 1.7 %pack_y.2 = (f32[4,36,8,128]{3,2,1,0:T(8,128)}, f32[4,36,8,128]{3,2,1,0:T(8,128)}) custom-call(s32[7]{0:T(128)S(1)} %stack.23.place_ref, f32[4,16,16,128]{3,2,1,0:T(8,128)S(1)} %get-tuple-element.32.fields_ref.centre_ref, f32[4,2,16,128]{3,2,1,0:T(8,128)S(1)} %get-tuple-element.36.ends_ref, f32[4,9,16,128]{3,2,1,0:T(8,128)S(1)} %collective-permute-done.2.x_first_ref, ...), custom_call_target="tpu_custom_call" | custom-call | bytes 167772160 | tf_op jit(solution)/shard_map/pack_y/pallas_call | solution.py:645
  36.0 0.0 collective-permute-start.4
  36.0 2.5 %collective-permute-start.5 = (f32[4,36,8,128]{3,2,1,0:T(8,128)}, f32[4,36,8,128]{3,2,1,0:T(8,128)S(1)}, u32[]{:S(2)}, u32[]{:S(2)}) collective-permute-start(f32[4,36,8,128]{3,2,1,0:T(8,128)} %get-tuple-element.40), channel_id=1, source_target_pairs={{8,16},{24,32},{40,48},{16,8},{32,24},{48,40},{9,17},{25,33},{41,4... | collective-permute-start | bytes 1769480 | tf_op jit(solution)/shard_map/ppermute | solution.py:588
  38.4 7.9 %all-to-all-start.1 = ((f32[32,16,128]{2,1,0:T(8,128)}), f32[32,16,128]{2,1,0:T(8,128)S(1)}, u32[]{:S(2)}, u32[]{:S(2)}) async-start(f32[32,16,128]{2,1,0:T(8,128)} %copy-done), calls=%async_computation.1 | async-start | bytes 524288 | tf_op jit(solution)/shard_map/all_to_all | solution.py:736
  46.4 0.0 copy-start.7
  47.1 5.2 %all-to-all-done.1.sums_ref = f32[32,16,128]{2,1,0:T(8,128)S(1)} async-done(((f32[32,16,128]{2,1,0:T(8,128)}), f32[32,16,128]{2,1,0:T(8,128)S(1)}, u32[]{:S(2)}, u32[]{:S(2)}) %all-to-all-start.1) | async-done | bytes 262176 | tf_op jit(solution)/shard_map/all_to_all | solution.py:736
  52.3 0.0 collective-permute-done.4.y_first_ref
  52.3 0.0 collective-permute-done.5.y_second_ref
  52.3 13.6 %first_sweep.1 = (f32[8,160,128]{2,1,0:T(8,128)}, f32[8,160,128]{2,1,0:T(8,128)}, f32[8,160,128]{2,1,0:T(8,128)}, f32[8,160,128]{2,1,0:T(8,128)}, f32[2,16,16,12...) custom-call(s32[7]{0:T(128)S(1)} %stack.23.place_ref, ...), custom_call_target="tpu_custom_call" | custom-call | tf_op jit(solution)/shard_map/first_sweep/pallas_call | solution.py:739
  65.9 11.4 %all-to-all-start.2 = ((f32[256,2,128]{2,1,0:T(2,128)}), f32[256,2,128]{2,1,0:T(2,128)S(1)}, u32[]{:S(2)}, u32[]{:S(2)}) async-start(f32[256,2,128]{2,1,0:T(2,128)} %get-tuple-element.49), calls=%async_computation.2 | async-start | bytes 524288 | tf_op jit(solution)/shard_map/all_to_all | solution.py:760
  77.4 1.8 %collective-permute-start.6 = (f32[2,16,128]{2,1,0:T(8,128)S(1)}, f32[2,16,128]{2,1,0:T(8,128)S(1)}, u32[]{:S(2)}, u32[]{:S(2)}) collective-permute-start(f32[2,16,128]{2,1,0:T(8,128)S(1)} %get-tuple-element.42), channel_id=1, source_target_pairs={{0,1},{1,0},{2,3},{3,2},{4,5},{5,4},{6,7},{7,6},{8,9},{9,8},{10,11... | collective-permute-start | bytes 49160 | tf_op jit(solution)/shard_map/ppermute | solution.py:588
  79.1 0.7 collective-permute-start.7
  79.8 4.6 %collective-permute-done.6.z_first_ref = f32[2,16,128]{2,1,0:T(8,128)S(1)} collective-permute-done((f32[2,16,128]{2,1,0:T(8,128)S(1)}, f32[2,16,128]{2,1,0:T(8,128)S(1)}, u32[]{:S(2)}, u32[]{:S(2)}) %collective-permute-start.6) | collective-permute-done | bytes 16416 | tf_op jit(solution)/shard_map/ppermute | solution.py:588
  84.4 0.0 collective-permute-done.7.z_second_ref
  84.4 0.6 pack_x.3
  85.0 1.3 collective-permute-start.8
  86.2 1.9 %collective-permute-start.9 = (f32[2,9,16,128]{3,2,1,0:T(8,128)S(1)}, f32[2,9,16,128]{3,2,1,0:T(8,128)S(1)}, u32[]{:S(2)}, u32[]{:S(2)}) collective-permute-start(f32[2,9,16,128]{3,2,1,0:T(8,128)S(1)} %get-tuple-element.46), channel_id=1, source_target_pairs={{64,128},{128,64},{65,129},{129,65},{66,130},{130,66},{67,131},{13... | collective-permute-start | bytes 442376 | tf_op jit(solution)/shard_map/ppermute | solution.py:588
  88.2 2.4 %collective-permute-done.8.x_first_ref = f32[2,9,16,128]{3,2,1,0:T(8,128)S(1)} collective-permute-done((f32[2,9,16,128]{3,2,1,0:T(8,128)S(1)}, f32[2,9,16,128]{3,2,1,0:T(8,128)S(1)}, u32[]{:S(2)}, u32[]{:S(2)}) %collective-permute-start.8) | collective-permute-done | bytes 147488 | tf_op jit(solution)/shard_map/ppermute | solution.py:588
  90.6 2.7 %collective-permute-done.9.x_second_ref = f32[2,9,16,128]{3,2,1,0:T(8,128)S(1)} collective-permute-done((f32[2,9,16,128]{3,2,1,0:T(8,128)S(1)}, f32[2,9,16,128]{3,2,1,0:T(8,128)S(1)}, u32[]{:S(2)}, u32[]{:S(2)}) %collective-permute-start.9) | collective-permute-done | bytes 147488 | tf_op jit(solution)/shard_map/ppermute | solution.py:588
  93.3 0.0 copy-start.6
  93.3 0.0 copy-start.8
  93.3 0.6 pack_y.3
  93.9 0.0 copy-start.1
  93.9 0.1 collective-permute-start.10
  94.0 2.5 %collective-permute-start.11 = (f32[2,36,8,128]{3,2,1,0:T(8,128)S(1)}, f32[2,36,8,128]{3,2,1,0:T(8,128)S(1)}, u32[]{:S(2)}, u32[]{:S(2)}) collective-permute-start(f32[2,36,8,128]{3,2,1,0:T(8,128)S(1)} %get-tuple-element.48), channel_id=1, source_target_pairs={{8,16},{24,32},{40,48},{16,8},{32,24},{48,40},{9,17},{25,33},{41,4... | collective-permute-start | bytes 884744 | tf_op jit(solution)/shard_map/ppermute | solution.py:588
  96.5 0.0 collective-permute-done.10.y_first_ref
  96.5 5.7 %collective-permute-done.11.y_second_ref = f32[2,36,8,128]{3,2,1,0:T(8,128)S(1)} collective-permute-done((f32[2,36,8,128]{3,2,1,0:T(8,128)S(1)}, f32[2,36,8,128]{3,2,1,0:T(8,128)S(1)}, u32[]{:S(2)}, u32[]{:S(2)}) %collective-permute-start.11) | collective-permute-done | bytes 294944 | tf_op jit(solution)/shard_map/ppermute | solution.py:588
  102.1 0.0 copy-start.4
  102.1 0.7 copy-done.4
  102.9 0.0 all-to-all-done.2.part_ref
  102.9 0.0 copy-done.7
  102.9 0.0 copy-start.5
  102.9 1.0 copy-done.5
  103.8 14.3 %second_sweep.1 = (f32[16,16,128]{2,1,0:T(8,128)}, f32[16,16,128]{2,1,0:T(8,128)}, f32[8,128]{1,0:T(8,128)}) custom-call(s32[7]{0:T(128)S(1)} %stack.23.place_ref, f32[1]{0:T(128)S(6)} %copy.17.current_ref, f32[2,16,16,128]{3,2,1,0:T(8,128)S(1)} %get-tuple-element.41.fields_ref.centre_ref, f32[2,2,16,128]{3,2,1,0:T(8,128)S(1)} %get-tuple-element.44.ends_ref, ...), custom_call_target="tpu_custom_call" | custom-call | tf_op jit(solution)/shard_map/second_sweep/pallas_call | solution.py:761
  118.1 8.5 %all-to-all-start.3 = ((f32[8,1,128]{2,1,0:T(1,128)}), f32[8,1,128]{2,1,0:T(1,128)S(1)}, u32[]{:S(2)}, u32[]{:S(2)}) async-start(f32[8,1,128]{2,1,0:T(1,128)} %bitcast.14), calls=%async_computation.3 | async-start | bytes 8192 | tf_op jit(solution)/shard_map/all_to_all | solution.py:788
  126.6 0.0 copy-done.6
  126.6 0.0 copy-done.8
  126.6 0.0 copy-done.1
  126.6 0.6 shells.1
  127.2 7.0 %all-to-all-done.3 = f32[8,1,128]{2,1,0:T(1,128)S(1)} async-done(((f32[8,1,128]{2,1,0:T(1,128)}), f32[8,1,128]{2,1,0:T(1,128)S(1)}, u32[]{:S(2)}, u32[]{:S(2)}) %all-to-all-start.3) | async-done | bytes 4128 | tf_op jit(solution)/shard_map/all_to_all | solution.py:788
  134.2 0.6 add_bitcast_fusion
  (3 shorter events, 0.1 us)
Async XLA Ops:
  6.0 16.9 %all-to-all-start = ((f32[8,16,128]{2,1,0:T(8,128)}), f32[8,16,128]{2,1,0:T(8,128)S(1)}, u32[]{:S(2)}, u32[]{:S(2)}) async-start(f32[8,16,128]{2,1,0:T(8,128)} %get-tuple-element.35), calls=%async_computation | async-start | bytes 131072 | tf_op jit(solution)/shard_map/all_to_all | solution.py:726
  14.4 4.6 %collective-permute-start = (f32[4,16,128]{2,1,0:T(8,128)S(1)}, f32[4,16,128]{2,1,0:T(8,128)S(1)}, u32[]{:S(2)}, u32[]{:S(2)}) collective-permute-start(f32[4,16,128]{2,1,0:T(8,128)S(1)} %get-tuple-element.33), channel_id=1, source_target_pairs={{0,1},{1,0},{2,3},{3,2},{4,5},{5,4},{6,7},{7,6},{8,9},{9,8},{10,11... | collective-permute-start | bytes 98312 | tf_op jit(solution)/shard_map/ppermute | solution.py:588
  16.5 2.6 %collective-permute-start.1 = (f32[4,16,128]{2,1,0:T(8,128)S(1)}, f32[4,16,128]{2,1,0:T(8,128)S(1)}, u32[]{:S(2)}, u32[]{:S(2)}) collective-permute-start(f32[4,16,128]{2,1,0:T(8,128)S(1)} %get-tuple-element.34), channel_id=1, source_target_pairs={{1,2},{3,4},{5,6},{2,1},{4,3},{6,5},{9,10},{11,12},{13,14},{10,9},... | collective-permute-start | bytes 98312 | tf_op jit(solution)/shard_map/ppermute | solution.py:588
  22.8 0.6 copy-start.2
  24.1 7.4 %collective-permute-start.2 = (f32[4,9,16,128]{3,2,1,0:T(8,128)S(1)}, f32[4,9,16,128]{3,2,1,0:T(8,128)S(1)}, u32[]{:S(2)}, u32[]{:S(2)}) collective-permute-start(f32[4,9,16,128]{3,2,1,0:T(8,128)S(1)} %get-tuple-element.37), channel_id=1, source_target_pairs={{0,64},{64,0},{128,192},{192,128},{1,65},{65,1},{129,193},{193,129... | collective-permute-start | bytes 884744 | tf_op jit(solution)/shard_map/ppermute | solution.py:588
  25.4 8.9 %collective-permute-start.3 = (f32[4,9,16,128]{3,2,1,0:T(8,128)S(1)}, f32[4,9,16,128]{3,2,1,0:T(8,128)S(1)}, u32[]{:S(2)}, u32[]{:S(2)}) collective-permute-start(f32[4,9,16,128]{3,2,1,0:T(8,128)S(1)} %get-tuple-element.38), channel_id=1, source_target_pairs={{64,128},{128,64},{65,129},{129,65},{66,130},{130,66},{67,131},{13... | collective-permute-start | bytes 884744 | tf_op jit(solution)/shard_map/ppermute | solution.py:588
  27.3 0.8 copy-start.3
  28.2 0.7 copy-start
  36.0 16.3 %collective-permute-start.4 = (f32[4,36,8,128]{3,2,1,0:T(8,128)}, f32[4,36,8,128]{3,2,1,0:T(8,128)S(1)}, u32[]{:S(2)}, u32[]{:S(2)}) collective-permute-start(f32[4,36,8,128]{3,2,1,0:T(8,128)} %get-tuple-element.39), channel_id=1, source_target_pairs={{0,8},{8,0},{16,24},{24,16},{32,40},{40,32},{48,56},{56,48},{1,9},... | collective-permute-start | bytes 1769480 | tf_op jit(solution)/shard_map/ppermute | solution.py:588
  36.0 16.3 %collective-permute-start.5 = (f32[4,36,8,128]{3,2,1,0:T(8,128)}, f32[4,36,8,128]{3,2,1,0:T(8,128)S(1)}, u32[]{:S(2)}, u32[]{:S(2)}) collective-permute-start(f32[4,36,8,128]{3,2,1,0:T(8,128)} %get-tuple-element.40), channel_id=1, source_target_pairs={{8,16},{24,32},{40,48},{16,8},{32,24},{48,40},{9,17},{25,33},{41,4... | collective-permute-start | bytes 1769480 | tf_op jit(solution)/shard_map/ppermute | solution.py:588
  38.4 13.8 %all-to-all-start.1 = ((f32[32,16,128]{2,1,0:T(8,128)}), f32[32,16,128]{2,1,0:T(8,128)S(1)}, u32[]{:S(2)}, u32[]{:S(2)}) async-start(f32[32,16,128]{2,1,0:T(8,128)} %copy-done), calls=%async_computation.1 | async-start | bytes 524288 | tf_op jit(solution)/shard_map/all_to_all | solution.py:736
  46.4 56.5 %copy-start.7 = (s32[1,1,2048]{2,1,0:T(1,128)S(1)}, s32[1,1,2048]{2,1,0:T(1,128)}, u32[]{:S(2)}) copy-start(s32[1,1,2048]{2,1,0:T(1,128)} %param.18) | copy-start | bytes 24580
  65.9 37.0 %all-to-all-start.2 = ((f32[256,2,128]{2,1,0:T(2,128)}), f32[256,2,128]{2,1,0:T(2,128)S(1)}, u32[]{:S(2)}, u32[]{:S(2)}) async-start(f32[256,2,128]{2,1,0:T(2,128)} %get-tuple-element.49), calls=%async_computation.2 | async-start | bytes 524288 | tf_op jit(solution)/shard_map/all_to_all | solution.py:760
  77.4 7.0 %collective-permute-start.6 = (f32[2,16,128]{2,1,0:T(8,128)S(1)}, f32[2,16,128]{2,1,0:T(8,128)S(1)}, u32[]{:S(2)}, u32[]{:S(2)}) collective-permute-start(f32[2,16,128]{2,1,0:T(8,128)S(1)} %get-tuple-element.42), channel_id=1, source_target_pairs={{0,1},{1,0},{2,3},{3,2},{4,5},{5,4},{6,7},{7,6},{8,9},{9,8},{10,11... | collective-permute-start | bytes 49160 | tf_op jit(solution)/shard_map/ppermute | solution.py:588
  79.1 5.2 %collective-permute-start.7 = (f32[2,16,128]{2,1,0:T(8,128)S(1)}, f32[2,16,128]{2,1,0:T(8,128)S(1)}, u32[]{:S(2)}, u32[]{:S(2)}) collective-permute-start(f32[2,16,128]{2,1,0:T(8,128)S(1)} %get-tuple-element.43), channel_id=1, source_target_pairs={{1,2},{3,4},{5,6},{2,1},{4,3},{6,5},{9,10},{11,12},{13,14},{10,9},... | collective-permute-start | bytes 49160 | tf_op jit(solution)/shard_map/ppermute | solution.py:588
  85.0 5.6 %collective-permute-start.8 = (f32[2,9,16,128]{3,2,1,0:T(8,128)S(1)}, f32[2,9,16,128]{3,2,1,0:T(8,128)S(1)}, u32[]{:S(2)}, u32[]{:S(2)}) collective-permute-start(f32[2,9,16,128]{3,2,1,0:T(8,128)S(1)} %get-tuple-element.45), channel_id=1, source_target_pairs={{0,64},{64,0},{128,192},{192,128},{1,65},{65,1},{129,193},{193,129... | collective-permute-start | bytes 442376 | tf_op jit(solution)/shard_map/ppermute | solution.py:588
  86.2 7.0 %collective-permute-start.9 = (f32[2,9,16,128]{3,2,1,0:T(8,128)S(1)}, f32[2,9,16,128]{3,2,1,0:T(8,128)S(1)}, u32[]{:S(2)}, u32[]{:S(2)}) collective-permute-start(f32[2,9,16,128]{3,2,1,0:T(8,128)S(1)} %get-tuple-element.46), channel_id=1, source_target_pairs={{64,128},{128,64},{65,129},{129,65},{66,130},{130,66},{67,131},{13... | collective-permute-start | bytes 442376 | tf_op jit(solution)/shard_map/ppermute | solution.py:588
  93.3 33.3 %copy-start.6 = (f32[1,1,64,128]{3,2,1,0:T(8,128)S(1)}, f32[1,1,64,128]{3,2,1,0:T(8,128)}, u32[]{:S(2)}) copy-start(f32[1,1,64,128]{3,2,1,0:T(8,128)} %param.24) | copy-start | bytes 98308
  93.3 33.3 %copy-start.8 = (s32[1,1,128]{2,1,0:T(1,128)S(1)}, s32[1,1,128]{2,1,0:T(1,128)}, u32[]{:S(2)}) copy-start(s32[1,1,128]{2,1,0:T(1,128)} %param.23) | copy-start | bytes 1540
  93.9 32.8 %copy-start.1 = (f32[1,1,64,64,128]{4,3,2,1,0:T(8,128)S(1)}, f32[1,1,64,64,128]{4,3,2,1,0:T(8,128)}, u32[]{:S(2)}) copy-start(f32[1,1,64,64,128]{4,3,2,1,0:T(8,128)} %param.25) | copy-start | bytes 6291460
  93.9 2.6 %collective-permute-start.10 = (f32[2,36,8,128]{3,2,1,0:T(8,128)S(1)}, f32[2,36,8,128]{3,2,1,0:T(8,128)S(1)}, u32[]{:S(2)}, u32[]{:S(2)}) collective-permute-start(f32[2,36,8,128]{3,2,1,0:T(8,128)S(1)} %get-tuple-element.47), channel_id=1, source_target_pairs={{0,8},{8,0},{16,24},{24,16},{32,40},{40,32},{48,56},{56,48},{1,9},... | collective-permute-start | bytes 884744 | tf_op jit(solution)/shard_map/ppermute | solution.py:588
  94.0 8.2 %collective-permute-start.11 = (f32[2,36,8,128]{3,2,1,0:T(8,128)S(1)}, f32[2,36,8,128]{3,2,1,0:T(8,128)S(1)}, u32[]{:S(2)}, u32[]{:S(2)}) collective-permute-start(f32[2,36,8,128]{3,2,1,0:T(8,128)S(1)} %get-tuple-element.48), channel_id=1, source_target_pairs={{8,16},{24,32},{40,48},{16,8},{32,24},{48,40},{9,17},{25,33},{41,4... | collective-permute-start | bytes 884744 | tf_op jit(solution)/shard_map/ppermute | solution.py:588
  102.1 0.7 copy-start.4
  102.9 1.0 copy-start.5
  118.1 16.1 %all-to-all-start.3 = ((f32[8,1,128]{2,1,0:T(1,128)}), f32[8,1,128]{2,1,0:T(1,128)S(1)}, u32[]{:S(2)}, u32[]{:S(2)}) async-start(f32[8,1,128]{2,1,0:T(1,128)} %bitcast.14), calls=%async_computation.3 | async-start | bytes 8192 | tf_op jit(solution)/shard_map/all_to_all | solution.py:788

commit v4 on v3

--- a/solution.py
+++ b/solution.py
@@ -18,16 +18,16 @@
 ROWS = 160
 FIRST = 16
 TILES = 18
-UNROLL = 18
 PART_ROWS = 2
 SUM_ROWS = 16
-SETUP = 6
-LAST = 4
+SETUP = 18
+LAST = 16
 f32 = jnp.float32
 bf16 = jnp.bfloat16
 VMEM = pl.BlockSpec(memory_space=pltpu.VMEM)
 SMEM = pl.BlockSpec(memory_space=pltpu.SMEM)
 HBM = pl.BlockSpec(memory_space=pltpu.HBM)
+ANY = pl.BlockSpec(memory_space=pl.ANY)
 
 
 LONG = pl.CostEstimate(flops=0, bytes_accessed=160 * 1024 * 1024, transcendentals=0)
@@ -39,6 +39,10 @@
 
 def in_hbm(*arrays):
     return [pltpu.with_memory_space_constraint(array, pltpu.HBM) for array in arrays]
+
+
+def in_vmem(*arrays):
+    return [pltpu.with_memory_space_constraint(array, pltpu.VMEM) for array in arrays]
 
 
 def copies(sources, targets, sems):
@@ -351,7 +355,7 @@
 
     tiles(set_system, unroll=SETUP)
 
-    def iteration(c_now, p_now, c_then, p_then):
+    def iteration(c_now, p_now, c_then, p_then, first=0, last=TILES):
         def relax(r):
             rows = pl.ds(r, 8)
             c = [c_now[n, rows] for n in range(8)]
@@ -364,7 +368,7 @@
                 c_then[n, rows] = (rc[n, rows] + next_c + coup[n, rows] * p[n]) * gc[n, rows]
                 p_then[n, rows] = (rp[n, rows] + next_p) * gp[n, rows]
 
-        tiles(relax, unroll=UNROLL)
+        tiles(relax, first, last, unroll=last - first)
 
     def pair(_, carry):
         iteration(dc, dp, dc_next, dp_next)
@@ -373,7 +377,7 @@
 
     lax.fori_loop(0, (ITERS - 1) // 2, pair, 0)
     if ITERS % 2 == 0:
-        iteration(dc, dp, dc_next, dp_next)
+        iteration(dc, dp, dc_next, dp_next, 1, TILES - 1)
         return dc_next, dp_next
     return dc, dp
 
@@ -634,23 +638,23 @@
     z_first, z_second = trade(z_first, z_second, "gz")
     x_first, x_second, ends = pl.pallas_call(
         pack_x_kernel,
-        in_specs=[SMEM] + [VMEM] * 3 + [HBM] * len(before_x),
+        in_specs=[SMEM] + [VMEM] * 3 + [ANY] * len(before_x),
         out_specs=[VMEM] * 3,
         out_shape=[shape(count, 9, 16, 128), shape(count, 9, 16, 128), shape(count, 2, 16, 128)],
         compiler_params=params(8),
         cost_estimate=LONG,
         name="pack_x",
-    )(place, fields, z_first, z_second, *in_hbm(*before_x))
+    )(place, fields, z_first, z_second, *before_x)
     x_first, x_second = trade(x_first, x_second, "gx")
     y_first, y_second = pl.pallas_call(
         pack_y_kernel,
-        in_specs=[SMEM] + [VMEM] * 4 + [HBM] * len(before_y),
+        in_specs=[SMEM] + [VMEM] * 4 + [ANY] * len(before_y),
         out_specs=[VMEM] * 2,
         out_shape=[shape(count, 36, 8, 128)] * 2,
         compiler_params=params(8),
         cost_estimate=LONG,
         name="pack_y",
-    )(place, fields, ends, x_first, x_second, *in_hbm(*before_y))
+    )(place, fields, ends, x_first, x_second, *before_y)
     y_first, y_second = trade(y_first, y_second, "gy")
     return fields, ends, x_first, x_second, y_first, y_second
 
@@ -771,7 +775,7 @@
         + work_scratch(),
         compiler_params=params(),
         name="second_sweep",
-    )(place, applied_current, *pieces, part, state, cell, position, *in_hbm(start, k, w, circuit))
+    )(place, applied_current, *in_vmem(*pieces), part, state, cell, position, *in_hbm(start, k, w, circuit))
     base, surface_column = pl.pallas_call(
         shell_kernel,
         grid=(8,),

time: 136 us -> 133 us (0.978)
  local copies, waits for them, and re-layouts: 3.94 us -> 1.79 us
    unnamed x18 -> x12, local copies, waits for them, and re-layouts: 3.86 us -> 1.7 us
  transfers between devices with their start and end apart: 16 -> 16, of which waited for: 10 -> 10; matrix products, arithmetic and copies ran while one was open for 0% -> 0% of each run, Pallas kernels for 1% -> 2%
where the time goes in v4:
time: 133 us
  starting transfers between devices  52.8 us (40%)
  waiting for transfers between devices  39.5 us (30%)
  Pallas kernels  35.9 us (27%)
  between operations  2.13 us (2%)
  local copies, waits for them, and re-layouts  1.79 us (1%)
    pallas_call x1, Pallas kernels, on_device(): pl.pallas_call(second_kernel, in_specs=[SMEM] * 2 + [VMEM] * 10 + [HBM] *...  13.7 us
    pallas_call x1, Pallas kernels, on_device(): pl.pallas_call(first_kernel, in_specs=[SMEM] * 2 + [VMEM] * 7, out_specs=...  12.8 us
    ppermute x6, waiting for transfers between devices, trade(): lax.ppermute(first, axis, pairs)  12.3 us
    all_to_all x1, starting transfers between devices, on_device(): part = lax.all_to_all(part, ('gx', 'gy', 'gz'), 0, 0, tiled=True)  11.4 us
    ppermute x6, waiting for transfers between devices, trade(): lax.ppermute(second, axis, others)  11.2 us
    ppermute x6, starting transfers between devices, trade(): lax.ppermute(second, axis, others)  10.1 us
    all_to_all x1, starting transfers between devices, on_device(): column = lax.all_to_all(column, 'gz', 0, 0, tiled=True)  8.48 us
    all_to_all x1, starting transfers between devices, on_device(): lax.all_to_all(flux, 'gz', 0, 0, tiled=True)  8.47 us
  transfers between devices with their start and end apart: 16, of which 10 were waited for; matrix products, arithmetic and copies ran while one was open for 0% of the time, Pallas kernels for 2%

profile of v4, /device:TPU:12, one launch (start us, length us, event | category | flops | bytes accessed | tf_op | source)
XLA Modules:
  0.0 132.8 jit_solution(1059651224443539794)
XLA Ops:
  1.3 0.1 stack.23.place_ref
  1.4 4.6 %prepare.1 = (f32[4,16,16,128]{3,2,1,0:T(8,128)S(1)}, f32[4,16,128]{2,1,0:T(8,128)S(1)}, f32[4,16,128]{2,1,0:T(8,128)S(1)}, f32[8,16,128]{2,1,0:T(8,128)}, s32[16,128]{1,0:T(8,128)S(1)}) custom-call(s32[7]{0:T(128)S(1)} %stack.23.place_ref, s32[1,1,1]{2,1,0:T(1,128)S(6)} %copy.18.count_ref, s32[16,128]{1,0:T(8,128)} %bitcast.21, s32[16,128]{1,0:T(8,128)} %bitcast.25, ...), custom_call_target="tpu_custom_call" | custom-call | tf_op jit(solution)/shard_map/prepare/pallas_call | solution.py:707
  6.0 8.5 %all-to-all-start = ((f32[8,16,128]{2,1,0:T(8,128)}), f32[8,16,128]{2,1,0:T(8,128)S(1)}, u32[]{:S(2)}, u32[]{:S(2)}) async-start(f32[8,16,128]{2,1,0:T(8,128)} %get-tuple-element.35), calls=%async_computation | async-start | bytes 131072 | tf_op jit(solution)/shard_map/all_to_all | solution.py:730
  14.4 2.0 %collective-permute-start = (f32[4,16,128]{2,1,0:T(8,128)S(1)}, f32[4,16,128]{2,1,0:T(8,128)S(1)}, u32[]{:S(2)}, u32[]{:S(2)}) collective-permute-start(f32[4,16,128]{2,1,0:T(8,128)S(1)} %get-tuple-element.33), channel_id=1, source_target_pairs={{0,1},{1,0},{2,3},{3,2},{4,5},{5,4},{6,7},{7,6},{8,9},{9,8},{10,11... | collective-permute-start | bytes 98312 | tf_op jit(solution)/shard_map/ppermute | solution.py:592
  16.5 0.7 collective-permute-start.1
  17.1 2.0 %collective-permute-done.z_first_ref = f32[4,16,128]{2,1,0:T(8,128)S(1)} collective-permute-done((f32[4,16,128]{2,1,0:T(8,128)S(1)}, f32[4,16,128]{2,1,0:T(8,128)S(1)}, u32[]{:S(2)}, u32[]{:S(2)}) %collective-permute-start) | collective-permute-done | bytes 32800 | tf_op jit(solution)/shard_map/ppermute | solution.py:592
  19.1 0.0 collective-permute-done.1.z_second_ref
  19.1 3.7 %all-to-all-done.rest_0_.column_ref = f32[8,16,128]{2,1,0:T(8,128)S(1)} async-done(((f32[8,16,128]{2,1,0:T(8,128)}), f32[8,16,128]{2,1,0:T(8,128)S(1)}, u32[]{:S(2)}, u32[]{:S(2)}) %all-to-all-start) | async-done | bytes 65568 | tf_op jit(solution)/shard_map/all_to_all | solution.py:730
  22.8 0.6 pack_x.2
  23.5 1.3 collective-permute-start.2
  24.8 1.9 %collective-permute-start.3 = (f32[4,9,16,128]{3,2,1,0:T(8,128)S(1)}, f32[4,9,16,128]{3,2,1,0:T(8,128)S(1)}, u32[]{:S(2)}, u32[]{:S(2)}) collective-permute-start(f32[4,9,16,128]{3,2,1,0:T(8,128)S(1)} %get-tuple-element.38), channel_id=1, source_target_pairs={{64,128},{128,64},{65,129},{129,65},{66,130},{130,66},{67,131},{13... | collective-permute-start | bytes 884744 | tf_op jit(solution)/shard_map/ppermute | solution.py:592
  26.7 0.7 column.1.rest_0_
  27.4 3.5 %collective-permute-done.2.x_first_ref = f32[4,9,16,128]{3,2,1,0:T(8,128)S(1)} collective-permute-done((f32[4,9,16,128]{3,2,1,0:T(8,128)S(1)}, f32[4,9,16,128]{3,2,1,0:T(8,128)S(1)}, u32[]{:S(2)}, u32[]{:S(2)}) %collective-permute-start.2) | collective-permute-done | bytes 294944 | tf_op jit(solution)/shard_map/ppermute | solution.py:592
  30.9 2.8 %collective-permute-done.3.x_second_ref = f32[4,9,16,128]{3,2,1,0:T(8,128)S(1)} collective-permute-done((f32[4,9,16,128]{3,2,1,0:T(8,128)S(1)}, f32[4,9,16,128]{3,2,1,0:T(8,128)S(1)}, u32[]{:S(2)}, u32[]{:S(2)}) %collective-permute-start.3) | collective-permute-done | bytes 294944 | tf_op jit(solution)/shard_map/ppermute | solution.py:592
  33.7 1.6 %pack_y.2 = (f32[4,36,8,128]{3,2,1,0:T(8,128)}, f32[4,36,8,128]{3,2,1,0:T(8,128)}) custom-call(s32[7]{0:T(128)S(1)} %stack.23.place_ref, f32[4,16,16,128]{3,2,1,0:T(8,128)S(1)} %get-tuple-element.32.fields_ref.centre_ref, f32[4,2,16,128]{3,2,1,0:T(8,128)S(1)} %get-tuple-element.36.ends_ref, f32[4,9,16,128]{3,2,1,0:T(8,128)S(1)} %collective-permute-done.2.x_first_ref, ...), custom_call_target="tpu_custom_call" | custom-call | bytes 167772160 | tf_op jit(solution)/shard_map/pack_y/pallas_call | solution.py:649
  35.3 0.0 collective-permute-start.4
  35.3 2.5 %collective-permute-start.5 = (f32[4,36,8,128]{3,2,1,0:T(8,128)}, f32[4,36,8,128]{3,2,1,0:T(8,128)S(1)}, u32[]{:S(2)}, u32[]{:S(2)}) collective-permute-start(f32[4,36,8,128]{3,2,1,0:T(8,128)} %get-tuple-element.40), channel_id=1, source_target_pairs={{8,16},{24,32},{40,48},{16,8},{32,24},{48,40},{9,17},{25,33},{41,4... | collective-permute-start | bytes 1769480 | tf_op jit(solution)/shard_map/ppermute | solution.py:592
  37.8 7.9 %all-to-all-start.1 = ((f32[32,16,128]{2,1,0:T(8,128)}), f32[32,16,128]{2,1,0:T(8,128)S(1)}, u32[]{:S(2)}, u32[]{:S(2)}) async-start(f32[32,16,128]{2,1,0:T(8,128)} %column.1.rest_0_), calls=%async_computation.1 | async-start | bytes 524288 | tf_op jit(solution)/shard_map/all_to_all | solution.py:740
  45.7 0.0 copy-start.4
  46.4 5.2 %all-to-all-done.1.sums_ref = f32[32,16,128]{2,1,0:T(8,128)S(1)} async-done(((f32[32,16,128]{2,1,0:T(8,128)}), f32[32,16,128]{2,1,0:T(8,128)S(1)}, u32[]{:S(2)}, u32[]{:S(2)}) %all-to-all-start.1) | async-done | bytes 262176 | tf_op jit(solution)/shard_map/all_to_all | solution.py:740
  51.6 0.0 collective-permute-done.4.y_first_ref
  51.6 0.0 collective-permute-done.5.y_second_ref
  51.6 12.8 %first_sweep.1 = (f32[8,160,128]{2,1,0:T(8,128)}, f32[8,160,128]{2,1,0:T(8,128)}, f32[8,160,128]{2,1,0:T(8,128)}, f32[8,160,128]{2,1,0:T(8,128)}, f32[2,16,16,12...) custom-call(s32[7]{0:T(128)S(1)} %stack.23.place_ref, ...), custom_call_target="tpu_custom_call" | custom-call | tf_op jit(solution)/shard_map/first_sweep/pallas_call | solution.py:743
  64.4 11.4 %all-to-all-start.2 = ((f32[256,2,128]{2,1,0:T(2,128)}), f32[256,2,128]{2,1,0:T(2,128)S(1)}, u32[]{:S(2)}, u32[]{:S(2)}) async-start(f32[256,2,128]{2,1,0:T(2,128)} %get-tuple-element.49), calls=%async_computation.2 | async-start | bytes 524288 | tf_op jit(solution)/shard_map/all_to_all | solution.py:764
  75.9 1.8 %collective-permute-start.6 = (f32[2,16,128]{2,1,0:T(8,128)S(1)}, f32[2,16,128]{2,1,0:T(8,128)S(1)}, u32[]{:S(2)}, u32[]{:S(2)}) collective-permute-start(f32[2,16,128]{2,1,0:T(8,128)S(1)} %get-tuple-element.42), channel_id=1, source_target_pairs={{0,1},{1,0},{2,3},{3,2},{4,5},{5,4},{6,7},{7,6},{8,9},{9,8},{10,11... | collective-permute-start | bytes 49160 | tf_op jit(solution)/shard_map/ppermute | solution.py:592
  77.7 0.7 collective-permute-start.7
  78.3 4.6 %collective-permute-done.6.z_first_ref = f32[2,16,128]{2,1,0:T(8,128)S(1)} collective-permute-done((f32[2,16,128]{2,1,0:T(8,128)S(1)}, f32[2,16,128]{2,1,0:T(8,128)S(1)}, u32[]{:S(2)}, u32[]{:S(2)}) %collective-permute-start.6) | collective-permute-done | bytes 16416 | tf_op jit(solution)/shard_map/ppermute | solution.py:592
  82.9 0.0 collective-permute-done.7.z_second_ref
  82.9 0.6 pack_x.3
  83.5 1.3 collective-permute-start.8
  84.8 1.9 %collective-permute-start.9 = (f32[2,9,16,128]{3,2,1,0:T(8,128)S(1)}, f32[2,9,16,128]{3,2,1,0:T(8,128)S(1)}, u32[]{:S(2)}, u32[]{:S(2)}) collective-permute-start(f32[2,9,16,128]{3,2,1,0:T(8,128)S(1)} %get-tuple-element.46), channel_id=1, source_target_pairs={{64,128},{128,64},{65,129},{129,65},{66,130},{130,66},{67,131},{13... | collective-permute-start | bytes 442376 | tf_op jit(solution)/shard_map/ppermute | solution.py:592
  86.7 2.3 %collective-permute-done.8.x_first_ref = f32[2,9,16,128]{3,2,1,0:T(8,128)S(1)} collective-permute-done((f32[2,9,16,128]{3,2,1,0:T(8,128)S(1)}, f32[2,9,16,128]{3,2,1,0:T(8,128)S(1)}, u32[]{:S(2)}, u32[]{:S(2)}) %collective-permute-start.8) | collective-permute-done | bytes 147488 | tf_op jit(solution)/shard_map/ppermute | solution.py:592
  89.0 2.8 %collective-permute-done.9.x_second_ref = f32[2,9,16,128]{3,2,1,0:T(8,128)S(1)} collective-permute-done((f32[2,9,16,128]{3,2,1,0:T(8,128)S(1)}, f32[2,9,16,128]{3,2,1,0:T(8,128)S(1)}, u32[]{:S(2)}, u32[]{:S(2)}) %collective-permute-start.9) | collective-permute-done | bytes 147488 | tf_op jit(solution)/shard_map/ppermute | solution.py:592
  91.8 0.0 copy-start.3
  91.8 0.0 copy-start.5
  91.8 0.6 pack_y.3
  92.4 0.0 copy-start
  92.4 0.1 collective-permute-start.10
  92.5 2.5 %collective-permute-start.11 = (f32[2,36,8,128]{3,2,1,0:T(8,128)S(1)}, f32[2,36,8,128]{3,2,1,0:T(8,128)S(1)}, u32[]{:S(2)}, u32[]{:S(2)}) collective-permute-start(f32[2,36,8,128]{3,2,1,0:T(8,128)S(1)} %get-tuple-element.48), channel_id=1, source_target_pairs={{8,16},{24,32},{40,48},{16,8},{32,24},{48,40},{9,17},{25,33},{41,4... | collective-permute-start | bytes 884744 | tf_op jit(solution)/shard_map/ppermute | solution.py:592
  95.0 0.0 collective-permute-done.10.y_first_ref
  95.0 5.7 %collective-permute-done.11.y_second_ref = f32[2,36,8,128]{3,2,1,0:T(8,128)S(1)} collective-permute-done((f32[2,36,8,128]{3,2,1,0:T(8,128)S(1)}, f32[2,36,8,128]{3,2,1,0:T(8,128)S(1)}, u32[]{:S(2)}, u32[]{:S(2)}) %collective-permute-start.11) | collective-permute-done | bytes 294944 | tf_op jit(solution)/shard_map/ppermute | solution.py:592
  100.7 0.0 copy-start.1
  100.7 0.7 copy-done.1
  101.4 0.0 all-to-all-done.2.part_ref
  101.4 0.0 copy-done.4
  101.4 0.0 copy-start.2
  101.4 1.0 copy-done.2
  102.4 13.7 %second_sweep.1 = (f32[16,16,128]{2,1,0:T(8,128)}, f32[16,16,128]{2,1,0:T(8,128)}, f32[8,128]{1,0:T(8,128)}) custom-call(s32[7]{0:T(128)S(1)} %stack.23.place_ref, f32[1]{0:T(128)S(6)} %copy.17.current_ref, f32[2,16,16,128]{3,2,1,0:T(8,128)S(1)} %get-tuple-element.41.fields_ref.centre_ref, f32[2,2,16,128]{3,2,1,0:T(8,128)S(1)} %get-tuple-element.44.ends_ref, ...), custom_call_target="tpu_custom_call" | custom-call | tf_op jit(solution)/shard_map/second_sweep/pallas_call | solution.py:765
  116.1 8.5 %all-to-all-start.3 = ((f32[8,1,128]{2,1,0:T(1,128)}), f32[8,1,128]{2,1,0:T(1,128)S(1)}, u32[]{:S(2)}, u32[]{:S(2)}) async-start(f32[8,1,128]{2,1,0:T(1,128)} %bitcast.14), calls=%async_computation.3 | async-start | bytes 8192 | tf_op jit(solution)/shard_map/all_to_all | solution.py:792
  124.5 0.0 copy-done.3
  124.5 0.0 copy-done.5
  124.5 0.0 copy-done
  124.6 0.6 shells.1
  125.2 7.0 %all-to-all-done.3 = f32[8,1,128]{2,1,0:T(1,128)S(1)} async-done(((f32[8,1,128]{2,1,0:T(1,128)}), f32[8,1,128]{2,1,0:T(1,128)S(1)}, u32[]{:S(2)}, u32[]{:S(2)}) %all-to-all-start.3) | async-done | bytes 4128 | tf_op jit(solution)/shard_map/all_to_all | solution.py:792
  132.2 0.6 add_bitcast_fusion
  (2 shorter events, 0.0 us)
Async XLA Ops:
  6.0 16.9 %all-to-all-start = ((f32[8,16,128]{2,1,0:T(8,128)}), f32[8,16,128]{2,1,0:T(8,128)S(1)}, u32[]{:S(2)}, u32[]{:S(2)}) async-start(f32[8,16,128]{2,1,0:T(8,128)} %get-tuple-element.35), calls=%async_computation | async-start | bytes 131072 | tf_op jit(solution)/shard_map/all_to_all | solution.py:730
  14.4 4.6 %collective-permute-start = (f32[4,16,128]{2,1,0:T(8,128)S(1)}, f32[4,16,128]{2,1,0:T(8,128)S(1)}, u32[]{:S(2)}, u32[]{:S(2)}) collective-permute-start(f32[4,16,128]{2,1,0:T(8,128)S(1)} %get-tuple-element.33), channel_id=1, source_target_pairs={{0,1},{1,0},{2,3},{3,2},{4,5},{5,4},{6,7},{7,6},{8,9},{9,8},{10,11... | collective-permute-start | bytes 98312 | tf_op jit(solution)/shard_map/ppermute | solution.py:592
  16.5 2.6 %collective-permute-start.1 = (f32[4,16,128]{2,1,0:T(8,128)S(1)}, f32[4,16,128]{2,1,0:T(8,128)S(1)}, u32[]{:S(2)}, u32[]{:S(2)}) collective-permute-start(f32[4,16,128]{2,1,0:T(8,128)S(1)} %get-tuple-element.34), channel_id=1, source_target_pairs={{1,2},{3,4},{5,6},{2,1},{4,3},{6,5},{9,10},{11,12},{13,14},{10,9},... | collective-permute-start | bytes 98312 | tf_op jit(solution)/shard_map/ppermute | solution.py:592
  23.5 7.4 %collective-permute-start.2 = (f32[4,9,16,128]{3,2,1,0:T(8,128)S(1)}, f32[4,9,16,128]{3,2,1,0:T(8,128)S(1)}, u32[]{:S(2)}, u32[]{:S(2)}) collective-permute-start(f32[4,9,16,128]{3,2,1,0:T(8,128)S(1)} %get-tuple-element.37), channel_id=1, source_target_pairs={{0,64},{64,0},{128,192},{192,128},{1,65},{65,1},{129,193},{193,129... | collective-permute-start | bytes 884744 | tf_op jit(solution)/shard_map/ppermute | solution.py:592
  24.8 8.9 %collective-permute-start.3 = (f32[4,9,16,128]{3,2,1,0:T(8,128)S(1)}, f32[4,9,16,128]{3,2,1,0:T(8,128)S(1)}, u32[]{:S(2)}, u32[]{:S(2)}) collective-permute-start(f32[4,9,16,128]{3,2,1,0:T(8,128)S(1)} %get-tuple-element.38), channel_id=1, source_target_pairs={{64,128},{128,64},{65,129},{129,65},{66,130},{130,66},{67,131},{13... | collective-permute-start | bytes 884744 | tf_op jit(solution)/shard_map/ppermute | solution.py:592
  35.3 16.3 %collective-permute-start.4 = (f32[4,36,8,128]{3,2,1,0:T(8,128)}, f32[4,36,8,128]{3,2,1,0:T(8,128)S(1)}, u32[]{:S(2)}, u32[]{:S(2)}) collective-permute-start(f32[4,36,8,128]{3,2,1,0:T(8,128)} %get-tuple-element.39), channel_id=1, source_target_pairs={{0,8},{8,0},{16,24},{24,16},{32,40},{40,32},{48,56},{56,48},{1,9},... | collective-permute-start | bytes 1769480 | tf_op jit(solution)/shard_map/ppermute | solution.py:592
  35.3 16.3 %collective-permute-start.5 = (f32[4,36,8,128]{3,2,1,0:T(8,128)}, f32[4,36,8,128]{3,2,1,0:T(8,128)S(1)}, u32[]{:S(2)}, u32[]{:S(2)}) collective-permute-start(f32[4,36,8,128]{3,2,1,0:T(8,128)} %get-tuple-element.40), channel_id=1, source_target_pairs={{8,16},{24,32},{40,48},{16,8},{32,24},{48,40},{9,17},{25,33},{41,4... | collective-permute-start | bytes 1769480 | tf_op jit(solution)/shard_map/ppermute | solution.py:592
  37.8 13.8 %all-to-all-start.1 = ((f32[32,16,128]{2,1,0:T(8,128)}), f32[32,16,128]{2,1,0:T(8,128)S(1)}, u32[]{:S(2)}, u32[]{:S(2)}) async-start(f32[32,16,128]{2,1,0:T(8,128)} %column.1.rest_0_), calls=%async_computation.1 | async-start | bytes 524288 | tf_op jit(solution)/shard_map/all_to_all | solution.py:740
  45.7 55.6 %copy-start.4 = (s32[1,1,2048]{2,1,0:T(1,128)S(1)}, s32[1,1,2048]{2,1,0:T(1,128)}, u32[]{:S(2)}) copy-start(s32[1,1,2048]{2,1,0:T(1,128)} %param.18) | copy-start | bytes 24580
  64.4 37.0 %all-to-all-start.2 = ((f32[256,2,128]{2,1,0:T(2,128)}), f32[256,2,128]{2,1,0:T(2,128)S(1)}, u32[]{:S(2)}, u32[]{:S(2)}) async-start(f32[256,2,128]{2,1,0:T(2,128)} %get-tuple-element.49), calls=%async_computation.2 | async-start | bytes 524288 | tf_op jit(solution)/shard_map/all_to_all | solution.py:764
  75.9 7.0 %collective-permute-start.6 = (f32[2,16,128]{2,1,0:T(8,128)S(1)}, f32[2,16,128]{2,1,0:T(8,128)S(1)}, u32[]{:S(2)}, u32[]{:S(2)}) collective-permute-start(f32[2,16,128]{2,1,0:T(8,128)S(1)} %get-tuple-element.42), channel_id=1, source_target_pairs={{0,1},{1,0},{2,3},{3,2},{4,5},{5,4},{6,7},{7,6},{8,9},{9,8},{10,11... | collective-permute-start | bytes 49160 | tf_op jit(solution)/shard_map/ppermute | solution.py:592
  77.7 5.2 %collective-permute-start.7 = (f32[2,16,128]{2,1,0:T(8,128)S(1)}, f32[2,16,128]{2,1,0:T(8,128)S(1)}, u32[]{:S(2)}, u32[]{:S(2)}) collective-permute-start(f32[2,16,128]{2,1,0:T(8,128)S(1)} %get-tuple-element.43), channel_id=1, source_target_pairs={{1,2},{3,4},{5,6},{2,1},{4,3},{6,5},{9,10},{11,12},{13,14},{10,9},... | collective-permute-start | bytes 49160 | tf_op jit(solution)/shard_map/ppermute | solution.py:592
  83.5 5.5 %collective-permute-start.8 = (f32[2,9,16,128]{3,2,1,0:T(8,128)S(1)}, f32[2,9,16,128]{3,2,1,0:T(8,128)S(1)}, u32[]{:S(2)}, u32[]{:S(2)}) collective-permute-start(f32[2,9,16,128]{3,2,1,0:T(8,128)S(1)} %get-tuple-element.45), channel_id=1, source_target_pairs={{0,64},{64,0},{128,192},{192,128},{1,65},{65,1},{129,193},{193,129... | collective-permute-start | bytes 442376 | tf_op jit(solution)/shard_map/ppermute | solution.py:592
  84.8 7.0 %collective-permute-start.9 = (f32[2,9,16,128]{3,2,1,0:T(8,128)S(1)}, f32[2,9,16,128]{3,2,1,0:T(8,128)S(1)}, u32[]{:S(2)}, u32[]{:S(2)}) collective-permute-start(f32[2,9,16,128]{3,2,1,0:T(8,128)S(1)} %get-tuple-element.46), channel_id=1, source_target_pairs={{64,128},{128,64},{65,129},{129,65},{66,130},{130,66},{67,131},{13... | collective-permute-start | bytes 442376 | tf_op jit(solution)/shard_map/ppermute | solution.py:592
  91.8 32.8 %copy-start.3 = (f32[1,1,64,128]{3,2,1,0:T(8,128)S(1)}, f32[1,1,64,128]{3,2,1,0:T(8,128)}, u32[]{:S(2)}) copy-start(f32[1,1,64,128]{3,2,1,0:T(8,128)} %param.24) | copy-start | bytes 98308
  91.8 32.8 %copy-start.5 = (s32[1,1,128]{2,1,0:T(1,128)S(1)}, s32[1,1,128]{2,1,0:T(1,128)}, u32[]{:S(2)}) copy-start(s32[1,1,128]{2,1,0:T(1,128)} %param.23) | copy-start | bytes 1540
  92.4 32.2 %copy-start = (f32[1,1,64,64,128]{4,3,2,1,0:T(8,128)S(1)}, f32[1,1,64,64,128]{4,3,2,1,0:T(8,128)}, u32[]{:S(2)}) copy-start(f32[1,1,64,64,128]{4,3,2,1,0:T(8,128)} %param.25) | copy-start | bytes 6291460
  92.4 2.6 %collective-permute-start.10 = (f32[2,36,8,128]{3,2,1,0:T(8,128)S(1)}, f32[2,36,8,128]{3,2,1,0:T(8,128)S(1)}, u32[]{:S(2)}, u32[]{:S(2)}) collective-permute-start(f32[2,36,8,128]{3,2,1,0:T(8,128)S(1)} %get-tuple-element.47), channel_id=1, source_target_pairs={{0,8},{8,0},{16,24},{24,16},{32,40},{40,32},{48,56},{56,48},{1,9},... | collective-permute-start | bytes 884744 | tf_op jit(solution)/shard_map/ppermute | solution.py:592
  92.5 8.2 %collective-permute-start.11 = (f32[2,36,8,128]{3,2,1,0:T(8,128)S(1)}, f32[2,36,8,128]{3,2,1,0:T(8,128)S(1)}, u32[]{:S(2)}, u32[]{:S(2)}) collective-permute-start(f32[2,36,8,128]{3,2,1,0:T(8,128)S(1)} %get-tuple-element.48), channel_id=1, source_target_pairs={{8,16},{24,32},{40,48},{16,8},{32,24},{48,40},{9,17},{25,33},{41,4... | collective-permute-start | bytes 884744 | tf_op jit(solution)/shard_map/ppermute | solution.py:592
  100.7 0.7 copy-start.1
  101.4 1.0 copy-start.2
  116.1 16.1 %all-to-all-start.3 = ((f32[8,1,128]{2,1,0:T(1,128)}), f32[8,1,128]{2,1,0:T(1,128)S(1)}, u32[]{:S(2)}, u32[]{:S(2)}) async-start(f32[8,1,128]{2,1,0:T(1,128)} %bitcast.14), calls=%async_computation.3 | async-start | bytes 8192 | tf_op jit(solution)/shard_map/all_to_all | solution.py:792

commit v5 on v4

--- a/solution.py
+++ b/solution.py
@@ -788,7 +788,7 @@
         out_shape=[shape(64, 128)] * 2,
         compiler_params=params(8),
         name="shells",
-    )(shell_inverse.reshape(64, 64, 128), shells, conc)
+    )(*in_hbm(shell_inverse.reshape(64, 64, 128)), shells, conc)
     flux = jnp.sum(lax.all_to_all(flux, "gz", 0, 0, tiled=True), axis=0, keepdims=True)
     updated = base + shell_step * flux * surface_column
     return (concentration, potential, updated[None, None])

time: 133 us -> 132 us (level)
  waiting for transfers between devices: 39.5 us -> 35.7 us
  Pallas kernels: 35.9 us -> 39.4 us
  local copies, waits for them, and re-layouts: 1.79 us -> 0.11 us
    pallas_call x1, Pallas kernels: 0.59 us -> 4.23 us  [on_device(): pl.pallas_call(shell_kernel, grid=(8,), in_specs=[pl.BlockSpec((8, 64, 12...]
    all_to_all x1, waiting for transfers between devices: 6.98 us -> 3.35 us  [on_device(): lax.all_to_all(flux, 'gz', 0, 0, tiled=True)]
    unnamed x12 -> x6, local copies, waits for them, and re-layouts: 1.7 us -> 0.02 us
  transfers between devices with their start and end apart: 16 -> 16, of which waited for: 10 -> 10; matrix products, arithmetic and copies ran while one was open for 0% -> 0% of each run, Pallas kernels for 2% -> 5%
where the time goes in v5:
time: 132 us; the launch traced here: 131 us
  starting transfers between devices  52.8 us (40%)
  Pallas kernels  39.4 us (30%)
  waiting for transfers between devices  35.7 us (27%)
  between operations  2.13 us (2%)
    pallas_call x1, Pallas kernels, on_device(): pl.pallas_call(second_kernel, in_specs=[SMEM] * 2 + [VMEM] * 10 + [HBM] *...  13.7 us
    pallas_call x1, Pallas kernels, on_device(): pl.pallas_call(first_kernel, in_specs=[SMEM] * 2 + [VMEM] * 7, out_specs=...  12.8 us
    ppermute x6, waiting for transfers between devices, trade(): lax.ppermute(first, axis, pairs)  12.4 us
    all_to_all x1, starting transfers between devices, on_device(): part = lax.all_to_all(part, ('gx', 'gy', 'gz'), 0, 0, tiled=True)  11.4 us
    ppermute x6, waiting for transfers between devices, trade(): lax.ppermute(second, axis, others)  11.1 us
    ppermute x6, starting transfers between devices, trade(): lax.ppermute(second, axis, others)  10.1 us
    all_to_all x1, starting transfers between devices, on_device(): column = lax.all_to_all(column, 'gz', 0, 0, tiled=True)  8.48 us
    all_to_all x1, starting transfers between devices, on_device(): lax.all_to_all(flux, 'gz', 0, 0, tiled=True)  8.45 us
  transfers between devices with their start and end apart: 16, of which 10 were waited for; matrix products, arithmetic and copies ran while one was open for 0% of the time, Pallas kernels for 5%

profile of v5, /device:TPU:12, one launch (start us, length us, event | category | flops | bytes accessed | tf_op | source)
XLA Modules:
  0.0 130.9 jit_solution(6683531131179760103)
XLA Ops:
  1.3 0.1 stack.23.place_ref
  1.4 4.6 %prepare.1 = (f32[4,16,16,128]{3,2,1,0:T(8,128)S(1)}, f32[4,16,128]{2,1,0:T(8,128)S(1)}, f32[4,16,128]{2,1,0:T(8,128)S(1)}, f32[8,16,128]{2,1,0:T(8,128)}, s32[16,128]{1,0:T(8,128)S(1)}) custom-call(s32[7]{0:T(128)S(1)} %stack.23.place_ref, s32[1,1,1]{2,1,0:T(1,128)S(6)} %copy.18.count_ref, s32[16,128]{1,0:T(8,128)} %bitcast.20, s32[16,128]{1,0:T(8,128)} %bitcast.25, ...), custom_call_target="tpu_custom_call" | custom-call | tf_op jit(solution)/shard_map/prepare/pallas_call | solution.py:707
  6.0 8.5 %all-to-all-start = ((f32[8,16,128]{2,1,0:T(8,128)}), f32[8,16,128]{2,1,0:T(8,128)S(1)}, u32[]{:S(2)}, u32[]{:S(2)}) async-start(f32[8,16,128]{2,1,0:T(8,128)} %get-tuple-element.35), calls=%async_computation | async-start | bytes 131072 | tf_op jit(solution)/shard_map/all_to_all | solution.py:730
  14.4 2.0 %collective-permute-start = (f32[4,16,128]{2,1,0:T(8,128)S(1)}, f32[4,16,128]{2,1,0:T(8,128)S(1)}, u32[]{:S(2)}, u32[]{:S(2)}) collective-permute-start(f32[4,16,128]{2,1,0:T(8,128)S(1)} %get-tuple-element.33), channel_id=1, source_target_pairs={{0,1},{1,0},{2,3},{3,2},{4,5},{5,4},{6,7},{7,6},{8,9},{9,8},{10,11... | collective-permute-start | bytes 98312 | tf_op jit(solution)/shard_map/ppermute | solution.py:592
  16.5 0.7 collective-permute-start.1
  17.1 2.0 %collective-permute-done.z_first_ref = f32[4,16,128]{2,1,0:T(8,128)S(1)} collective-permute-done((f32[4,16,128]{2,1,0:T(8,128)S(1)}, f32[4,16,128]{2,1,0:T(8,128)S(1)}, u32[]{:S(2)}, u32[]{:S(2)}) %collective-permute-start) | collective-permute-done | bytes 32800 | tf_op jit(solution)/shard_map/ppermute | solution.py:592
  19.1 0.0 collective-permute-done.1.z_second_ref
  19.1 3.7 %all-to-all-done.rest_0_.column_ref = f32[8,16,128]{2,1,0:T(8,128)S(1)} async-done(((f32[8,16,128]{2,1,0:T(8,128)}), f32[8,16,128]{2,1,0:T(8,128)S(1)}, u32[]{:S(2)}, u32[]{:S(2)}) %all-to-all-start) | async-done | bytes 65568 | tf_op jit(solution)/shard_map/all_to_all | solution.py:730
  22.8 0.6 pack_x.2
  23.5 1.3 collective-permute-start.2
  24.8 1.9 %collective-permute-start.3 = (f32[4,9,16,128]{3,2,1,0:T(8,128)S(1)}, f32[4,9,16,128]{3,2,1,0:T(8,128)S(1)}, u32[]{:S(2)}, u32[]{:S(2)}) collective-permute-start(f32[4,9,16,128]{3,2,1,0:T(8,128)S(1)} %get-tuple-element.38), channel_id=1, source_target_pairs={{64,128},{128,64},{65,129},{129,65},{66,130},{130,66},{67,131},{13... | collective-permute-start | bytes 884744 | tf_op jit(solution)/shard_map/ppermute | solution.py:592
  26.7 0.7 column.1.rest_0_
  27.4 3.5 %collective-permute-done.2.x_first_ref = f32[4,9,16,128]{3,2,1,0:T(8,128)S(1)} collective-permute-done((f32[4,9,16,128]{3,2,1,0:T(8,128)S(1)}, f32[4,9,16,128]{3,2,1,0:T(8,128)S(1)}, u32[]{:S(2)}, u32[]{:S(2)}) %collective-permute-start.2) | collective-permute-done | bytes 294944 | tf_op jit(solution)/shard_map/ppermute | solution.py:592
  30.9 2.8 %collective-permute-done.3.x_second_ref = f32[4,9,16,128]{3,2,1,0:T(8,128)S(1)} collective-permute-done((f32[4,9,16,128]{3,2,1,0:T(8,128)S(1)}, f32[4,9,16,128]{3,2,1,0:T(8,128)S(1)}, u32[]{:S(2)}, u32[]{:S(2)}) %collective-permute-start.3) | collective-permute-done | bytes 294944 | tf_op jit(solution)/shard_map/ppermute | solution.py:592
  33.7 1.5 %pack_y.2 = (f32[4,36,8,128]{3,2,1,0:T(8,128)}, f32[4,36,8,128]{3,2,1,0:T(8,128)S(1)}) custom-call(s32[7]{0:T(128)S(1)} %stack.23.place_ref, f32[4,16,16,128]{3,2,1,0:T(8,128)S(1)} %get-tuple-element.32.fields_ref.centre_ref, f32[4,2,16,128]{3,2,1,0:T(8,128)S(1)} %get-tuple-element.36.ends_ref, f32[4,9,16,128]{3,2,1,0:T(8,128)S(1)} %collective-permute-done.2.x_first_ref, ...), custom_call_target="tpu_custom_call" | custom-call | bytes 167772160 | tf_op jit(solution)/shard_map/pack_y/pallas_call | solution.py:649
  35.2 0.0 collective-permute-start.4
  35.2 2.5 %collective-permute-start.5 = (f32[4,36,8,128]{3,2,1,0:T(8,128)S(1)}, f32[4,36,8,128]{3,2,1,0:T(8,128)S(1)}, u32[]{:S(2)}, u32[]{:S(2)}) collective-permute-start(f32[4,36,8,128]{3,2,1,0:T(8,128)S(1)} %get-tuple-element.40), channel_id=1, source_target_pairs={{8,16},{24,32},{40,48},{16,8},{32,24},{48,40},{9,17},{25,33},{41,4... | collective-permute-start | bytes 1769480 | tf_op jit(solution)/shard_map/ppermute | solution.py:592
  37.6 7.9 %all-to-all-start.1 = ((f32[32,16,128]{2,1,0:T(8,128)}), f32[32,16,128]{2,1,0:T(8,128)S(1)}, u32[]{:S(2)}, u32[]{:S(2)}) async-start(f32[32,16,128]{2,1,0:T(8,128)} %column.1.rest_0_), calls=%async_computation.1 | async-start | bytes 524288 | tf_op jit(solution)/shard_map/all_to_all | solution.py:740
  45.6 0.0 copy-start.1
  46.3 5.2 %all-to-all-done.1.sums_ref = f32[32,16,128]{2,1,0:T(8,128)S(1)} async-done(((f32[32,16,128]{2,1,0:T(8,128)}), f32[32,16,128]{2,1,0:T(8,128)S(1)}, u32[]{:S(2)}, u32[]{:S(2)}) %all-to-all-start.1) | async-done | bytes 262176 | tf_op jit(solution)/shard_map/all_to_all | solution.py:740
  51.5 0.0 collective-permute-done.4.y_first_ref
  51.5 0.0 collective-permute-done.5.y_second_ref
  51.5 12.8 %first_sweep.1 = (f32[8,160,128]{2,1,0:T(8,128)}, f32[8,160,128]{2,1,0:T(8,128)}, f32[8,160,128]{2,1,0:T(8,128)}, f32[8,160,128]{2,1,0:T(8,128)}, f32[2,16,16,12...) custom-call(s32[7]{0:T(128)S(1)} %stack.23.place_ref, ...), custom_call_target="tpu_custom_call" | custom-call | tf_op jit(solution)/shard_map/first_sweep/pallas_call | solution.py:743
  64.3 11.4 %all-to-all-start.2 = ((f32[256,2,128]{2,1,0:T(2,128)}), f32[256,2,128]{2,1,0:T(2,128)S(1)}, u32[]{:S(2)}, u32[]{:S(2)}) async-start(f32[256,2,128]{2,1,0:T(2,128)} %get-tuple-element.49), calls=%async_computation.2 | async-start | bytes 524288 | tf_op jit(solution)/shard_map/all_to_all | solution.py:764
  75.8 1.8 %collective-permute-start.6 = (f32[2,16,128]{2,1,0:T(8,128)S(1)}, f32[2,16,128]{2,1,0:T(8,128)S(1)}, u32[]{:S(2)}, u32[]{:S(2)}) collective-permute-start(f32[2,16,128]{2,1,0:T(8,128)S(1)} %get-tuple-element.42), channel_id=1, source_target_pairs={{0,1},{1,0},{2,3},{3,2},{4,5},{5,4},{6,7},{7,6},{8,9},{9,8},{10,11... | collective-permute-start | bytes 49160 | tf_op jit(solution)/shard_map/ppermute | solution.py:592
  77.5 0.7 collective-permute-start.7
  78.2 4.6 %collective-permute-done.6.z_first_ref = f32[2,16,128]{2,1,0:T(8,128)S(1)} collective-permute-done((f32[2,16,128]{2,1,0:T(8,128)S(1)}, f32[2,16,128]{2,1,0:T(8,128)S(1)}, u32[]{:S(2)}, u32[]{:S(2)}) %collective-permute-start.6) | collective-permute-done | bytes 16416 | tf_op jit(solution)/shard_map/ppermute | solution.py:592
  82.8 0.0 collective-permute-done.7.z_second_ref
  82.8 0.6 pack_x.3
  83.4 1.3 collective-permute-start.8
  84.6 1.9 %collective-permute-start.9 = (f32[2,9,16,128]{3,2,1,0:T(8,128)S(1)}, f32[2,9,16,128]{3,2,1,0:T(8,128)S(1)}, u32[]{:S(2)}, u32[]{:S(2)}) collective-permute-start(f32[2,9,16,128]{3,2,1,0:T(8,128)S(1)} %get-tuple-element.46), channel_id=1, source_target_pairs={{64,128},{128,64},{65,129},{129,65},{66,130},{130,66},{67,131},{13... | collective-permute-start | bytes 442376 | tf_op jit(solution)/shard_map/ppermute | solution.py:592
  86.6 2.4 %collective-permute-done.8.x_first_ref = f32[2,9,16,128]{3,2,1,0:T(8,128)S(1)} collective-permute-done((f32[2,9,16,128]{3,2,1,0:T(8,128)S(1)}, f32[2,9,16,128]{3,2,1,0:T(8,128)S(1)}, u32[]{:S(2)}, u32[]{:S(2)}) %collective-permute-start.8) | collective-permute-done | bytes 147488 | tf_op jit(solution)/shard_map/ppermute | solution.py:592
  88.9 2.7 %collective-permute-done.9.x_second_ref = f32[2,9,16,128]{3,2,1,0:T(8,128)S(1)} collective-permute-done((f32[2,9,16,128]{3,2,1,0:T(8,128)S(1)}, f32[2,9,16,128]{3,2,1,0:T(8,128)S(1)}, u32[]{:S(2)}, u32[]{:S(2)}) %collective-permute-start.9) | collective-permute-done | bytes 147488 | tf_op jit(solution)/shard_map/ppermute | solution.py:592
  91.7 0.6 pack_y.3
  92.3 0.0 copy-start
  92.3 0.0 copy-start.2
  92.3 0.1 collective-permute-start.10
  92.4 2.5 %collective-permute-start.11 = (f32[2,36,8,128]{3,2,1,0:T(8,128)S(1)}, f32[2,36,8,128]{3,2,1,0:T(8,128)S(1)}, u32[]{:S(2)}, u32[]{:S(2)}) collective-permute-start(f32[2,36,8,128]{3,2,1,0:T(8,128)S(1)} %get-tuple-element.48), channel_id=1, source_target_pairs={{8,16},{24,32},{40,48},{16,8},{32,24},{48,40},{9,17},{25,33},{41,4... | collective-permute-start | bytes 884744 | tf_op jit(solution)/shard_map/ppermute | solution.py:592
  94.9 0.0 collective-permute-done.10.y_first_ref
  94.9 5.5 %collective-permute-done.11.y_second_ref = f32[2,36,8,128]{3,2,1,0:T(8,128)S(1)} collective-permute-done((f32[2,36,8,128]{3,2,1,0:T(8,128)S(1)}, f32[2,36,8,128]{3,2,1,0:T(8,128)S(1)}, u32[]{:S(2)}, u32[]{:S(2)}) %collective-permute-start.11) | collective-permute-done | bytes 294944 | tf_op jit(solution)/shard_map/ppermute | solution.py:592
  100.4 0.0 all-to-all-done.2.part_ref
  100.4 0.0 copy-done.1
  100.4 13.7 %second_sweep.1 = (f32[16,16,128]{2,1,0:T(8,128)}, f32[16,16,128]{2,1,0:T(8,128)}, f32[8,128]{1,0:T(8,128)}) custom-call(s32[7]{0:T(128)S(1)} %stack.23.place_ref, f32[1]{0:T(128)S(6)} %copy.17.current_ref, f32[2,16,16,128]{3,2,1,0:T(8,128)S(1)} %get-tuple-element.41.fields_ref.centre_ref, f32[2,2,16,128]{3,2,1,0:T(8,128)S(1)} %get-tuple-element.44.ends_ref, ...), custom_call_target="tpu_custom_call" | custom-call | tf_op jit(solution)/shard_map/second_sweep/pallas_call | solution.py:765
  114.1 8.5 %all-to-all-start.3 = ((f32[8,1,128]{2,1,0:T(1,128)}), f32[8,1,128]{2,1,0:T(1,128)S(1)}, u32[]{:S(2)}, u32[]{:S(2)}) async-start(f32[8,1,128]{2,1,0:T(1,128)} %bitcast.14), calls=%async_computation.3 | async-start | bytes 8192 | tf_op jit(solution)/shard_map/all_to_all | solution.py:792
  122.6 0.0 copy-done
  122.6 0.0 copy-done.2
  122.6 4.2 %shells.1 = (f32[64,128]{1,0:T(8,128)S(1)}, f32[64,128]{1,0:T(8,128)S(1)}) custom-call(f32[64,64,128]{2,1,0:T(8,128)} %bitcast.24, s32[1,128]{1,0:T(1,128)S(1)} %bitcast.23, f32[64,128]{1,0:T(8,128)S(1)} %bitcast.19), custom_call_target="tpu_custom_call" | custom-call | tf_op jit(solution)/shard_map/shells/pallas_call | solution.py:779
  126.8 3.3 %all-to-all-done.3 = f32[8,1,128]{2,1,0:T(1,128)S(1)} async-done(((f32[8,1,128]{2,1,0:T(1,128)}), f32[8,1,128]{2,1,0:T(1,128)S(1)}, u32[]{:S(2)}, u32[]{:S(2)}) %all-to-all-start.3) | async-done | bytes 4128 | tf_op jit(solution)/shard_map/all_to_all | solution.py:792
  130.2 0.6 add_bitcast_fusion
  (2 shorter events, 0.0 us)
Async XLA Ops:
  6.0 16.9 %all-to-all-start = ((f32[8,16,128]{2,1,0:T(8,128)}), f32[8,16,128]{2,1,0:T(8,128)S(1)}, u32[]{:S(2)}, u32[]{:S(2)}) async-start(f32[8,16,128]{2,1,0:T(8,128)} %get-tuple-element.35), calls=%async_computation | async-start | bytes 131072 | tf_op jit(solution)/shard_map/all_to_all | solution.py:730
  14.4 4.6 %collective-permute-start = (f32[4,16,128]{2,1,0:T(8,128)S(1)}, f32[4,16,128]{2,1,0:T(8,128)S(1)}, u32[]{:S(2)}, u32[]{:S(2)}) collective-permute-start(f32[4,16,128]{2,1,0:T(8,128)S(1)} %get-tuple-element.33), channel_id=1, source_target_pairs={{0,1},{1,0},{2,3},{3,2},{4,5},{5,4},{6,7},{7,6},{8,9},{9,8},{10,11... | collective-permute-start | bytes 98312 | tf_op jit(solution)/shard_map/ppermute | solution.py:592
  16.5 2.6 %collective-permute-start.1 = (f32[4,16,128]{2,1,0:T(8,128)S(1)}, f32[4,16,128]{2,1,0:T(8,128)S(1)}, u32[]{:S(2)}, u32[]{:S(2)}) collective-permute-start(f32[4,16,128]{2,1,0:T(8,128)S(1)} %get-tuple-element.34), channel_id=1, source_target_pairs={{1,2},{3,4},{5,6},{2,1},{4,3},{6,5},{9,10},{11,12},{13,14},{10,9},... | collective-permute-start | bytes 98312 | tf_op jit(solution)/shard_map/ppermute | solution.py:592
  23.5 7.4 %collective-permute-start.2 = (f32[4,9,16,128]{3,2,1,0:T(8,128)S(1)}, f32[4,9,16,128]{3,2,1,0:T(8,128)S(1)}, u32[]{:S(2)}, u32[]{:S(2)}) collective-permute-start(f32[4,9,16,128]{3,2,1,0:T(8,128)S(1)} %get-tuple-element.37), channel_id=1, source_target_pairs={{0,64},{64,0},{128,192},{192,128},{1,65},{65,1},{129,193},{193,129... | collective-permute-start | bytes 884744 | tf_op jit(solution)/shard_map/ppermute | solution.py:592
  24.8 8.9 %collective-permute-start.3 = (f32[4,9,16,128]{3,2,1,0:T(8,128)S(1)}, f32[4,9,16,128]{3,2,1,0:T(8,128)S(1)}, u32[]{:S(2)}, u32[]{:S(2)}) collective-permute-start(f32[4,9,16,128]{3,2,1,0:T(8,128)S(1)} %get-tuple-element.38), channel_id=1, source_target_pairs={{64,128},{128,64},{65,129},{129,65},{66,130},{130,66},{67,131},{13... | collective-permute-start | bytes 884744 | tf_op jit(solution)/shard_map/ppermute | solution.py:592
  35.2 16.3 %collective-permute-start.4 = (f32[4,36,8,128]{3,2,1,0:T(8,128)}, f32[4,36,8,128]{3,2,1,0:T(8,128)S(1)}, u32[]{:S(2)}, u32[]{:S(2)}) collective-permute-start(f32[4,36,8,128]{3,2,1,0:T(8,128)} %get-tuple-element.39), channel_id=1, source_target_pairs={{0,8},{8,0},{16,24},{24,16},{32,40},{40,32},{48,56},{56,48},{1,9},... | collective-permute-start | bytes 1769480 | tf_op jit(solution)/shard_map/ppermute | solution.py:592
  35.2 16.3 %collective-permute-start.5 = (f32[4,36,8,128]{3,2,1,0:T(8,128)S(1)}, f32[4,36,8,128]{3,2,1,0:T(8,128)S(1)}, u32[]{:S(2)}, u32[]{:S(2)}) collective-permute-start(f32[4,36,8,128]{3,2,1,0:T(8,128)S(1)} %get-tuple-element.40), channel_id=1, source_target_pairs={{8,16},{24,32},{40,48},{16,8},{32,24},{48,40},{9,17},{25,33},{41,4... | collective-permute-start | bytes 1769480 | tf_op jit(solution)/shard_map/ppermute | solution.py:592
  37.6 13.8 %all-to-all-start.1 = ((f32[32,16,128]{2,1,0:T(8,128)}), f32[32,16,128]{2,1,0:T(8,128)S(1)}, u32[]{:S(2)}, u32[]{:S(2)}) async-start(f32[32,16,128]{2,1,0:T(8,128)} %column.1.rest_0_), calls=%async_computation.1 | async-start | bytes 524288 | tf_op jit(solution)/shard_map/all_to_all | solution.py:740
  45.6 54.8 %copy-start.1 = (s32[1,1,2048]{2,1,0:T(1,128)S(1)}, s32[1,1,2048]{2,1,0:T(1,128)}, u32[]{:S(2)}) copy-start(s32[1,1,2048]{2,1,0:T(1,128)} %param.18) | copy-start | bytes 24580
  64.3 36.1 %all-to-all-start.2 = ((f32[256,2,128]{2,1,0:T(2,128)}), f32[256,2,128]{2,1,0:T(2,128)S(1)}, u32[]{:S(2)}, u32[]{:S(2)}) async-start(f32[256,2,128]{2,1,0:T(2,128)} %get-tuple-element.49), calls=%async_computation.2 | async-start | bytes 524288 | tf_op jit(solution)/shard_map/all_to_all | solution.py:764
  75.8 7.0 %collective-permute-start.6 = (f32[2,16,128]{2,1,0:T(8,128)S(1)}, f32[2,16,128]{2,1,0:T(8,128)S(1)}, u32[]{:S(2)}, u32[]{:S(2)}) collective-permute-start(f32[2,16,128]{2,1,0:T(8,128)S(1)} %get-tuple-element.42), channel_id=1, source_target_pairs={{0,1},{1,0},{2,3},{3,2},{4,5},{5,4},{6,7},{7,6},{8,9},{9,8},{10,11... | collective-permute-start | bytes 49160 | tf_op jit(solution)/shard_map/ppermute | solution.py:592
  77.5 5.2 %collective-permute-start.7 = (f32[2,16,128]{2,1,0:T(8,128)S(1)}, f32[2,16,128]{2,1,0:T(8,128)S(1)}, u32[]{:S(2)}, u32[]{:S(2)}) collective-permute-start(f32[2,16,128]{2,1,0:T(8,128)S(1)} %get-tuple-element.43), channel_id=1, source_target_pairs={{1,2},{3,4},{5,6},{2,1},{4,3},{6,5},{9,10},{11,12},{13,14},{10,9},... | collective-permute-start | bytes 49160 | tf_op jit(solution)/shard_map/ppermute | solution.py:592
  83.4 5.5 %collective-permute-start.8 = (f32[2,9,16,128]{3,2,1,0:T(8,128)S(1)}, f32[2,9,16,128]{3,2,1,0:T(8,128)S(1)}, u32[]{:S(2)}, u32[]{:S(2)}) collective-permute-start(f32[2,9,16,128]{3,2,1,0:T(8,128)S(1)} %get-tuple-element.45), channel_id=1, source_target_pairs={{0,64},{64,0},{128,192},{192,128},{1,65},{65,1},{129,193},{193,129... | collective-permute-start | bytes 442376 | tf_op jit(solution)/shard_map/ppermute | solution.py:592
  84.6 7.0 %collective-permute-start.9 = (f32[2,9,16,128]{3,2,1,0:T(8,128)S(1)}, f32[2,9,16,128]{3,2,1,0:T(8,128)S(1)}, u32[]{:S(2)}, u32[]{:S(2)}) collective-permute-start(f32[2,9,16,128]{3,2,1,0:T(8,128)S(1)} %get-tuple-element.46), channel_id=1, source_target_pairs={{64,128},{128,64},{65,129},{129,65},{66,130},{130,66},{67,131},{13... | collective-permute-start | bytes 442376 | tf_op jit(solution)/shard_map/ppermute | solution.py:592
  92.3 30.3 %copy-start = (f32[1,1,64,128]{3,2,1,0:T(8,128)S(1)}, f32[1,1,64,128]{3,2,1,0:T(8,128)}, u32[]{:S(2)}) copy-start(f32[1,1,64,128]{3,2,1,0:T(8,128)} %param.24) | copy-start | bytes 98308
  92.3 30.3 %copy-start.2 = (s32[1,1,128]{2,1,0:T(1,128)S(1)}, s32[1,1,128]{2,1,0:T(1,128)}, u32[]{:S(2)}) copy-start(s32[1,1,128]{2,1,0:T(1,128)} %param.23) | copy-start | bytes 1540
  92.3 2.6 %collective-permute-start.10 = (f32[2,36,8,128]{3,2,1,0:T(8,128)S(1)}, f32[2,36,8,128]{3,2,1,0:T(8,128)S(1)}, u32[]{:S(2)}, u32[]{:S(2)}) collective-permute-start(f32[2,36,8,128]{3,2,1,0:T(8,128)S(1)} %get-tuple-element.47), channel_id=1, source_target_pairs={{0,8},{8,0},{16,24},{24,16},{32,40},{40,32},{48,56},{56,48},{1,9},... | collective-permute-start | bytes 884744 | tf_op jit(solution)/shard_map/ppermute | solution.py:592
  92.4 8.0 %collective-permute-start.11 = (f32[2,36,8,128]{3,2,1,0:T(8,128)S(1)}, f32[2,36,8,128]{3,2,1,0:T(8,128)S(1)}, u32[]{:S(2)}, u32[]{:S(2)}) collective-permute-start(f32[2,36,8,128]{3,2,1,0:T(8,128)S(1)} %get-tuple-element.48), channel_id=1, source_target_pairs={{8,16},{24,32},{40,48},{16,8},{32,24},{48,40},{9,17},{25,33},{41,4... | collective-permute-start | bytes 884744 | tf_op jit(solution)/shard_map/ppermute | solution.py:592
  114.1 16.1 %all-to-all-start.3 = ((f32[8,1,128]{2,1,0:T(1,128)}), f32[8,1,128]{2,1,0:T(1,128)S(1)}, u32[]{:S(2)}, u32[]{:S(2)}) async-start(f32[8,1,128]{2,1,0:T(1,128)} %bitcast.14), calls=%async_computation.3 | async-start | bytes 8192 | tf_op jit(solution)/shard_map/all_to_all | solution.py:792
